TPU v7x, 32 devices: a whole 2x2x4 slice. The times are simulated.
32 devices in a mesh: rep: 2 (over y), shard: 4 (over z), seq: 4 (over x, core).
Axes of the slice: x: 2, y: 2, z: 4, core: 2. Of those that a mesh axis runs over, the one named last changes fastest.
Arguments:
- tokens: bfloat16 [32768, 768], P(('rep', 'shard', 'seq')), may hold values from -6 to 6
- doc_lengths: int32 [8, 4], P(('rep', 'shard')), may hold values from 1 to 3584, as said below
- expert_ids: int32 [32768, 1], P(('rep', 'shard', 'seq')), may hold values from 0 to 15; in each aligned block of 1024 rows (0 to 1023, 1024 to 2047, ...) at most 80 rows name the same one
- cotangent: bfloat16 [32768, 768], P(('rep', 'shard', 'seq')), may hold values from -6 to 6
- gain_attn: bfloat16 [768], P(('shard', 'seq')), may hold values from 0.5 to 1.5
- gain_ffn: bfloat16 [768], P(('shard', 'seq')), may hold values from 0.5 to 1.5
- w_query: bfloat16 [768, 768], P(('shard', 'seq')), may hold values from -0.078125 to 0.078125
- w_key: bfloat16 [768, 768], P(('shard', 'seq')), may hold values from -0.078125 to 0.078125
- w_value: bfloat16 [768, 768], P(('shard', 'seq')), may hold values from -0.21875 to 0.21875
- w_attn_out: bfloat16 [768, 768], P(('shard', 'seq')), may hold values from -3.5 to 3.5
- rel_table: bfloat16 [32, 12], P(('shard', 'seq')), may hold values from -4 to 4
- w_router: bfloat16 [768, 16], P(('shard', 'seq')), may hold values from -0.15625 to 0.15625
- w_expert_in: bfloat16 [16, 768, 3072], P(('shard', 'seq')), may hold values from -0.21875 to 0.21875
- w_expert_out: bfloat16 [16, 3072, 768], P(('shard', 'seq')), may hold values from -1.75 to 1.75
Outputs:
- mixed: bfloat16 [32768, 768], P(('rep', 'shard', 'seq'))
- loss: float32 [], replicated
- importance: float32 [16], replicated
- d_tokens: float32 [32768, 768], P(('rep', 'shard', 'seq'))
- d_gain_attn: float32 [768], P(('shard', 'seq'))
- d_gain_ffn: float32 [768], P(('shard', 'seq'))
- d_query: float32 [768, 768], P(('shard', 'seq'))
- d_key: float32 [768, 768], P(('shard', 'seq'))
- d_value: float32 [768, 768], P(('shard', 'seq'))
- d_attn_out: float32 [768, 768], P(('shard', 'seq'))
- d_rel_table: float32 [32, 12], P(('shard', 'seq'))
- d_router: float32 [768, 16], P(('shard', 'seq'))
- d_expert_in: float32 [16, 768, 3072], P(('shard', 'seq'))
- d_expert_out: float32 [16, 3072, 768], P(('shard', 'seq'))
Inputs may be any that keep to these rules, and one draw needn't show every extreme that they name: `doc_lengths`: in each sequence one document has exactly 3584 positions; the lengths sum to less than 4096; sequence 0 has a document of 1 position. `expert_ids`: among the rows of one device at most 80 name the same expert.
All inputs are finite; a program needn't handle non-finite values.
Results may differ from a plain program's by a relative error of at most 0.02.
Values may be sent and summed in bfloat16 or wider, within the bound.
No kernel may reach another device: no remote copies, remote signals or barrier semaphores. Data moves between devices by JAX's collectives and lax.ppermute only.
A program may use at most 384 MiB of HBM per device.

v0:
```python
import math

import jax
import jax.numpy as jnp
from jax import lax
from jax.sharding import PartitionSpec as P

D = 768
HEADS = 12
HEAD = 64
FF = 3072
BUCKETS = 32
MAXDIST = 128
WINDOW = 1024
DOCS = 4
EXP_DEV = 1


EPSILON = 1e-06
AUX_WEIGHT = 0.01
MASKED_SCORE = -1e30
PRECISE = lax.Precision.HIGHEST


def with_halo(block, sides, width):
    for axis, dim in sides:
        count = lax.axis_size(axis)
        forward = [(i, i + 1) for i in range(count - 1)]
        backward = [(target, source) for source, target in forward]
        low = lax.ppermute(
            lax.slice_in_dim(block, block.shape[dim] - width, None, axis=dim), axis, forward
        )
        high = lax.ppermute(lax.slice_in_dim(block, 0, width, axis=dim), axis, backward)
        block = jnp.concatenate([low, block, high], axis=dim)
    return block


def passed_along(x, axis, by):
    size = lax.axis_size(axis)
    pairs = [(i, i + by) for i in range(size) if 0 <= i + by < size]
    return lax.ppermute(x, axis, pairs)


def rms_norm(vectors, gains):
    return (
        vectors * lax.rsqrt(jnp.mean(vectors * vectors, axis=-1, keepdims=True) + EPSILON) * gains
    )


def thresholds(max_distance, half_count):
    exact_span = half_count // 2
    collected = list(range(1, exact_span + 1))
    for target_level in range(exact_span + 1, half_count):
        candidate = exact_span
        while (
            exact_span
            + int(
                math.log(candidate / exact_span)
                / math.log(max_distance / exact_span)
                * (half_count - exact_span)
            )
            < target_level
        ):
            candidate += 1
        collected.append(candidate)
    return collected


def bucket_of(distance, half_count, limits):
    magnitude = jnp.abs(distance)
    bucket_id = (distance > 0).astype(jnp.int32) * half_count
    for boundary in limits:
        bucket_id = bucket_id + (magnitude >= boundary).astype(jnp.int32)
    return bucket_id


def low_dot(matrix_a, matrix_b):
    return jnp.dot(matrix_a, matrix_b, preferred_element_type=jnp.float32)


def gelu_tanh(values):
    return jax.nn.gelu(values, approximate=True)


def doc_index(places, doc_ends):
    return jnp.sum((places[:, None] >= doc_ends[None, :]).astype(jnp.int32), axis=1)


def toeplitz(band, block_rows):
    head_count, band_len = band.shape
    span = block_rows + band_len - 1
    padded = jnp.concatenate([band, jnp.zeros((head_count, block_rows), jnp.float32)], axis=1)
    tiled = jnp.broadcast_to(padded[:, None, :], (head_count, block_rows, span + 1))
    tiled = tiled.reshape(head_count, block_rows * (span + 1))[:, : block_rows * span]
    return tiled.reshape(head_count, block_rows, span)


def diag_sums(grid, block_rows, band_len):
    head_count = grid.shape[0]
    span = grid.shape[2]
    flat_grid = grid.reshape(head_count, block_rows * span)
    padded = jnp.concatenate([flat_grid, jnp.zeros((head_count, block_rows), jnp.float32)], axis=1)
    padded = padded.reshape(head_count, block_rows, span + 1)
    return jnp.sum(padded, axis=1)[:, :band_len]


def unpack(full):
    w_qkv = jnp.concatenate([full[0], full[1], full[2]], axis=1)
    return (
        w_qkv,
        full[3],
        full[4].astype(jnp.float32),
        full[5].astype(jnp.float32),
        full[6].astype(jnp.float32),
        full[7],
    )


def shards(
    tokens,
    doc_lengths,
    expert_ids,
    cotangent,
    gain_attn,
    gain_ffn,
    w_query,
    w_key,
    w_value,
    w_attn_out,
    rel_table,
    w_router,
    w_expert_in,
    w_expert_out,
):
    row_count = tokens.shape[0]
    group_size = lax.axis_size(("shard", "seq"))
    all_devices = lax.axis_size(("rep", "shard", "seq"))
    experts = EXP_DEV * group_size
    capacity = 5 * row_count // (4 * experts)
    half_window = WINDOW // 2
    band_len = 2 * half_window + 1
    block_rows = min(512, row_count)
    block_count = row_count // block_rows
    span = block_rows + 2 * half_window
    shared = (w_query, w_key, w_value, w_attn_out, gain_attn, gain_ffn, rel_table, w_router)
    gathered = (
        lax.all_gather(shared[0], ("shard", "seq"), axis=0, tiled=True),
        lax.all_gather(shared[1], ("shard", "seq"), axis=0, tiled=True),
        lax.all_gather(shared[2], ("shard", "seq"), axis=0, tiled=True),
        lax.all_gather(shared[3], ("shard", "seq"), axis=0, tiled=True),
        lax.all_gather(shared[4], ("shard", "seq"), axis=0, tiled=True),
        lax.all_gather(shared[5], ("shard", "seq"), axis=0, tiled=True),
        lax.all_gather(shared[6], ("shard", "seq"), axis=0, tiled=True),
        lax.all_gather(shared[7], ("shard", "seq"), axis=0, tiled=True),
    )
    w_qkv, w_out_attn, g_attn, g_ffn, table, router = unpack(gathered)
    inputs = tokens.astype(jnp.float32)
    attn_normed, attn_pull = jax.vjp(rms_norm, inputs, g_attn)
    normed_one = attn_normed.astype(jnp.bfloat16)
    projected = low_dot(normed_one, w_qkv).astype(jnp.bfloat16)
    queries = projected[:, :D]
    key_value = projected[:, D:]
    padded_kv = with_halo(key_value, (("seq", 0),), half_window)
    first_place = lax.axis_index("seq") * row_count
    doc_ends = jnp.cumsum(doc_lengths[0])
    total_live = doc_ends[DOCS - 1]
    q_places = first_place + jnp.arange(row_count, dtype=jnp.int32)
    k_places = first_place - half_window + jnp.arange(row_count + 2 * half_window, dtype=jnp.int32)
    q_docs = doc_index(q_places, doc_ends)
    k_docs = doc_index(k_places, doc_ends)
    q_live = q_places < total_live
    k_live = (k_places >= 0) & (k_places < total_live)
    limits = thresholds(MAXDIST, BUCKETS // 2)
    offsets = jnp.arange(band_len, dtype=jnp.int32) - half_window
    band_hot = (
        bucket_of(offsets, BUCKETS // 2, limits)[:, None]
        == jnp.arange(BUCKETS, dtype=jnp.int32)[None, :]
    ).astype(jnp.float32)
    band = jnp.dot(band_hot, table, precision=PRECISE).T
    rel_bias = toeplitz(band, block_rows)
    reach = (
        jnp.arange(span, dtype=jnp.int32)[None, :]
        - jnp.arange(block_rows, dtype=jnp.int32)[:, None]
    )
    in_band = (reach >= 0) & (reach <= 2 * half_window)
    on_diag = reach == half_window
    q_heads = queries.reshape(row_count, HEADS, HEAD)
    k_heads = padded_kv[:, :D].reshape(-1, HEADS, HEAD)
    v_heads = padded_kv[:, D:].reshape(-1, HEADS, HEAD)

    def block_scores(block_id):
        first_row = block_id * block_rows
        q_block = lax.dynamic_slice_in_dim(q_heads, first_row, block_rows, 0)
        k_block = lax.dynamic_slice_in_dim(k_heads, first_row, span, 0)
        v_block = lax.dynamic_slice_in_dim(v_heads, first_row, span, 0)
        q_doc_block = lax.dynamic_slice_in_dim(q_docs, first_row, block_rows, 0)
        k_doc_block = lax.dynamic_slice_in_dim(k_docs, first_row, span, 0)
        k_live_block = lax.dynamic_slice_in_dim(k_live, first_row, span, 0)
        allowed = (q_doc_block[:, None] == k_doc_block[None, :]) & k_live_block[
            None, :
        ] & in_band | on_diag
        scores = (
            jnp.einsum("qhd,khd->hqk", q_block, k_block, preferred_element_type=jnp.float32)
            + rel_bias
        )
        scores = jnp.where(allowed[None], scores, MASKED_SCORE)
        return (q_block, k_block, v_block, scores)

    def forward_block(block_id):
        q_block, k_block, v_block, scores = block_scores(block_id)
        peak = jnp.max(scores, axis=-1, keepdims=True)
        expo = jnp.exp(scores - peak)
        totals = jnp.sum(expo, axis=-1, keepdims=True)
        weights = (expo / totals).astype(jnp.bfloat16)
        context_block = jnp.einsum(
            "hqk,khd->qhd", weights, v_block, preferred_element_type=jnp.float32
        )
        return (context_block.astype(jnp.bfloat16), (peak + jnp.log(totals))[:, :, 0])

    ctx_blocks, lse_blocks = lax.map(forward_block, jnp.arange(block_count, dtype=jnp.int32))
    context = ctx_blocks.reshape(row_count, D)
    attn_out = low_dot(context, w_out_attn)
    hidden_state = inputs + attn_out
    ffn_normed, ffn_pull = jax.vjp(rms_norm, hidden_state, g_ffn)
    normed_two = ffn_normed.astype(jnp.bfloat16)
    router_logits = low_dot(normed_two, router)
    router_probs = jax.nn.softmax(router_logits, axis=-1)
    is_live = q_live.astype(jnp.float32)
    chosen_ids = expert_ids[:, 0]
    chosen = (chosen_ids[:, None] == jnp.arange(experts, dtype=jnp.int32)[None, :]).astype(
        jnp.int32
    ) * q_live.astype(jnp.int32)[:, None]
    chosen_f = chosen.astype(jnp.float32)
    gating = jnp.sum(router_probs * chosen_f, axis=1)
    ranked = jnp.cumsum(chosen, axis=0)
    slot_index = jnp.sum(ranked * chosen, axis=1) - 1
    target = jnp.where(q_live, chosen_ids * capacity + slot_index, experts * capacity)
    counts_all, mass_all = lax.psum(
        (jnp.sum(chosen_f, axis=0), jnp.sum(router_probs * is_live[:, None], axis=0)),
        ("rep", "shard", "seq"),
    )
    live_all = jnp.sum(counts_all)
    shares = counts_all / live_all
    balance = experts * jnp.sum(shares * mass_all) / live_all
    importance = experts * mass_all / (row_count * all_devices)
    outgoing = (
        jnp.zeros((experts * capacity, D), jnp.bfloat16)
        .at[target]
        .set(normed_two, mode="drop")
        .reshape(experts, capacity, D)
    )
    arrived = lax.all_to_all(outgoing, ("shard", "seq"), split_axis=0, concat_axis=0, tiled=True)
    item_count = arrived.shape[1]
    grid = arrived.reshape(group_size, EXP_DEV, item_count, D)
    pre_act = jnp.einsum("gecd,edf->gecf", grid, w_expert_in, preferred_element_type=jnp.float32)
    inner_act = gelu_tanh(pre_act).astype(jnp.bfloat16)
    produced = jnp.einsum(
        "gecf,efd->gecd", inner_act, w_expert_out, preferred_element_type=jnp.float32
    ).astype(jnp.bfloat16)
    returned = lax.all_to_all(
        produced.reshape(experts, item_count, D),
        ("shard", "seq"),
        split_axis=0,
        concat_axis=0,
        tiled=True,
    )
    came_back = jnp.concatenate(
        [returned.reshape(experts * capacity, D), jnp.zeros((1, D), jnp.bfloat16)], axis=0
    )
    expert_rows = came_back[target].astype(jnp.float32)
    mixed = (hidden_state + gating[:, None] * expert_rows).astype(jnp.bfloat16)
    upstream = cotangent.astype(jnp.float32)
    d_gating = jnp.sum(upstream * expert_rows, axis=1)
    d_rows = (gating[:, None] * upstream).astype(jnp.bfloat16)
    grad_out = (
        jnp.zeros((experts * capacity, D), jnp.bfloat16)
        .at[target]
        .set(d_rows, mode="drop")
        .reshape(experts, capacity, D)
    )
    grad_in = lax.all_to_all(grad_out, ("shard", "seq"), split_axis=0, concat_axis=0, tiled=True)
    grid_in = arrived.reshape(group_size, EXP_DEV, capacity, D)
    pre_kept = pre_act.reshape(experts, item_count, FF).reshape(group_size, EXP_DEV, capacity, FF)
    grid_grad = grad_in.reshape(group_size, EXP_DEV, capacity, D)
    gelu_value, gelu_pull = jax.vjp(gelu_tanh, pre_kept)
    inner_act = gelu_value.astype(jnp.bfloat16)
    d_inner = jnp.einsum(
        "gecd,efd->gecf", grid_grad, w_expert_out, preferred_element_type=jnp.float32
    )
    d_pre = gelu_pull(d_inner)[0].astype(jnp.bfloat16)
    d_routed = jnp.einsum(
        "gecf,edf->gecd", d_pre, w_expert_in, preferred_element_type=jnp.float32
    ).astype(jnp.bfloat16)
    d_expert_out = jnp.einsum(
        "gecf,gecd->efd", inner_act, grid_grad, preferred_element_type=jnp.float32
    )
    d_expert_in = jnp.einsum("gecd,gecf->edf", grid_in, d_pre, preferred_element_type=jnp.float32)
    back_grad = lax.all_to_all(
        d_routed.reshape(experts, capacity, D),
        ("shard", "seq"),
        split_axis=0,
        concat_axis=0,
        tiled=True,
    )
    back_rows = jnp.concatenate(
        [back_grad.reshape(experts * capacity, D), jnp.zeros((1, D), jnp.bfloat16)], axis=0
    )
    d_normed_expert = back_rows[target].astype(jnp.float32)
    d_probs = (
        chosen_f * d_gating[:, None]
        + is_live[:, None] * (AUX_WEIGHT * experts / live_all) * shares[None, :]
    )
    d_logits = (
        router_probs * (d_probs - jnp.sum(d_probs * router_probs, axis=1, keepdims=True))
    ).astype(jnp.bfloat16)
    d_normed_two = d_normed_expert + low_dot(d_logits, router.T)
    d_router = jnp.einsum("td,te->de", normed_two, d_logits, preferred_element_type=jnp.float32)
    hidden_back = ffn_pull(d_normed_two)
    d_hidden = upstream + hidden_back[0]
    d_gain_ffn = hidden_back[1]
    d_attn = d_hidden.astype(jnp.bfloat16)
    d_context = low_dot(d_attn, w_out_attn.T).astype(jnp.bfloat16)
    d_attn_out = jnp.einsum("td,te->de", context, d_attn, preferred_element_type=jnp.float32)
    dctx_heads = d_context.reshape(row_count, HEADS, HEAD)

    def backward_block(carry, block_id):
        kv_grad, diag_grad = carry
        q_block, k_block, v_block, scores = block_scores(block_id)
        first_row = block_id * block_rows
        lse_block = lse_blocks[block_id]
        probs = jnp.exp(scores - lse_block[:, :, None])
        weights = probs.astype(jnp.bfloat16)
        d_block = lax.dynamic_slice_in_dim(dctx_heads, first_row, block_rows, 0)
        d_weights = jnp.einsum("qhd,khd->hqk", d_block, v_block, preferred_element_type=jnp.float32)
        d_values = jnp.einsum("hqk,qhd->khd", weights, d_block, preferred_element_type=jnp.float32)
        inner_sum = jnp.sum(d_weights * probs, axis=-1, keepdims=True)
        d_scores = (probs * (d_weights - inner_sum)).astype(jnp.bfloat16)
        d_queries = jnp.einsum(
            "hqk,khd->qhd", d_scores, k_block, preferred_element_type=jnp.float32
        ).astype(jnp.bfloat16)
        d_keys = jnp.einsum("hqk,qhd->khd", d_scores, q_block, preferred_element_type=jnp.float32)
        piece = jnp.concatenate([d_keys.reshape(span, D), d_values.reshape(span, D)], axis=1)
        current = lax.dynamic_slice_in_dim(kv_grad, first_row, span, 0)
        kv_grad = lax.dynamic_update_slice_in_dim(kv_grad, current + piece, first_row, 0)
        diag_grad = diag_grad + diag_sums(d_scores.astype(jnp.float32), block_rows, band_len)
        return ((kv_grad, diag_grad), (d_queries.reshape(block_rows, D), inner_sum[:, :, 0]))

    start_carry = (
        jnp.zeros((row_count + 2 * half_window, 2 * D), jnp.float32),
        jnp.zeros((HEADS, band_len), jnp.float32),
    )
    final_carry, scan_out = lax.scan(
        backward_block, start_carry, jnp.arange(block_count, dtype=jnp.int32)
    )
    kv_grad, diag_grad = final_carry
    dq_blocks, inner_blocks = scan_out
    d_queries_all = dq_blocks.reshape(row_count, D)
    center = kv_grad[half_window : half_window + row_count]
    from_above = passed_along(kv_grad[:half_window].astype(jnp.bfloat16), "seq", -1).astype(
        jnp.float32
    )
    from_below = passed_along(
        kv_grad[half_window + row_count :].astype(jnp.bfloat16), "seq", 1
    ).astype(jnp.float32)
    center = center.at[:half_window].add(from_below).at[row_count - half_window :].add(from_above)
    d_projected = jnp.concatenate([d_queries_all, center.astype(jnp.bfloat16)], axis=1)
    d_normed_one = low_dot(d_projected, w_qkv.T)
    d_w_qkv = jnp.einsum("td,te->de", normed_one, d_projected, preferred_element_type=jnp.float32)
    attn_back = attn_pull(d_normed_one)
    d_tokens = d_hidden + attn_back[0]
    d_gain_attn = attn_back[1]
    d_table = jnp.dot(band_hot.T, diag_grad.T, precision=PRECISE)
    reduced = (
        lax.psum_scatter(
            d_w_qkv[:, :D].astype(jnp.bfloat16), ("shard", "seq"), scatter_dimension=0, tiled=True
        ).astype(jnp.float32),
        lax.psum_scatter(
            d_w_qkv[:, D : 2 * D].astype(jnp.bfloat16),
            ("shard", "seq"),
            scatter_dimension=0,
            tiled=True,
        ).astype(jnp.float32),
        lax.psum_scatter(
            d_w_qkv[:, 2 * D :].astype(jnp.bfloat16),
            ("shard", "seq"),
            scatter_dimension=0,
            tiled=True,
        ).astype(jnp.float32),
        lax.psum_scatter(
            d_attn_out.astype(jnp.bfloat16), ("shard", "seq"), scatter_dimension=0, tiled=True
        ).astype(jnp.float32),
        lax.psum_scatter(
            d_gain_attn.astype(jnp.bfloat16), ("shard", "seq"), scatter_dimension=0, tiled=True
        ).astype(jnp.float32),
        lax.psum_scatter(
            d_gain_ffn.astype(jnp.bfloat16), ("shard", "seq"), scatter_dimension=0, tiled=True
        ).astype(jnp.float32),
        lax.psum_scatter(
            d_table.astype(jnp.bfloat16), ("shard", "seq"), scatter_dimension=0, tiled=True
        ).astype(jnp.float32),
        lax.psum_scatter(
            d_router.astype(jnp.bfloat16), ("shard", "seq"), scatter_dimension=0, tiled=True
        ).astype(jnp.float32),
    )
    summed = (
        lax.psum(reduced[0].astype(jnp.bfloat16), "rep").astype(jnp.float32),
        lax.psum(reduced[1].astype(jnp.bfloat16), "rep").astype(jnp.float32),
        lax.psum(reduced[2].astype(jnp.bfloat16), "rep").astype(jnp.float32),
        lax.psum(reduced[3].astype(jnp.bfloat16), "rep").astype(jnp.float32),
        lax.psum(reduced[4].astype(jnp.bfloat16), "rep").astype(jnp.float32),
        lax.psum(reduced[5].astype(jnp.bfloat16), "rep").astype(jnp.float32),
        lax.psum(reduced[6].astype(jnp.bfloat16), "rep").astype(jnp.float32),
        lax.psum(reduced[7].astype(jnp.bfloat16), "rep").astype(jnp.float32),
        lax.psum(d_expert_in.astype(jnp.bfloat16), "rep").astype(jnp.float32),
        lax.psum(d_expert_out.astype(jnp.bfloat16), "rep").astype(jnp.float32),
    )
    return (
        mixed,
        balance,
        importance,
        d_tokens,
        summed[4],
        summed[5],
        summed[0],
        summed[1],
        summed[2],
        summed[3],
        summed[6],
        summed[7],
        summed[8],
        summed[9],
    )


def solution(mesh):
    return jax.shard_map(
        shards,
        mesh=mesh,
        in_specs=(
            P(("rep", "shard", "seq"), None),
            P(("rep", "shard"), None),
            P(("rep", "shard", "seq"), None),
            P(("rep", "shard", "seq"), None),
            P(("shard", "seq")),
            P(("shard", "seq")),
            P(("shard", "seq"), None),
            P(("shard", "seq"), None),
            P(("shard", "seq"), None),
            P(("shard", "seq"), None),
            P(("shard", "seq"), None),
            P(("shard", "seq"), None),
            P(("shard", "seq"), None, None),
            P(("shard", "seq"), None, None),
        ),
        out_specs=(
            P(("rep", "shard", "seq"), None),
            P(),
            P(),
            P(("rep", "shard", "seq"), None),
            P(("shard", "seq")),
            P(("shard", "seq")),
            P(("shard", "seq"), None),
            P(("shard", "seq"), None),
            P(("shard", "seq"), None),
            P(("shard", "seq"), None),
            P(("shard", "seq"), None),
            P(("shard", "seq"), None),
            P(("shard", "seq"), None, None),
            P(("shard", "seq"), None, None),
        ),
        check_vma=False,
    )
```

profile of v0, /device:TPU:0, one launch (start us, length us, event | category | flops | bytes accessed | tf_op | source)
XLA Modules:
  0.0 2036.8 jit_solution(10104393480380658290)
XLA Ops:
  16.5 35.1 %all-reduce.10 = (bf16[768]{0:T(1024)(128)(2,1)S(1)}, bf16[768]{0:T(1024)(128)(2,1)S(1)}) all-reduce(bf16[768]{0:T(1024)(128)(2,1)S(1)} %dynamic-update-slice.6, bf16[768]{0:T(1024)(128)(2,1)S(1)} %dynamic-update-slice.7), channel_id=1, replica_groups=mesh['rep'=2,'shard'=4,'seq'=4] {'shard','seq'}, use_global_device_ids=true, to_apply=%add.4 | all-reduce | flops 1536 | bytes 6144
  52.1 17.2 all-gather
  78.1 13.4 broadcast_in_dim.57
  91.4 87.0 %reshape.467 = f32[12,786944]{1,0:T(8,128)} reshape(f32[12,512,1537]{2,1,0:T(8,128)} %broadcast_in_dim.57) | data formatting | bytes 75546624 | tf_op jit(solution)/shard_map/reshape | solution.py:94
  178.4 33.3 %slice.128 = f32[12,786432]{1,0:T(8,128)} slice(f32[12,786944]{1,0:T(8,128)} %reshape.467), slice={[0:12], [0:786432]} | slice | bytes 75497472 | tf_op jit(solution)/shard_map/slice | solution.py:94
  211.8 46.0 %copy.114 = f32[2,8,512,1536]{3,2,1,0:T(8,128)} copy(f32[2,8,512,1536]{3,1,2,0:T(8,128)} %bitcast.216) | data formatting | bytes 100663296
  257.7 27.6 %slice.137 = f32[12,512,1536]{2,1,0:T(8,128)} slice(f32[16,512,1536]{2,1,0:T(8,128)} %bitcast.217), slice={[0:12], [0:512], [0:1536]} | slice | bytes 75497472 | tf_op jit(solution)/shard_map/reshape | solution.py:95
  328.2 132.1 %while.30 = (s32[]{:T(128)}, bf16[2,512,12,64]{1,3,2,0:T(8,128)(2,1)}, f32[2,12,512]{2,1,0:T(8,128)}, s32[2]{0:T(128)S(1)}, bf16[2048,12,64]{0,2,1:T(8,128)(2,1)...) while((s32[]{:T(128)}, ...), condition=%wide.region_7.8_spmd.clone, body=%wide.region_4.7_spmd.clone.sunk | while | flops 2498881536 | bytes 184275824 | solution.py:220
  333.3 28.4 %fusion.219 = (f32[12,512]{1,0:T(8,128)S(1)}, f32[12,512,1536]{2,1,0:T(8,128)}) fusion(f32[12,512,1536]{2,1,0:T(8,128)} %get-tuple-element.651, bf16[2048,12,64]{0,2,1:T(8,128)(2,1)S(1)} %get-tuple-element.650, s32[]{:T(128)S(6)} %select_n.71, bf16[1024,12,64]{0,2,1:T(8,128)(2,1)} %get-tuple-element.649, s32[]{:T(128)S(6)} %select_n.72, ...), kind=kOutput, calls=%fused_computation.226.clone.1 | convolution fusion | flops 1236264960 | bytes 79454216 | tf_op jit(solution)/shard_map/while/body/eval_jaxpr/qhd,khd->hqk/dot_general | solution.py:203
  361.7 16.8 fusion.220
  378.6 14.4 fusion.221
  399.2 28.4 %fusion.219 = (f32[12,512]{1,0:T(8,128)S(1)}, f32[12,512,1536]{2,1,0:T(8,128)}) fusion(f32[12,512,1536]{2,1,0:T(8,128)} %get-tuple-element.651, bf16[2048,12,64]{0,2,1:T(8,128)(2,1)S(1)} %get-tuple-element.650, s32[]{:T(128)S(6)} %select_n.71, bf16[1024,12,64]{0,2,1:T(8,128)(2,1)} %get-tuple-element.649, s32[]{:T(128)S(6)} %select_n.72, ...), kind=kOutput, calls=%fused_computation.226.clone.1 | convolution fusion | flops 1236264960 | bytes 79454216 | tf_op jit(solution)/shard_map/while/body/eval_jaxpr/qhd,khd->hqk/dot_general | solution.py:203
  427.7 16.8 fusion.220
  444.5 14.4 fusion.221
  481.8 59.7 %all_to_all.20 = bf16[16,80,768]{2,1,0:T(8,128)(2,1)S(1)} all-to-all(bf16[16,80,768]{2,1,0:T(8,128)(2,1)} %bitcast.223), channel_id=1, replica_groups=mesh['rep'=2,'shard'=4,'seq'=4] {'shard','seq'}, dimensions={0} | all-to-all | bytes 3932160 | tf_op jit(solution)/shard_map/all_to_all | solution.py:252
  571.6 66.3 %psum.84 = f32[16]{0:T(128)S(1)} all-reduce(f32[16]{0:T(128)S(1)} %fusion.132), channel_id=1, replica_groups=mesh['rep'=2,'shard'=4,'seq'=4] {'rep','shard','seq'}, use_global_device_ids=true, to_apply=%region_17.18 | all-reduce | flops 16 | bytes 128 | tf_op jit(solution)/shard_map/psum | solution.py:238
  638.5 21.3 %all-gather.1 = bf16[16,48,16]{1,2,0:T(8,128)(2,1)S(1)} all-gather(bf16[1,48,16]{1,2,0:T(8,128)(2,1)S(1)} %bitcast.241), channel_id=1, replica_groups=mesh['rep'=2,'shard'=4,'seq'=4] {'shard','seq'}, dimensions={0}, use_global_device_ids=true | all-gather | bytes 26112 | tf_op jit(solution)/shard_map/all_gather | solution.py:154
  695.2 49.1 %all_to_all.21 = bf16[16,80,768]{2,1,0:T(8,128)(2,1)S(1)} all-to-all(bf16[16,80,768]{2,1,0:T(8,128)(2,1)} %bitcast.222), channel_id=1, replica_groups=mesh['rep'=2,'shard'=4,'seq'=4] {'shard','seq'}, dimensions={0} | all-to-all | bytes 3932160 | tf_op jit(solution)/shard_map/all_to_all | solution.py:281
  744.3 19.2 fusion.63
  777.6 38.8 %all-to-all-done.3 = bf16[16,80,768]{2,1,0:T(8,128)(2,1)} async-done(((bf16[16,80,768]{2,1,0:T(8,128)(2,1)}), bf16[16,80,768]{2,1,0:T(8,128)(2,1)}, u32[]{:S(2)}, u32[]{:S(2)}) %all-to-all-start.3) | async-done | bytes 1966112 | tf_op jit(solution)/shard_map/all_to_all | solution.py:298
  845.7 608.5 %while.31 = (s32[]{:T(128)}, f32[2048,1536]{0,1:T(8,128)}, f32[12,1025]{1,0:T(8,128)}, bf16[2,512,768]{2,1,0:T(8,128)(2,1)}, s32[2]{0:T(128)}, /*index=5*/bf16[1...) while((s32[]{:T(128)}, f32[2048,1536]{0,1:T(8,128)}, ...), condition=%wide.region_29.30_spmd.clone, body=%wide.region_26.29_spmd.clone.sunk | while | flops 6155808768 | bytes 735401600 | solution.py:352
  853.9 26.3 %subtract_exponential_fusion.4 = f32[12,512,1536]{2,1,0:T(8,128)} fusion(f32[12,512,1536]{2,1,0:T(8,128)} %get-tuple-element.711, f32[12,512]{1,0:T(8,128)S(1)} %dynamic-slice_bitcast_fusion.2, pred[512,1536]{1,0:T(8,128)(4,1)S(1)} %fusion.230, bf16[2048,12,64]{0,2,1:T(8,128)(2,1)S(1)} %get-tuple-element.710, s32[]{:T(128)S(6)} %select_n.74, ...), kind=kOutput, calls=%fused_computation.31.clone.1 | convolution fusion | flops 1236271104 | bytes 79462408 | tf_op jit(solution)/shard_map/while/body/eval_jaxpr/qhd,khd->hqk/dot_general | solution.py:203
  880.2 16.0 fusion.231
  896.2 28.6 %multiply_reduce_fusion.8 = (f32[12,512]{1,0:T(8,128)S(1)}, f32[12,512,1536]{2,1,0:T(8,128)}) fusion(f32[12,512,1536]{2,1,0:T(8,128)} %subtract_exponential_fusion.4, bf16[2048,12,64]{0,2,1:T(8,128)(2,1)} %get-tuple-element.714, s32[]{:T(128)S(6)} %select_n.74, bf16[1024,12,64]{0,2,1:T(8,128)(2,1)} %get-tuple-element.713, s32[]{:T(128)S(6)} %select_n.76), kind=kOutput, calls=%fused_computation.30.clone.1 | convolution fusion | flops 1226827776 | bytes 78667784 | tf_op jit(solution)/shard_map/while/body/eval_jaxpr/qhd,khd->hqk/dot_general | solution.py:334
  924.8 31.0 %multiply_convert_fusion.6 = bf16[12,512,1536]{2,1,0:T(8,128)(2,1)} fusion(f32[12,512,1536]{2,1,0:T(8,128)} %subtract_exponential_fusion.4, f32[12,512,1536]{2,1,0:T(8,128)} %get-tuple-element.607, f32[12,512]{1,0:T(8,128)S(1)} %get-tuple-element.608), kind=kLoop, calls=%fused_computation.29.clone.1 | loop fusion | flops 28311552 | bytes 94396416 | tf_op jit(solution)/shard_map/while/body/eval_jaxpr/convert_element_type | solution.py:337
  969.0 12.3 fusion.232
  1000.3 22.7 %copy.120 = bf16[2,8,512,1536]{3,1,2,0:T(8,128)(2,1)S(1)} copy(bf16[2,8,512,1536]{3,2,1,0:T(8,128)(2,1)} %bitcast.209) | data formatting | bytes 50331648 | tf_op jit(solution)/shard_map/while
  1023.0 16.1 pad_convert_fusion.2
  1039.1 91.9 %reshape.551 = f32[12,512,1537]{2,1,0:T(8,128)} reshape(f32[12,786944]{1,0:T(8,128)} %pad_convert_fusion.2) | data formatting | bytes 75546624 | tf_op jit(solution)/shard_map/while/body/eval_jaxpr/reshape | solution.py:103
  1131.0 15.3 reduce_sum.239
  1155.0 26.4 %subtract_exponential_fusion.4 = f32[12,512,1536]{2,1,0:T(8,128)} fusion(f32[12,512,1536]{2,1,0:T(8,128)} %get-tuple-element.711, f32[12,512]{1,0:T(8,128)S(1)} %dynamic-slice_bitcast_fusion.2, pred[512,1536]{1,0:T(8,128)(4,1)S(1)} %fusion.230, bf16[2048,12,64]{0,2,1:T(8,128)(2,1)S(1)} %get-tuple-element.710, s32[]{:T(128)S(6)} %select_n.74, ...), kind=kOutput, calls=%fused_computation.31.clone.1 | convolution fusion | flops 1236271104 | bytes 79462408 | tf_op jit(solution)/shard_map/while/body/eval_jaxpr/qhd,khd->hqk/dot_general | solution.py:203
  1181.4 16.0 fusion.231
  1197.4 28.5 %multiply_reduce_fusion.8 = (f32[12,512]{1,0:T(8,128)S(1)}, f32[12,512,1536]{2,1,0:T(8,128)}) fusion(f32[12,512,1536]{2,1,0:T(8,128)} %subtract_exponential_fusion.4, bf16[2048,12,64]{0,2,1:T(8,128)(2,1)} %get-tuple-element.714, s32[]{:T(128)S(6)} %select_n.74, bf16[1024,12,64]{0,2,1:T(8,128)(2,1)} %get-tuple-element.713, s32[]{:T(128)S(6)} %select_n.76), kind=kOutput, calls=%fused_computation.30.clone.1 | convolution fusion | flops 1226827776 | bytes 78667784 | tf_op jit(solution)/shard_map/while/body/eval_jaxpr/qhd,khd->hqk/dot_general | solution.py:334
  1225.9 31.0 %multiply_convert_fusion.6 = bf16[12,512,1536]{2,1,0:T(8,128)(2,1)} fusion(f32[12,512,1536]{2,1,0:T(8,128)} %subtract_exponential_fusion.4, f32[12,512,1536]{2,1,0:T(8,128)} %get-tuple-element.607, f32[12,512]{1,0:T(8,128)S(1)} %get-tuple-element.608), kind=kLoop, calls=%fused_computation.29.clone.1 | loop fusion | flops 28311552 | bytes 94396416 | tf_op jit(solution)/shard_map/while/body/eval_jaxpr/convert_element_type | solution.py:337
  1270.0 12.3 fusion.232
  1301.4 22.7 %copy.120 = bf16[2,8,512,1536]{3,1,2,0:T(8,128)(2,1)S(1)} copy(bf16[2,8,512,1536]{3,2,1,0:T(8,128)(2,1)} %bitcast.209) | data formatting | bytes 50331648 | tf_op jit(solution)/shard_map/while
  1324.1 16.1 pad_convert_fusion.2
  1340.1 91.9 %reshape.551 = f32[12,512,1537]{2,1,0:T(8,128)} reshape(f32[12,786944]{1,0:T(8,128)} %pad_convert_fusion.2) | data formatting | bytes 75546624 | tf_op jit(solution)/shard_map/while/body/eval_jaxpr/reshape | solution.py:103
  1432.1 15.3 reduce_sum.239
  1501.3 14.1 fusion.91
  1526.5 13.4 reduce-scatter.14.cloned.1.call-done
  1539.9 60.6 %reduce-scatter.12.cloned.1.call-done = bf16[48,768]{1,0:T(8,128)(2,1)} async-done(((bf16[768,768]{1,0:T(8,128)(2,1)}), bf16[48,768]{1,0:T(8,128)(2,1)}) %reduce-scatter.12.cloned.1.call-update) | async-done | bytes 73744 | tf_op jit(solution)/shard_map/reduce_scatter | solution.py:383
  1600.5 60.7 %reduce-scatter.10.cloned.1.call-done = bf16[48,768]{1,0:T(8,128)(2,1)} async-done(((bf16[768,768]{1,0:T(8,128)(2,1)}), bf16[48,768]{1,0:T(8,128)(2,1)}) %reduce-scatter.10.cloned.1.call-update) | async-done | bytes 73744 | tf_op jit(solution)/shard_map/reduce_scatter | solution.py:377
  1661.2 60.7 %reduce-scatter.8.cloned.1.call-done = bf16[48,768]{1,0:T(8,128)(2,1)} async-done(((bf16[768,768]{1,0:T(8,128)(2,1)}), bf16[48,768]{1,0:T(8,128)(2,1)}) %reduce-scatter.8.cloned.1.call-update) | async-done | bytes 73744 | tf_op jit(solution)/shard_map/reduce_scatter | solution.py:374
  1723.4 40.1 %psum.85 = f32[16]{0:T(128)S(1)} all-reduce(f32[16]{0:T(128)S(1)} %copy-done.60), channel_id=1, replica_groups=mesh['rep'=2,'shard'=4,'seq'=4] {'rep','shard','seq'}, use_global_device_ids=true, to_apply=%region_20.21 | all-reduce | flops 16 | bytes 128 | tf_op jit(solution)/shard_map/psum | solution.py:238
  1766.6 11.5 reduce-scatter.16.cloned.1.call-done
  1794.5 57.8 %all-reduce.9 = (bf16[768]{0:T(1024)(128)(2,1)S(1)}, bf16[768]{0:T(1024)(128)(2,1)S(1)}, bf16[32,12]{1,0:T(8,128)(2,1)S(1)}) all-reduce(bf16[768]{0:T(1024)(128)(2,1)S(1)} %get-tuple-element.352, bf16[768]{0:T(1024)(128)(2,1)S(1)} %copy-done.54, ...), channel_id=2, replica_groups=mesh['rep'=2,'shard'=4,'seq'=4] {'shard','seq'}, use_global_device_ids=true, to_apply=%region_32.33.clone | all-reduce | flops 1920 | bytes 7680
  1859.8 150.6 %all-reduce.15.cloned.1.call-done = (bf16[48,768]{1,0:T(8,128)(2,1)}, bf16[48,768]{1,0:T(8,128)(2,1)}, bf16[48,768]{1,0:T(8,128)(2,1)}, bf16[48,768]{1,0:T(8,128...) async-done(((bf16[48,768]{1,0:T(8,128)(2,1)}, bf16[48,768]{1,0:T(8,128)(2,1)}, bf16[48,768]{1,0:T(8,128)(2,1)}, bf16[48,768]{1,0:T(8,128)(2,1)}, ...) | async-done | bytes 9732112 | tf_op jit(solution)/shard_map/psum | solution.py:406
  (387 shorter events, 379.5 us)
Async XLA Ops:
  7.2 278.1 %all-gather.7.cloned.1.call-start = ((), (), s32[]{:S(2)}) async-start(), calls=%async_computation.9 | async-start | bytes 1253376 | tf_op jit(solution)/shard_map/all_gather | solution.py:147
  7.9 279.8 %all-gather.9.cloned.1.call-start = ((), (), s32[]{:S(2)}) async-start(), calls=%async_computation.10 | async-start | bytes 1253376 | tf_op jit(solution)/shard_map/all_gather | solution.py:148
  8.7 281.5 %all-gather.11.cloned.1.call-start = ((), (), s32[]{:S(2)}) async-start(), calls=%async_computation.11 | async-start | bytes 1253376 | tf_op jit(solution)/shard_map/all_gather | solution.py:149
  9.4 455.6 %all-gather.13.cloned.1.call-start = ((), (), s32[]{:S(2)}) async-start(), calls=%async_computation.12 | async-start | bytes 1253376 | tf_op jit(solution)/shard_map/all_gather | solution.py:150
  12.1 296.3 %copy-start.33 = (s32[1024]{0:T(1024)}, s32[1024]{0:T(1024)S(1)}, u32[]{:S(2)}) copy-start(s32[1024]{0:T(1024)S(1)} %fusion.161) | copy-start | bytes 12292
  12.7 78.7 %copy-start.55 = (s32[1025]{0:T(1024)}, s32[1025]{0:T(1024)S(1)}, u32[]{:S(2)}) copy-start(s32[1025]{0:T(1024)S(1)} %convert_add_fusion.3) | copy-start | bytes 12304
  51.5 241.0 %copy-start.49 = (f32[768]{0:T(1024)}, f32[768]{0:T(1024)S(1)}, u32[]{:S(2)}) copy-start(f32[768]{0:T(1024)S(1)} %convert_element_type.337) | copy-start | bytes 9220
  76.6 216.0 %copy-start.8 = (bf16[1024,768]{0,1:T(8,128)(2,1)}, bf16[1024,768]{0,1:T(8,128)(2,1)S(1)}, u32[]{:S(2)}) copy-start(bf16[1024,768]{0,1:T(8,128)(2,1)S(1)} %copy.85) | copy-start | bytes 4718596
  77.0 215.6 %copy-start.51 = (f32[1024]{0:T(1024)}, f32[1024]{0:T(1024)S(1)}, u32[]{:S(2)}) copy-start(f32[1024]{0:T(1024)S(1)} %fusion.158) | copy-start | bytes 12292
  301.1 13.5 collective-permute-start
  304.4 10.1 collective-permute-start.1
  361.7 16.8 copy-start.26
  481.8 74.8 %slice-start.10 = ((s8[4718592]{0:T(1024)(128)(4,1)}), s8[4194304]{0:T(1024)(128)(4,1)S(1)}, s32[]{:S(2)}) async-start(s8[4718592]{0:T(1024)(128)(4,1)} %bitcast.247), calls=%async_computation.29 | async-start | bytes 8388608
  566.8 71.7 %copy-start.59 = (bf16[48,16]{0,1:T(8,128)(2,1)S(1)}, bf16[48,16]{0,1:T(8,128)(2,1)}, u32[]{:S(2)}) copy-start(bf16[48,16]{0,1:T(8,128)(2,1)} %param.33) | copy-start | bytes 4612
  566.8 98.8 %copy-start.53 = (s32[1024,1]{0,1:T(1,128)S(1)}, s32[1024,1]{0,1:T(1,128)}, u32[]{:S(2)}) copy-start(s32[1024,1]{0,1:T(1,128)} %get-tuple-element.422) | copy-start | bytes 12292
  566.8 100.7 %all-to-all-start.1 = ((bf16[16,80,768]{2,1,0:T(8,128)(2,1)}), bf16[16,80,768]{2,1,0:T(8,128)(2,1)}, u32[]{:S(2)}, u32[]{:S(2)}) async-start(bf16[16,80,768]{2,1,0:T(8,128)(2,1)} %fusion.109), calls=%async_computation.1 | async-start | bytes 3932160 | tf_op jit(solution)/shard_map/all_to_all | solution.py:260
  637.9 27.8 %copy-start.61 = (f32[16]{0:T(128)}, f32[16]{0:T(128)S(1)}, u32[]{:S(2)}) copy-start(f32[16]{0:T(128)S(1)} %psum.84) | copy-start | bytes 196
  665.0 164.4 %copy-start.42 = (f32[1024]{0:T(1024)}, f32[1024]{0:T(1024)S(1)}, u32[]{:S(2)}) copy-start(f32[1024]{0:T(1024)S(1)} %broadcast_select_fusion) | copy-start | bytes 12292
  665.6 163.8 %copy-start.57 = (f32[16]{0:T(128)}, f32[16]{0:T(128)S(1)}, u32[]{:S(2)}) copy-start(f32[16]{0:T(128)S(1)} %broadcast_divide_fusion) | copy-start | bytes 196
  667.4 162.0 %copy-start.23 = (f32[1024,16]{0,1:T(8,128)}, f32[1024,16]{0,1:T(8,128)S(1)}, u32[]{:S(2)}) copy-start(f32[1024,16]{0,1:T(8,128)S(1)} %get-tuple-element.446) | copy-start | bytes 196612
  667.4 162.0 %copy-start.36 = (f32[1024]{0:T(1024)}, f32[1024]{0:T(1024)S(1)}, u32[]{:S(2)}) copy-start(f32[1024]{0:T(1024)S(1)} %get-tuple-element.445) | copy-start | bytes 12292
  667.5 161.9 %copy-start.40 = (f32[1024]{0:T(1024)}, f32[1024]{0:T(1024)S(1)}, u32[]{:S(2)}) copy-start(f32[1024]{0:T(1024)S(1)} %fusion.139) | copy-start | bytes 12292
  683.1 146.3 %copy-start.38 = (f32[1024]{0:T(1024)}, f32[1024]{0:T(1024)S(1)}, u32[]{:S(2)}) copy-start(f32[1024]{0:T(1024)S(1)} %fusion.101) | copy-start | bytes 12292
  683.8 145.6 %copy-start.45 = (f32[1024]{0:T(1024)}, f32[1024]{0:T(1024)S(1)}, u32[]{:S(2)}) copy-start(f32[1024]{0:T(1024)S(1)} %get-tuple-element.354) | copy-start | bytes 12292
  695.2 68.3 %slice-start.12 = ((s8[4718592]{0:T(1024)(128)(4,1)}), s8[4194304]{0:T(1024)(128)(4,1)S(1)}, s32[]{:S(2)}) async-start(s8[4718592]{0:T(1024)(128)(4,1)} %bitcast.249), calls=%async_computation.31 | async-start | bytes 8388608
  744.3 19.2 copy-start.19
  744.3 19.2 slice-start.13
  773.1 43.3 %all-to-all-start.3 = ((bf16[16,80,768]{2,1,0:T(8,128)(2,1)}), bf16[16,80,768]{2,1,0:T(8,128)(2,1)}, u32[]{:S(2)}, u32[]{:S(2)}) async-start(bf16[16,80,768]{2,1,0:T(8,128)(2,1)} %fusion.114), calls=%async_computation.3 | async-start | bytes 3932160 | tf_op jit(solution)/shard_map/all_to_all | solution.py:298
  777.6 762.4 %reduce-scatter.14.cloned.1.call-start = ((), (), s32[]{:S(2)}) async-start(), calls=%async_computation.16 | async-start | bytes 1253376 | tf_op jit(solution)/shard_map/reduce_scatter | solution.py:389
  846.1 109.7 %copy-start = (bf16[2048,12,64]{0,2,1:T(8,128)(2,1)}, bf16[2048,12,64]{0,2,1:T(8,128)(2,1)S(1)}, u32[]{:S(2)}) copy-start(bf16[2048,12,64]{0,2,1:T(8,128)(2,1)S(1)} %get-tuple-element.710) | copy-start | bytes 9437188 | tf_op jit(solution)/shard_map/while
  969.0 21.5 %slice-start = ((s8[18874368]{0:T(1024)(128)(4,1)}), s8[4194304]{0:T(1024)(128)(4,1)S(1)}, s32[]{:S(2)}) async-start(s8[18874368]{0:T(1024)(128)(4,1)} %bitcast.207), calls=%async_computation.19 | async-start | bytes 8388608 | tf_op jit(solution)/shard_map/while
  969.0 21.5 %slice-start.1 = ((s8[18874368]{0:T(1024)(128)(4,1)}), s8[4194304]{0:T(1024)(128)(4,1)S(1)}, s32[]{:S(2)}) async-start(s8[18874368]{0:T(1024)(128)(4,1)} %bitcast.207), calls=%async_computation.20 | async-start | bytes 8388608 | tf_op jit(solution)/shard_map/while
  969.0 21.5 %slice-start.2 = ((s8[18874368]{0:T(1024)(128)(4,1)}), s8[4194304]{0:T(1024)(128)(4,1)S(1)}, s32[]{:S(2)}) async-start(s8[18874368]{0:T(1024)(128)(4,1)} %bitcast.207), calls=%async_computation.21 | async-start | bytes 8388608 | tf_op jit(solution)/shard_map/while
  1147.1 109.7 %copy-start = (bf16[2048,12,64]{0,2,1:T(8,128)(2,1)}, bf16[2048,12,64]{0,2,1:T(8,128)(2,1)S(1)}, u32[]{:S(2)}) copy-start(bf16[2048,12,64]{0,2,1:T(8,128)(2,1)S(1)} %get-tuple-element.710) | copy-start | bytes 9437188 | tf_op jit(solution)/shard_map/while
  1270.0 21.5 %slice-start = ((s8[18874368]{0:T(1024)(128)(4,1)}), s8[4194304]{0:T(1024)(128)(4,1)S(1)}, s32[]{:S(2)}) async-start(s8[18874368]{0:T(1024)(128)(4,1)} %bitcast.207), calls=%async_computation.19 | async-start | bytes 8388608 | tf_op jit(solution)/shard_map/while
  1270.0 21.5 %slice-start.1 = ((s8[18874368]{0:T(1024)(128)(4,1)}), s8[4194304]{0:T(1024)(128)(4,1)S(1)}, s32[]{:S(2)}) async-start(s8[18874368]{0:T(1024)(128)(4,1)} %bitcast.207), calls=%async_computation.20 | async-start | bytes 8388608 | tf_op jit(solution)/shard_map/while
  1270.0 21.5 %slice-start.2 = ((s8[18874368]{0:T(1024)(128)(4,1)}), s8[4194304]{0:T(1024)(128)(4,1)S(1)}, s32[]{:S(2)}) async-start(s8[18874368]{0:T(1024)(128)(4,1)} %bitcast.207), calls=%async_computation.21 | async-start | bytes 8388608 | tf_op jit(solution)/shard_map/while
  1461.7 15.3 collective-permute-start.2
  1465.5 16.6 collective-permute-start.3
  1476.1 124.4 %reduce-scatter.12.cloned.1.call-start = ((), (), s32[]{:S(2)}) async-start(), calls=%async_computation.15 | async-start | bytes 1253376 | tf_op jit(solution)/shard_map/reduce_scatter | solution.py:383
  1498.2 163.1 %reduce-scatter.10.cloned.1.call-start = ((), (), s32[]{:S(2)}) async-start(), calls=%async_computation.14 | async-start | bytes 1253376 | tf_op jit(solution)/shard_map/reduce_scatter | solution.py:377
  1498.9 223.0 %reduce-scatter.8.cloned.1.call-start = ((), (), s32[]{:S(2)}) async-start(), calls=%async_computation.13 | async-start | bytes 1253376 | tf_op jit(solution)/shard_map/reduce_scatter | solution.py:374
  1499.7 278.4 %reduce-scatter.16.cloned.1.call-start = ((), (), s32[]{:S(2)}) async-start(), calls=%async_computation.17 | async-start | bytes 208896
  1501.2 509.1 %all-reduce.15.cloned.1.call-start = ((), (), s32[]{:S(2)}) async-start(), calls=%async_computation.18 | async-start | bytes 19464192 | tf_op jit(solution)/shard_map/psum | solution.py:406
  1721.9 41.5 %copy-start.62 = (f32[16]{0:T(128)S(1)}, f32[16]{0:T(128)}, u32[]{:S(2)}) copy-start(f32[16]{0:T(128)} %copy-done.61) | copy-start | bytes 196
  1721.9 56.9 %copy-start.15 = (bf16[1024,768]{0,1:T(8,128)(2,1)S(1)}, bf16[1024,768]{0,1:T(8,128)(2,1)}, u32[]{:S(2)}) copy-start(bf16[1024,768]{0,1:T(8,128)(2,1)} %get-tuple-element.438) | copy-start | bytes 4718596
  1722.0 58.4 %copy-start.22 = (f32[12,1025]{1,0:T(8,128)S(1)}, f32[12,1025]{1,0:T(8,128)}, u32[]{:S(2)}) copy-start(f32[12,1025]{1,0:T(8,128)} %get-tuple-element.194) | copy-start | bytes 147604
  1722.0 58.4 %copy-start.56 = (s32[1025]{0:T(1024)S(1)}, s32[1025]{0:T(1024)}, u32[]{:S(2)}) copy-start(s32[1025]{0:T(1024)} %copy-done.55) | copy-start | bytes 12304
  (61 other events, 409.6 us)
Sparse Core Ops, SparseCore 0:
  10.3 41.1 all-gather.6
  53.7 37.3 all-gather.8
  93.4 37.2 all-gather.10
  132.9 37.2 all-gather.12
  1476.3 63.6 reduce-scatter.13
  1543.4 57.0 reduce-scatter.11
  1604.1 57.0 reduce-scatter.9
  1664.8 57.0 reduce-scatter.7
  1725.4 52.5 reduce-scatter.15
  1781.5 228.8 all-reduce.14
where the time goes:
time: 2040 us
  local copies, waits for them, and re-layouts  596 us (29%)
  waiting for transfers between devices  400 us (20%)
  matrix products  382 us (19%)
  blocking collectives  352 us (17%)
  other arithmetic  253 us (12%)
  between operations  20.6 us (1%)
    reshape x2, local copies, waits for them, and re-layouts, diag_sums(): padded = padded.reshape(head_count, block_rows, span + 1)  184 us
    psum x1, waiting for transfers between devices, shards(): lax.psum(reduced[0].astype(jnp.bfloat16), 'rep').astype(jnp.float32)  151 us
    dot_general x4, matrix products, block_scores(): jnp.einsum('qhd,khd->hqk', q_block, k_block, preferred_element_type=jnp.f...  109 us
    psum x2, blocking collectives, shards(): lax.psum((jnp.sum(chosen_f, axis=0), jnp.sum(router_probs * is_live[:, No...  106 us
    unnamed x2, blocking collectives  92.9 us
    reshape x1, local copies, waits for them, and re-layouts, toeplitz(): tiled.reshape(head_count, block_rows * (span + 1))[:, :block_rows * span]  87 us
    unnamed x147, local copies, waits for them, and re-layouts  76.5 us
    while x60, local copies, waits for them, and re-layouts  67.3 us
  transfers between devices with their start and end apart: 16, of which 7 were waited for; matrix products, arithmetic and copies ran while one was open for 24% of the time, Pallas kernels for 0%

commit v1 on v0

v1 whole, which is shorter than its diff:
```python
import functools
import math

import jax
import jax.numpy as jnp
import numpy as np
from jax import lax
from jax.experimental import pallas as pl
from jax.experimental.pallas import tpu as pltpu
from jax.sharding import PartitionSpec as P

D = 768
HEADS = 12
HEAD = 64
BUCKETS = 32
MAXDIST = 128
WINDOW = 1024
DOCS = 4
MASKED_SCORE = -1e30
HALF = WINDOW // 2
QB = 256
SUB = 128
KB = QB + WINDOW
PAIRS = HEADS // 2
VMEM_LIMIT = 56 * 1024 * 1024


def thresholds(max_distance, half_count):
    exact_span = half_count // 2
    collected = list(range(1, exact_span + 1))
    for target_level in range(exact_span + 1, half_count):
        candidate = exact_span
        while (
            exact_span
            + int(
                math.log(candidate / exact_span)
                / math.log(max_distance / exact_span)
                * (half_count - exact_span)
            )
            < target_level
        ):
            candidate += 1
        collected.append(candidate)
    return collected


LIMITS = thresholds(MAXDIST, BUCKETS // 2)
assert LIMITS[-1] <= SUB


def bucket_table(distance):
    distance = np.asarray(distance)
    magnitude = np.abs(distance)
    bucket_id = (distance > 0).astype(np.int32) * (BUCKETS // 2)
    for boundary in LIMITS:
        bucket_id = bucket_id + (magnitude >= boundary)
    return bucket_id


def bias_buckets():
    lane = np.arange(2 * SUB)
    rows = []
    for m in (-1, 0, 1):
        rows.append(bucket_table(SUB * m - lane + np.where(lane >= SUB, 2 * SUB, 0)))
    rows.append(np.full(2 * SUB, bucket_table(-WINDOW)))
    rows.append(np.full(2 * SUB, bucket_table(WINDOW)))
    rows += [np.zeros(2 * SUB, np.int32)] * 3
    return np.stack(rows)


def grad_buckets():
    lane = np.arange(SUB)
    rows = [bucket_table(SUB * m - lane) for m in (-1, 0, 1)]
    rows += [bucket_table(SUB * (m + 1) - lane) for m in (-1, 0, 1)]
    rows.append(np.full(SUB, bucket_table(-WINDOW)))
    rows.append(np.full(SUB, bucket_table(WINDOW)))
    return np.stack(rows)


def one_hot(ids):
    return (ids[..., None] == np.arange(BUCKETS)).astype(np.float32)


def dot(a, b):
    return jnp.dot(a, b, preferred_element_type=jnp.float32)


def dot_nt(a, b):
    return lax.dot_general(a, b, (((1,), (1,)), ((), ())), preferred_element_type=jnp.float32)


def head_lanes(shape, axis, h):
    place = lax.broadcasted_iota(jnp.int32, shape, axis)
    return (place < HEAD) if h == 0 else (place >= HEAD)


def fold8(x, op):
    return op(x.reshape(x.shape[0] // 8, 8, x.shape[1]), axis=0)


def forward_kernel(
    q_ref, k_ref, v_ref, qf_ref, kf_ref, live_ref, w_ref, ctx_ref, e_ref, inv_ref, vt, bias, s_ref
):
    step = pl.program_id(1)

    @pl.when(step == 0)
    def _():
        for s in range(v_ref.shape[0] // QB):
            vt[:, s * QB : (s + 1) * QB] = v_ref[s * QB : (s + 1) * QB, :].T
        for h in range(2):
            for m in range(3):
                row = jnp.broadcast_to(w_ref[h, m : m + 1, :], (SUB, 2 * SUB))
                bias[h, m] = pltpu.roll(row, 0, 1, stride=1, stride_axis=0)[:, :SUB]

    base = pl.multiple_of(step * QB, QB)
    q = q_ref[...]
    qf = qf_ref[...]
    row_id = lax.broadcasted_iota(jnp.int32, (SUB, SUB), 0)
    col_id = lax.broadcasted_iota(jnp.int32, (SUB, SUB), 1)
    contexts = []
    for h in range(2):
        qx = jnp.concatenate([jnp.where(head_lanes(q.shape, 1, h), q, 0), qf], axis=1)
        neg = w_ref[h, 3:4, :SUB]
        pos = w_ref[h, 4:5, :SUB]
        tops = {(b, kind): None for b in range(2) for kind in "nvp"}
        for c in range(KB // QB):
            place = pl.multiple_of(base + c * QB, QB)
            kx = jnp.concatenate([k_ref[pl.ds(place, QB), :], kf_ref[pl.ds(place, QB), :]], axis=1)
            st = dot_nt(kx, qx)
            for a in range(2 * c, 2 * c + 2):
                for b in range(2):
                    m = a - b - 4
                    if abs(m) > 4:
                        continue
                    x = st[(a - 2 * c) * SUB : (a - 2 * c + 1) * SUB, b * SUB : (b + 1) * SUB]
                    if m == -4:
                        x = jnp.where(row_id >= col_id, x, MASKED_SCORE)
                    if m == 4:
                        x = jnp.where(row_id <= col_id, x, MASKED_SCORE)
                    if abs(m) <= 1:
                        x = x + bias[h, m + 1]
                    s_ref[h, a * SUB : (a + 1) * SUB, b * SUB : (b + 1) * SUB] = x
                    kind = "n" if m < -1 else "p" if m > 1 else "v"
                    top = fold8(x, jnp.max)
                    old = tops[b, kind]
                    tops[b, kind] = top if old is None else jnp.maximum(old, top)
        peaks = []
        for b in range(2):
            peak = jnp.maximum(
                jnp.maximum(tops[b, "n"] + neg, tops[b, "p"] + pos), tops[b, "v"]
            )
            peaks.append(jnp.max(peak, axis=0, keepdims=True))
        totals = [jnp.zeros((8, SUB), jnp.float32)] * 2
        ct = jnp.zeros((HEAD, QB), jnp.float32)
        for c in range(KB // QB):
            for a in range(2 * c, 2 * c + 2):
                for b in range(2):
                    m = a - b - 4
                    rows = slice(a * SUB, (a + 1) * SUB)
                    cols = slice(b * SUB, (b + 1) * SUB)
                    if abs(m) > 4:
                        e_ref[0, 0, h, rows, cols] = jnp.zeros((SUB, SUB), jnp.bfloat16)
                        continue
                    peak = peaks[b]
                    if m < -1:
                        peak = peak - neg
                    if m > 1:
                        peak = peak - pos
                    e = jnp.exp(s_ref[h, rows, cols] - peak)
                    totals[b] = totals[b] + fold8(e, jnp.sum)
                    e_ref[0, 0, h, rows, cols] = e.astype(jnp.bfloat16)
            place = pl.multiple_of(base + c * QB, QB)
            ct = ct + dot(
                vt[h * HEAD : (h + 1) * HEAD, pl.ds(place, QB)],
                e_ref[0, 0, h, c * QB : (c + 1) * QB, :],
            )
        total = jnp.concatenate([jnp.sum(t, axis=0, keepdims=True) for t in totals], axis=1)
        inv = 1.0 / total
        inv_ref[0, 0, h : h + 1, :] = inv
        contexts.append(ct * inv)
    context = jnp.concatenate(contexts, axis=0).T.astype(jnp.bfloat16)
    own = v_ref[pl.ds(pl.multiple_of(base + HALF, QB), QB), :]
    ctx_ref[...] = jnp.where(live_ref[...] > 0, context, own)


def backward_kernel(
    q_ref,
    k_ref,
    v_ref,
    live_ref,
    e_ref,
    inv_ref,
    ctx_ref,
    dctx_ref,
    dq_ref,
    dk_ref,
    dv_ref,
    db_ref,
    kt,
    dk_acc,
    dv_acc,
    acc,
    far,
):
    step = pl.program_id(1)

    @pl.when(step == 0)
    def _():
        for s in range(k_ref.shape[0] // QB):
            kt[:, s * QB : (s + 1) * QB] = k_ref[s * QB : (s + 1) * QB, :].T
        dk_acc[...] = jnp.zeros_like(dk_acc)
        dv_acc[...] = jnp.zeros_like(dv_acc)
        acc[...] = jnp.zeros_like(acc)
        far[...] = jnp.zeros_like(far)

    base = pl.multiple_of(step * QB, QB)
    q = q_ref[...]
    dctx = dctx_ref[...].astype(jnp.float32)
    is_live = live_ref[...] > 0
    kept = jnp.where(is_live, dctx, 0.0)
    prod = (kept * ctx_ref[...].astype(jnp.float32)).T
    kept_t = kept.T
    qs, dts, deltas = [], [], []
    for h in range(2):
        inv = inv_ref[0, 0, h : h + 1, :]
        qs.append(jnp.where(head_lanes(q.shape, 1, h), q, 0))
        dts.append(
            jnp.where(head_lanes(kept_t.shape, 0, h), kept_t * inv, 0.0).astype(jnp.bfloat16)
        )
        deltas.append(
            jnp.sum(prod[h * HEAD : (h + 1) * HEAD], axis=0, keepdims=True) * inv
        )
    q_both = jnp.concatenate(qs, axis=0)
    dt_both = jnp.concatenate(dts, axis=1)
    fars = [[jnp.zeros((8, SUB), jnp.float32)] * 2 for _ in range(2)]
    dqt = [jnp.zeros((HEAD, QB), jnp.float32)] * 2
    for c in range(KB // QB):
        place = pl.multiple_of(base + c * QB, QB)
        vc = v_ref[pl.ds(place, QB), :]
        grads, weights = [], []
        for h in range(2):
            dp = dot(vc, dts[h])
            e = e_ref[0, 0, h, c * QB : (c + 1) * QB, :]
            ds = e.astype(jnp.float32) * (dp - deltas[h])
            for a in range(2 * c, 2 * c + 2):
                for b in range(2):
                    m = a - b - 4
                    x = ds[(a - 2 * c) * SUB : (a - 2 * c + 1) * SUB, b * SUB : (b + 1) * SUB]
                    if abs(m) > 4:
                        continue
                    if abs(m) <= 1:
                        acc[h, m + 1] += x
                    else:
                        side = 0 if m < 0 else 1
                        fars[h][side] = fars[h][side] + fold8(x, jnp.sum)
            ds = ds.astype(jnp.bfloat16)
            dqt[h] = dqt[h] + dot(kt[h * HEAD : (h + 1) * HEAD, pl.ds(place, QB)], ds)
            grads.append(ds)
            weights.append(e)
        dk_acc[pl.ds(place, QB), :] += dot(jnp.concatenate(grads, axis=1), q_both)
        dv_acc[pl.ds(place, QB), :] += dot_nt(jnp.concatenate(weights, axis=1), dt_both)
    dq_ref[...] = jnp.concatenate(dqt, axis=0).T.astype(jnp.bfloat16)
    own = pl.ds(pl.multiple_of(base + HALF, QB), QB)
    dv_acc[own, :] += dctx - kept
    for h in range(2):
        for side in range(2):
            far[h, side] += fars[h][side]

    @pl.when(step == pl.num_programs(1) - 1)
    def _():
        dk_ref[...] = dk_acc[...].astype(jnp.bfloat16)
        dv_ref[...] = dv_acc[...].astype(jnp.bfloat16)
        row_id = lax.broadcasted_iota(jnp.int32, (SUB, SUB), 0)
        col_id = lax.broadcasted_iota(jnp.int32, (SUB, SUB), 1)
        sublane = lax.broadcasted_iota(jnp.int32, (8, SUB), 0)
        for h in range(2):
            sums = []
            for upper in (True, False):
                for m in range(3):
                    x = jnp.where((col_id >= row_id) == upper, acc[h, m], 0.0)
                    y = x[:8]
                    for g in range(1, SUB // 8):
                        y = y + pltpu.roll(x[8 * g : 8 * g + 8], SUB - 8 * g, 1)
                    for bit in range(3):
                        y = jnp.where(
                            (sublane >> bit) % 2 == 1, pltpu.roll(y, SUB - (1 << bit), 1), y
                        )
                    sums.append(jnp.sum(y, axis=0, keepdims=True))
            for side in range(2):
                sums.append(jnp.sum(far[h, side], axis=0, keepdims=True))
            db_ref[h] = jnp.concatenate(sums, axis=0)


def spec(shape, index):
    return pl.BlockSpec(shape, index)


def attention_forward(queries, key_value, q_feat, k_feat, live, bias_rows):
    rows, span = queries.shape[0], key_value.shape[0]
    steps = rows // QB
    return pl.pallas_call(
        forward_kernel,
        grid=(PAIRS, steps),
        in_specs=[
            spec((QB, SUB), lambda p, i: (i, p)),
            spec((span, SUB), lambda p, i: (0, p)),
            spec((span, SUB), lambda p, i: (0, p + PAIRS)),
            spec((QB, SUB), lambda p, i: (i, 0)),
            spec((span, SUB), lambda p, i: (0, 0)),
            spec((QB, SUB), lambda p, i: (i, 0)),
            spec((2, 8, 2 * SUB), lambda p, i: (p, 0, 0)),
        ],
        out_specs=[
            spec((QB, SUB), lambda p, i: (i, p)),
            spec((1, 1, 2, KB, QB), lambda p, i: (p, i, 0, 0, 0)),
            spec((1, 1, 8, QB), lambda p, i: (p, i, 0, 0)),
        ],
        out_shape=[
            jax.ShapeDtypeStruct((rows, D), jnp.bfloat16),
            jax.ShapeDtypeStruct((PAIRS, steps, 2, KB, QB), jnp.bfloat16),
            jax.ShapeDtypeStruct((PAIRS, steps, 8, QB), jnp.float32),
        ],
        scratch_shapes=[
            pltpu.VMEM((SUB, span), jnp.bfloat16),
            pltpu.VMEM((2, 3, SUB, SUB), jnp.float32),
            pltpu.VMEM((2, KB, QB), jnp.float32),
        ],
        compiler_params=pltpu.CompilerParams(
            dimension_semantics=("arbitrary", "arbitrary"), vmem_limit_bytes=VMEM_LIMIT
        ),
        cost_estimate=pl.CostEstimate(
            flops=4 * rows * KB * D * 4, bytes_accessed=45_000_000, transcendentals=rows * KB * HEADS
        ),
    )(queries, key_value, key_value, q_feat, k_feat, live, bias_rows)


def attention_backward(
    queries, key_value, live, expo, inverse, context, d_context, first, pairs
):
    rows, span = queries.shape[0], key_value.shape[0]
    steps = rows // QB
    return pl.pallas_call(
        backward_kernel,
        grid=(pairs, steps),
        in_specs=[
            spec((QB, SUB), lambda p, i: (i, p + first)),
            spec((span, SUB), lambda p, i: (0, p + first)),
            spec((span, SUB), lambda p, i: (0, p + first + PAIRS)),
            spec((QB, SUB), lambda p, i: (i, 0)),
            spec((1, 1, 2, KB, QB), lambda p, i: (p + first, i, 0, 0, 0)),
            spec((1, 1, 8, QB), lambda p, i: (p + first, i, 0, 0)),
            spec((QB, SUB), lambda p, i: (i, p + first)),
            spec((QB, SUB), lambda p, i: (i, p + first)),
        ],
        out_specs=[
            spec((QB, SUB), lambda p, i: (i, p)),
            spec((span, SUB), lambda p, i: (0, p)),
            spec((span, SUB), lambda p, i: (0, p)),
            spec((2, 8, SUB), lambda p, i: (p, 0, 0)),
        ],
        out_shape=[
            jax.ShapeDtypeStruct((rows, pairs * SUB), jnp.bfloat16),
            jax.ShapeDtypeStruct((span, pairs * SUB), jnp.bfloat16),
            jax.ShapeDtypeStruct((span, pairs * SUB), jnp.bfloat16),
            jax.ShapeDtypeStruct((2 * pairs, 8, SUB), jnp.float32),
        ],
        scratch_shapes=[
            pltpu.VMEM((SUB, span), jnp.bfloat16),
            pltpu.VMEM((span, SUB), jnp.float32),
            pltpu.VMEM((span, SUB), jnp.float32),
            pltpu.VMEM((2, 3, SUB, SUB), jnp.float32),
            pltpu.VMEM((2, 2, 8, SUB), jnp.float32),
        ],
        compiler_params=pltpu.CompilerParams(
            dimension_semantics=("arbitrary", "arbitrary"), vmem_limit_bytes=VMEM_LIMIT
        ),
        cost_estimate=pl.CostEstimate(
            flops=8 * rows * KB * pairs * SUB * 4, bytes_accessed=9_000_000 * pairs, transcendentals=0
        ),
    )(queries, key_value, key_value, live, expo, inverse, context, d_context)


FF = 3072
TILE = 256


def gelu_parts(v):
    scale = 0.7978845608
    square = v * v
    t = jnp.tanh(scale * v * (1.0 + 0.044715 * square))
    half = 0.5 * (1.0 + t)
    slope = half + 0.5 * v * (1.0 - t * t) * (scale + (3 * 0.044715 * scale) * square)
    return half * v, slope


def routing(x, router, pick, experts):
    logits = dot(x, router)
    lane = lax.broadcasted_iota(jnp.int32, logits.shape, 1)
    logits = jnp.where(lane < experts, logits, MASKED_SCORE)
    expo = jnp.exp(logits - jnp.max(logits, axis=1, keepdims=True))
    probs = expo / jnp.sum(expo, axis=1, keepdims=True)
    return probs, jnp.sum(probs * pick, axis=1, keepdims=True)


def hidden_pair(x, d_rows, w_in, w_out):
    inner, slope = gelu_parts(dot(x, w_in))
    d_pre = dot_nt(d_rows, w_out) * slope
    return inner.astype(jnp.bfloat16), d_pre.astype(jnp.bfloat16)


def row_chunks(rows):
    return [slice(s, s + QB) for s in range(0, rows, QB)]


def expert_kernel(
    experts,
    x_ref,
    c_ref,
    router_ref,
    pick_ref,
    aux_ref,
    win_ref,
    wout_ref,
    rows_ref,
    back_ref,
    act_ref,
    dpre_ref,
    drows_ref,
    dlog_ref,
    probs,
    rows_acc,
    back_acc,
):
    step = pl.program_id(0)
    pick = pick_ref[0:1, :]

    @pl.when(step == 0)
    def _():
        for r in row_chunks(x_ref.shape[0]):
            p, gate = routing(x_ref[r, :], router_ref[...], pick, experts)
            probs[r, :] = p
            drows_ref[r, :] = (gate * c_ref[r, :].astype(jnp.float32)).astype(jnp.bfloat16)
        rows_acc[...] = jnp.zeros_like(rows_acc)
        back_acc[...] = jnp.zeros_like(back_acc)

    w_in, w_out = win_ref[...], wout_ref[...]
    for r in row_chunks(x_ref.shape[0]):
        act, dpre = hidden_pair(x_ref[r, :], drows_ref[r, :], w_in, w_out)
        act_ref[r, :] = act
        dpre_ref[r, :] = dpre
        rows_acc[r, :] += dot(act, w_out)
        back_acc[r, :] += dot_nt(dpre, w_in)

    @pl.when(step == pl.num_programs(0) - 1)
    def _():
        for r in row_chunks(x_ref.shape[0]):
            rows = rows_acc[r, :].astype(jnp.bfloat16)
            rows_ref[r, :] = rows
            d_gate = jnp.sum(
                c_ref[r, :].astype(jnp.float32) * rows.astype(jnp.float32), axis=1, keepdims=True
            )
            p = probs[r, :]
            d_probs = pick * d_gate + aux_ref[0:1, :]
            d_log = p * (d_probs - jnp.sum(d_probs * p, axis=1, keepdims=True))
            d_log = d_log.astype(jnp.bfloat16)
            dlog_ref[r, :] = d_log
            back = back_acc[r, :].astype(jnp.bfloat16).astype(jnp.float32)
            back_ref[r, :] = (back + dot_nt(d_log, router_ref[...])).astype(jnp.bfloat16)


def whole(shape):
    return pl.BlockSpec(shape, lambda t: (0,) * len(shape))


def expert_pass(x, cot, router, pick, aux, w_in, w_out, experts):
    rows = x.shape[0]
    wide = jax.ShapeDtypeStruct((rows, FF), jnp.bfloat16)
    narrow = jax.ShapeDtypeStruct((rows, D), jnp.bfloat16)
    return pl.pallas_call(
        functools.partial(expert_kernel, experts),
        grid=(FF // TILE,),
        in_specs=[
            whole((rows, D)),
            whole((rows, D)),
            whole((D, SUB)),
            whole((8, SUB)),
            whole((8, SUB)),
            pl.BlockSpec((D, TILE), lambda t: (0, t)),
            pl.BlockSpec((TILE, D), lambda t: (t, 0)),
        ],
        out_specs=[
            whole((rows, D)),
            whole((rows, D)),
            pl.BlockSpec((rows, TILE), lambda t: (0, t)),
            pl.BlockSpec((rows, TILE), lambda t: (0, t)),
            whole((rows, D)),
            whole((rows, SUB)),
        ],
        out_shape=[narrow, narrow, wide, wide, narrow, jax.ShapeDtypeStruct((rows, SUB), jnp.bfloat16)],
        scratch_shapes=[
            pltpu.VMEM((rows, SUB), jnp.float32),
            pltpu.VMEM((rows, D), jnp.float32),
            pltpu.VMEM((rows, D), jnp.float32),
        ],
        compiler_params=pltpu.CompilerParams(
            dimension_semantics=("arbitrary",), vmem_limit_bytes=VMEM_LIMIT
        ),
        cost_estimate=pl.CostEstimate(
            flops=8 * rows * D * FF, bytes_accessed=30_000_000, transcendentals=rows * FF
        ),
    )(x, cot, router, pick, aux, w_in, w_out)


def transposed(target, source, place):
    for r in row_chunks(source.shape[0]):
        at = pl.multiple_of(place + r.start, QB)
        target[:, pl.ds(at, QB)] = source[r, :].T


def weight_kernel(experts, paired, *refs):
    if paired:
        (x_ref, drows_ref, act_ref, dpre_ref, rep_ref, x2_ref, c2_ref, router_ref, pick_ref, win_ref,
         wout_ref, din_ref, dout_ref, xt, dt, drows2, acts, dpres) = refs
        own = rep_ref[0] * x_ref.shape[0]
        other = x_ref.shape[0] - own
    else:
        x_ref, drows_ref, act_ref, dpre_ref, din_ref, dout_ref, xt, dt = refs
        own = 0

    @pl.when(pl.program_id(0) == 0)
    def _():
        transposed(xt, x_ref, own)
        transposed(dt, drows_ref, own)
        if paired:
            for r in row_chunks(x2_ref.shape[0]):
                _, gate = routing(x2_ref[r, :], router_ref[...], pick_ref[0:1, :], experts)
                drows2[r, :] = (gate * c2_ref[r, :].astype(jnp.float32)).astype(jnp.bfloat16)
            transposed(xt, x2_ref, other)
            transposed(dt, drows2, other)

    if paired:
        w_in, w_out = win_ref[...], wout_ref[...]
        for r in row_chunks(x2_ref.shape[0]):
            act, dpre = hidden_pair(x2_ref[r, :], drows2[r, :], w_in, w_out)
            at = pl.ds(pl.multiple_of(other + r.start, QB), QB)
            acts[at, :] = act
            dpres[at, :] = dpre
            at = pl.ds(pl.multiple_of(own + r.start, QB), QB)
            acts[at, :] = act_ref[r, :]
            dpres[at, :] = dpre_ref[r, :]
        act, dpre = acts[...], dpres[...]
    else:
        act, dpre = act_ref[...], dpre_ref[...]
    din_ref[...] = dot(xt[...], dpre)
    dout_ref[...] = dot(dt[...], act).T


def weight_pass(own, other, experts):
    x, drows, act, dpre = own
    rows = x.shape[0]
    paired = other is not None
    total = 2 * rows if paired else rows
    narrow, wide = whole((rows, D)), pl.BlockSpec((rows, TILE), lambda t: (0, t))
    in_specs = [narrow, narrow, wide, wide]
    scratch = [pltpu.VMEM((D, total), jnp.bfloat16)] * 2
    args = (x, drows, act, dpre)
    if paired:
        in_specs += [
            pl.BlockSpec(memory_space=pltpu.SMEM),
            narrow,
            narrow,
            whole((D, SUB)),
            whole((8, SUB)),
            pl.BlockSpec((D, TILE), lambda t: (0, t)),
            pl.BlockSpec((TILE, D), lambda t: (t, 0)),
        ]
        scratch += [
            pltpu.VMEM((rows, D), jnp.bfloat16),
            pltpu.VMEM((total, TILE), jnp.bfloat16),
            pltpu.VMEM((total, TILE), jnp.bfloat16),
        ]
        args += tuple(other)
    return pl.pallas_call(
        functools.partial(weight_kernel, experts, paired),
        grid=(FF // TILE,),
        in_specs=in_specs,
        out_specs=[
            pl.BlockSpec((D, TILE), lambda t: (0, t)),
            pl.BlockSpec((TILE, D), lambda t: (t, 0)),
        ],
        out_shape=[
            jax.ShapeDtypeStruct((D, FF), jnp.float32),
            jax.ShapeDtypeStruct((FF, D), jnp.float32),
        ],
        scratch_shapes=scratch,
        compiler_params=pltpu.CompilerParams(
            dimension_semantics=("arbitrary",), vmem_limit_bytes=VMEM_LIMIT
        ),
        cost_estimate=pl.CostEstimate(
            flops=(12 if paired else 4) * rows * D * FF,
            bytes_accessed=45_000_000,
            transcendentals=rows * FF if paired else 0,
        ),
    )(*args)


EPSILON = 1e-06
AUX_WEIGHT = 0.01
PRECISE = lax.Precision.HIGHEST
GROUP = ("shard", "seq")
EVERY = ("rep", "shard", "seq")


def exchange(x, axis, hop):
    count = lax.axis_size(axis)
    return lax.ppermute(x, axis, [(i, i ^ hop) for i in range(count)])


def bits_of(axis):
    return lax.axis_size(axis).bit_length() - 1


def bit_at(axis, bit):
    return (lax.axis_index(axis) >> bit) & 1


def both_halves(x, axis, bit, dim):
    other = exchange(x, axis, 1 << bit)
    size = x.shape[dim]
    rec = jnp.concatenate([other, x, other], axis=dim)
    return lax.dynamic_slice_in_dim(rec, (1 - bit_at(axis, bit)) * size, 2 * size, axis=dim)


def all_blocks(x, axis, dim):
    count = lax.axis_size(axis)
    size = x.shape[dim]
    turned = [
        lax.ppermute(x, axis, [(i, (i + k) % count) for i in range(count)])
        for k in range(count - 1, 0, -1)
    ]
    rec = jnp.concatenate(turned + [x] + turned, axis=dim)
    start = (count - 1 - lax.axis_index(axis)) * size
    return lax.dynamic_slice_in_dim(rec, start, count * size, axis=dim)


def gather_rows(x, parts):
    seq_bits = bits_of("seq")
    outs = []
    for turn, (start, stop) in enumerate(parts):
        y = x[:, start:stop].reshape((1,) * (1 + seq_bits) + (x.shape[0], stop - start))
        order = ["shard"] + list(range(seq_bits - 1, 0, -1))
        if turn % 2 == 1:
            order = order[::-1]
        for what in order + [0]:
            if what == "shard":
                y = all_blocks(y, "shard", 0)
            else:
                y = both_halves(y, "seq", what, seq_bits - what)
        outs.append(y.reshape(-1, stop - start))
    return outs


def half_kept(x, axis, bit, dim):
    size = x.shape[dim] // 2
    mine = bit_at(axis, bit)
    kept = lax.dynamic_slice_in_dim(x, mine * size, size, axis=dim)
    sent = lax.dynamic_slice_in_dim(x, (1 - mine) * size, size, axis=dim)
    got = exchange(sent, axis, 1 << bit)
    return (kept.astype(jnp.float32) + got.astype(jnp.float32)).astype(jnp.bfloat16)


def scatter_sums(x, parts):
    seq_bits, shard_bits = bits_of("seq"), bits_of("shard")
    rows = x.shape[0] >> (seq_bits + shard_bits)
    outs = []
    for turn, (start, stop) in enumerate(parts):
        y = x[:, start:stop].reshape((2,) * (shard_bits + seq_bits) + (rows, stop - start))
        far = [("shard", b) for b in range(shard_bits - 1, -1, -1)]
        near = [("seq", b) for b in range(seq_bits - 1, 0, -1)]
        order = near + far if turn % 2 == 0 else far + near
        for axis, bit in [("seq", 0)] + order:
            dim = shard_bits - 1 - bit if axis == "shard" else shard_bits + seq_bits - 1 - bit
            y = half_kept(y, axis, bit, dim)
        y = y.reshape(rows, stop - start)
        for bit in range(bits_of("rep")):
            total = y.astype(jnp.float32) + exchange(y, "rep", 1 << bit).astype(jnp.float32)
            y = total.astype(jnp.bfloat16)
        outs.append(total)
    return outs


def sum_everywhere(x):
    for axis in ("seq", "shard", "rep"):
        for bit in range(bits_of(axis)):
            x = x + exchange(x, axis, 1 << bit)
    return x


def rms_norm(vectors, gains):
    return (
        vectors * lax.rsqrt(jnp.mean(vectors * vectors, axis=-1, keepdims=True) + EPSILON) * gains
    )


def dot_tn(a, b):
    return lax.dot_general(a, b, (((0,), (0,)), ((), ())), preferred_element_type=jnp.float32)


def doc_index(places, doc_ends):
    return jnp.sum((places[:, None] >= doc_ends[None, :]).astype(jnp.int32), axis=1)


def wide_row(values):
    row = jnp.pad(values.astype(jnp.float32), (0, SUB - values.shape[0]))
    return jnp.broadcast_to(row[None, :], (8, SUB))


def routed_across(x):
    return lax.all_to_all(x, GROUP, split_axis=0, concat_axis=0, tiled=True)


def shards(
    tokens,
    doc_lengths,
    expert_ids,
    cotangent,
    gain_attn,
    gain_ffn,
    w_query,
    w_key,
    w_value,
    w_attn_out,
    rel_table,
    w_router,
    w_expert_in,
    w_expert_out,
):
    rows = tokens.shape[0]
    seq_count = lax.axis_size("seq")
    rep_count = lax.axis_size("rep")
    experts = lax.axis_size(GROUP)
    all_devices = lax.axis_size(EVERY)
    capacity = 5 * rows // (4 * experts)
    slots = experts * capacity
    shard_rows = w_query.shape[0]
    table_rows = rel_table.shape[0]
    w_in, w_out = w_expert_in[0], w_expert_out[0]

    up = [(i, i + 1) for i in range(seq_count - 1)]
    down = [(i + 1, i) for i in range(seq_count - 1)]
    token_span = jnp.concatenate(
        [lax.ppermute(tokens[rows - HALF :], "seq", up), tokens, lax.ppermute(tokens[:HALF], "seq", down)],
        axis=0,
    )
    small = jnp.concatenate(
        [
            w_router,
            gain_attn[:, None],
            gain_ffn[:, None],
            jnp.pad(rel_table, ((0, shard_rows - table_rows), (0, 0))),
        ],
        axis=1,
    )
    small = jnp.pad(small, ((0, 0), (0, SUB - small.shape[1])))
    first = jnp.concatenate([small, w_query, w_key, w_value], axis=1)
    cut = 10 * SUB
    left, right = gather_rows(first, [(0, cut), (cut, first.shape[1])])
    extra = left[:, :SUB]
    w_qkv = jnp.concatenate([left[:, SUB:], right], axis=1)
    router = extra[:, :experts]
    router_wide = jnp.pad(router, ((0, 0), (0, SUB - experts)))
    g_attn = extra[:, experts].astype(jnp.float32)
    g_ffn = extra[:, experts + 1].astype(jnp.float32)
    table = extra.reshape(experts, shard_rows, SUB)[:, :table_rows, experts + 2 : experts + 2 + HEADS]
    table = table.reshape(BUCKETS, HEADS).astype(jnp.float32)
    w_proj = jnp.concatenate(gather_rows(w_attn_out, [(0, 3 * SUB), (3 * SUB, D)]), axis=1)

    first_place = lax.axis_index("seq") * rows
    doc_ends = jnp.cumsum(doc_lengths[0])
    total_live = doc_ends[DOCS - 1]
    q_places = first_place + jnp.arange(rows, dtype=jnp.int32)
    k_places = first_place - HALF + jnp.arange(rows + 2 * HALF, dtype=jnp.int32)
    q_docs = doc_index(q_places, doc_ends)
    k_docs = doc_index(k_places, doc_ends)
    q_live = q_places < total_live
    k_live = (k_places >= 0) & (k_places < total_live)
    docs = jnp.arange(SUB, dtype=jnp.int32)[None, :]
    q_feat = ((q_docs[:, None] == docs) & (docs < DOCS)).astype(jnp.bfloat16)
    barred = (docs < DOCS) & ~((k_docs[:, None] == docs) & k_live[:, None])
    k_feat = jnp.where(barred, MASKED_SCORE, 0.0).astype(jnp.bfloat16)
    live = jnp.broadcast_to(q_live[:, None], (rows, SUB)).astype(jnp.bfloat16)
    chosen_ids = expert_ids[:, 0]
    chosen = (chosen_ids[:, None] == jnp.arange(experts, dtype=jnp.int32)[None, :]).astype(
        jnp.int32
    ) * q_live.astype(jnp.int32)[:, None]
    chosen_f = chosen.astype(jnp.float32)
    ranked = jnp.cumsum(chosen, axis=0)
    slot_index = jnp.sum(ranked * chosen, axis=1) - 1
    target = jnp.where(q_live, chosen_ids * capacity + slot_index, slots)
    hot = (target[None, :] == jnp.arange(slots, dtype=jnp.int32)[:, None]).astype(jnp.bfloat16)
    counts_all = sum_everywhere(jnp.sum(chosen_f, axis=0))
    live_all = jnp.sum(counts_all)
    shares = counts_all / live_all
    me = lax.axis_index(GROUP)
    pick = wide_row(jnp.arange(experts) == me)
    aux = wide_row((AUX_WEIGHT * experts / live_all) * shares)

    def to_experts(values):
        sent = dot(hot, values).astype(jnp.bfloat16)
        return routed_across(sent.reshape(experts, capacity, D)).reshape(slots, D)

    def from_experts(values):
        return dot_tn(hot, routed_across(values.reshape(experts, capacity, D)).reshape(slots, D))

    cot_rows = to_experts(cotangent)

    inputs = tokens.astype(jnp.float32)
    normed_span, span_pull = jax.vjp(rms_norm, token_span.astype(jnp.float32), g_attn)
    normed_span = normed_span.astype(jnp.bfloat16)
    normed_one = normed_span[HALF : HALF + rows]
    queries = dot(normed_one, w_qkv[:, :D]).astype(jnp.bfloat16)
    key_value = dot(normed_span, w_qkv[:, D:]).astype(jnp.bfloat16)
    bias_rows = jnp.einsum("rxb,bh->hrx", one_hot(bias_buckets()), table, precision=PRECISE)
    context, expo, inverse = attention_forward(queries, key_value, q_feat, k_feat, live, bias_rows)
    hidden_state = inputs + dot(context, w_proj)

    ffn_normed, ffn_pull = jax.vjp(rms_norm, hidden_state, g_ffn)
    normed_two = ffn_normed.astype(jnp.bfloat16)
    x_rows = to_experts(normed_two)
    out_rows, back_rows, act, d_pre, d_rows, d_logits = expert_pass(
        x_rows, cot_rows, router_wide, pick, aux, w_in, w_out, experts
    )
    d_normed_two = from_experts(back_rows)
    expert_rows = from_experts(out_rows)
    d_router = dot_tn(x_rows, d_logits)[:, :experts]
    own = (x_rows, d_rows, act, d_pre)
    if rep_count == 2:
        order = lax.axis_index("rep").reshape(1)
        x_other, cot_other = exchange(x_rows, "rep", 1), exchange(cot_rows, "rep", 1)
        other = (order, x_other, cot_other, router_wide, pick, w_in, w_out)
        d_expert_in, d_expert_out = weight_pass(own, other, experts)
    else:
        d_expert_in, d_expert_out = (
            lax.psum(g.astype(jnp.bfloat16), "rep").astype(jnp.float32)
            for g in weight_pass(own, None, experts)
        )

    router_probs = jax.nn.softmax(dot(normed_two, router), axis=-1)
    gating = jnp.sum(router_probs * chosen_f, axis=1)
    mass_all = sum_everywhere(jnp.sum(router_probs * q_live.astype(jnp.float32)[:, None], axis=0))
    balance = experts * jnp.sum(shares * mass_all) / live_all
    importance = experts * mass_all / (rows * all_devices)
    mixed = (hidden_state + gating[:, None] * expert_rows).astype(jnp.bfloat16)

    hidden_back, d_gain_ffn = ffn_pull(d_normed_two)
    d_hidden = cotangent.astype(jnp.float32) + hidden_back
    d_attn = d_hidden.astype(jnp.bfloat16)
    d_context = dot_nt(d_attn, w_proj).astype(jnp.bfloat16)
    d_attn_out = dot_tn(context, d_attn)
    more = jnp.concatenate([d_router, d_gain_ffn[:, None]], axis=1)
    more = jnp.pad(more, ((0, 0), (0, SUB - more.shape[1])))
    early = jnp.concatenate([d_attn_out, more], axis=1).astype(jnp.bfloat16)
    early_cut = 4 * SUB
    early = jnp.concatenate(scatter_sums(early, [(0, early_cut), (early_cut, D + SUB)]), axis=1)

    pieces, sums, d_bias = [], [], []
    for pairs in (range(0, 3), range(3, 6)):
        d_q, d_k, d_v, d_b = attention_backward(
            queries, key_value, live, expo, inverse, context, d_context, pairs[0], len(pairs)
        )
        pieces.append((d_q, d_k, d_v))
        d_bias.append(d_b)
        grads = jnp.concatenate(
            [
                dot_tn(normed_one, d_q).astype(jnp.bfloat16),
                dot_tn(normed_span, d_k).astype(jnp.bfloat16),
                dot_tn(normed_span, d_v).astype(jnp.bfloat16),
            ],
            axis=1,
        )
        width = grads.shape[1]
        half = width // (2 * SUB) * SUB
        summed = jnp.concatenate(scatter_sums(grads, [(0, half), (half, width)]), axis=1)
        sums.append(jnp.split(summed, 3, axis=1))
    d_query, d_key, d_value = (jnp.concatenate(s, axis=1) for s in zip(*sums))
    d_q, d_k, d_v = (jnp.concatenate(s, axis=1) for s in zip(*pieces))
    d_span = dot_nt(jnp.concatenate([d_k, d_v], axis=1), w_qkv[:, D:])
    d_span = jnp.concatenate(
        [d_span[:HALF], d_span[HALF : HALF + rows] + dot_nt(d_q, w_qkv[:, :D]), d_span[HALF + rows :]],
        axis=0,
    )
    from_above = lax.ppermute(d_span[:HALF].astype(jnp.bfloat16), "seq", down)
    from_below = lax.ppermute(d_span[HALF + rows :].astype(jnp.bfloat16), "seq", up)
    gap = jnp.zeros((rows - HALF, D), jnp.float32)
    d_normed_one = (
        d_span[HALF : HALF + rows]
        + jnp.concatenate([from_below.astype(jnp.float32), gap], axis=0)
        + jnp.concatenate([gap, from_above.astype(jnp.float32)], axis=0)
    )
    _, attn_pull = jax.vjp(lambda v: rms_norm(v, g_attn), inputs)
    d_tokens = d_hidden + attn_pull(d_normed_one)[0]
    d_gain_attn = span_pull(d_span)[1]
    d_table = jnp.einsum(
        "hrx,rxb->bh", jnp.concatenate(d_bias, axis=0), one_hot(grad_buckets()), precision=PRECISE
    )
    d_table = jnp.pad(
        d_table.reshape(experts, table_rows, HEADS), ((0, 0), (0, shard_rows - table_rows), (0, 0))
    ).reshape(D, HEADS)
    late = jnp.concatenate([d_gain_attn[:, None], d_table], axis=1).astype(jnp.bfloat16)
    late = jnp.pad(late, ((0, 0), (0, SUB - late.shape[1])))
    late = scatter_sums(late, [(0, SUB)])[0]
    return (
        mixed,
        balance,
        importance,
        d_tokens,
        late[:, 0],
        early[:, D + experts],
        d_query,
        d_key,
        d_value,
        early[:, :D],
        late[:table_rows, 1 : 1 + HEADS],
        early[:, D : D + experts],
        d_expert_in[None],
        d_expert_out[None],
    )


def solution(mesh):
    split = P(EVERY, None)
    shared = P(GROUP, None)
    gains = P(GROUP)
    stacked = P(GROUP, None, None)
    weights = (shared,) * 6 + (stacked,) * 2
    return jax.shard_map(
        shards,
        mesh=mesh,
        in_specs=(split, P(("rep", "shard"), None), split, split, gains, gains) + weights,
        out_specs=(split, P(), P(), split, gains, gains) + weights,
        check_vma=False,
    )
```

time: 2040 us -> 689 us (0.34)
  local copies, waits for them, and re-layouts: 596 us -> 51.2 us
  blocking collectives: 352 us -> 0 us
  matrix products: 382 us -> 65.1 us
  Pallas kernels: 0 us -> 223 us
  waiting for transfers between devices: 400 us -> 180 us
  other arithmetic: 253 us -> 50.8 us
  starting transfers between devices: 19.4 us -> 105 us
    dot_general x31 -> x21, matrix products: 382 us -> 65.1 us  [the longest x10 26.9 us: dot_tn(): lax.dot_general(a, b, (((0,), (0,)), ((), ())), preferred_element_type=jn...]
    reshape x5 -> x1, local copies, waits for them, and re-layouts: 299 us -> 1.41 us  [gather_rows(): x[:, start:stop].reshape((1,) * (1 + seq_bits) + (x.shape[0], stop - start))]
    pallas_call x0 -> x5, Pallas kernels: none -> 223 us  [the longest x2 79.5 us: attention_backward(): pl.pallas_call(backward_kernel, grid=(pairs, steps), in_specs=[spec((QB,...]
    reduce_scatter x4 -> x0, waiting for transfers between devices: 195 us -> none  [the longest x1 60.7 us: shards(): lax.psum_scatter(d_w_qkv[:, :D].astype(jnp.bfloat16), ('shard', 'seq'), s...]
    ppermute x4 -> x71, waiting for transfers between devices: 0.01 us -> 180 us  [the longest x55 131 us: exchange(): return lax.ppermute(x, axis, [(i, i ^ hop) for i in range(count)])]
    psum x1 -> x0, waiting for transfers between devices: 151 us -> none  [shards(): lax.psum(reduced[0].astype(jnp.bfloat16), 'rep').astype(jnp.float32)]
    psum x3 -> x0, blocking collectives: 112 us -> none  [the longest x2 106 us: shards(): lax.psum((jnp.sum(chosen_f, axis=0), jnp.sum(router_probs * is_live[:, No...]
    all_to_all x2 -> x0, blocking collectives: 109 us -> none  [the longest x1 59.7 us: shards(): lax.all_to_all(outgoing, ('shard', 'seq'), split_axis=0, concat_axis=0, t...]
  transfers between devices with their start and end apart: 16 -> 75, of which waited for: 7 -> 28; matrix products, arithmetic and copies ran while one was open for 24% -> 22% of each run, Pallas kernels for 0% -> 33%
where the time goes in v1:
time: 689 us; the launch traced here: 682 us
  Pallas kernels  223 us (32%)
  waiting for transfers between devices  180 us (26%)
  starting transfers between devices  105 us (15%)
  matrix products  65.1 us (9%)
  local copies, waits for them, and re-layouts  51.2 us (7%)
  other arithmetic  50.8 us (7%)
    ppermute x55, waiting for transfers between devices, exchange(): return lax.ppermute(x, axis, [(i, i ^ hop) for i in range(count)])  131 us
    pallas_call x2, Pallas kernels, attention_backward(): pl.pallas_call(backward_kernel, grid=(pairs, steps), in_specs=[spec((QB,...  79.5 us
    ppermute x55, starting transfers between devices, exchange(): return lax.ppermute(x, axis, [(i, i ^ hop) for i in range(count)])  56.5 us
    pallas_call x1, Pallas kernels, weight_pass(): pl.pallas_call(functools.partial(weight_kernel, experts, paired), grid=(F...  53 us
    ppermute x12, waiting for transfers between devices, all_blocks(): lax.ppermute(x, axis, [(i, (i + k) % count) for i in range(count)])  49.3 us
    pallas_call x1, Pallas kernels, attention_forward(): pl.pallas_call(forward_kernel, grid=(PAIRS, steps), in_specs=[spec((QB, S...  46 us
    pallas_call x1, Pallas kernels, expert_pass(): pl.pallas_call(functools.partial(expert_kernel, experts), grid=(FF // TIL...  44.8 us
    dot_general x10, matrix products, dot_tn(): lax.dot_general(a, b, (((0,), (0,)), ((), ())), preferred_element_type=jn...  26.9 us
  transfers between devices with their start and end apart: 75, of which 28 were waited for; matrix products, arithmetic and copies ran while one was open for 22% of the time, Pallas kernels for 33%

profile of v1, /device:TPU:0, one launch (start us, length us, event | category | flops | bytes accessed | tf_op | source)
XLA Modules:
  0.0 682.0 jit_solution(13150163155733987411)
XLA Ops:
  3.2 5.1 collective-permute-start.2
  10.7 2.8 collective-permute-start.12
  18.1 4.5 reduce-window.11
  25.0 5.1 fusion.18
  30.1 4.6 all-to-all-start.1
  47.7 24.5 %collective-permute-done.14 = bf16[1,1,1,48,384]{4,3,2,1,0:T(8,128)(2,1)S(1)} collective-permute-done((bf16[1,1,1,48,384]{4,3,2,1,0:T(8,128)(2,1)}, bf16[1,1,1,48,384]{4,3,2,1,0:T(8,128)(2,1)S(1)}, u32[]{:S(2)}, u32[]{:S(2)}) %collective-permute-start.14) | collective-permute-done | bytes 36896 | tf_op jit(solution)/shard_map/ppermute | solution.py:638
  78.7 3.2 collective-permute-done.7
  82.6 8.8 %collective-permute-done.18 = bf16[1,2,1,48,384]{4,3,2,1,0:T(8,128)(2,1)S(1)} collective-permute-done((bf16[1,2,1,48,384]{4,3,2,1,0:T(8,128)(2,1)S(1)}, bf16[1,2,1,48,384]{4,3,2,1,0:T(8,128)(2,1)S(1)}, u32[]{:S(2)}, u32[]{:S(2)}) %collective-permute-start.18) | collective-permute-done | bytes 73760 | tf_op jit(solution)/shard_map/ppermute | solution.py:638
  91.4 4.4 collective-permute-start.19
  99.9 4.4 collective-permute-done.20
  115.0 6.0 collective-permute-start.21
  121.0 9.2 %collective-permute-done.9 = bf16[1,2,1,48,1152]{4,3,2,1,0:T(8,128)(2,1)S(1)} collective-permute-done((bf16[1,2,1,48,1152]{4,3,2,1,0:T(8,128)(2,1)S(1)}, bf16[1,2,1,48,1152]{4,3,2,1,0:T(8,128)(2,1)S(1)}, u32[]{:S(2)}, u32[]{:S(2)}) %collective-permute-start.9) | collective-permute-done | bytes 221216 | tf_op jit(solution)/shard_map/ppermute | solution.py:638
  131.0 11.6 %collective-permute-done.5 = bf16[4,1,1,48,1280]{4,3,2,1,0:T(8,128)(2,1)S(1)} collective-permute-done((bf16[4,1,1,48,1280]{4,3,2,1,0:T(8,128)(2,1)S(1)}, bf16[4,1,1,48,1280]{4,3,2,1,0:T(8,128)(2,1)S(1)}, u32[]{:S(2)}, u32[]{:S(2)}) %collective-permute-start.5) | collective-permute-done | bytes 491552 | tf_op jit(solution)/shard_map/ppermute | solution.py:616
  149.0 2.6 convolution_convert_fusion.2.q_ref
  153.4 7.4 %convolution_convert_fusion.k_ref.v_ref = bf16[2048,1536]{1,0:T(8,128)(2,1)} fusion(bf16[2048,768]{0,1:T(8,128)(2,1)S(1)} %fusion.2, bf16[768,1152]{1,0:T(8,128)(2,1)S(1)} %bitcast.121, bf16[768,1152]{1,0:T(8,128)(2,1)S(1)} %slice.153), kind=kOutput, calls=%fused_computation.2 | convolution fusion | flops 4839702528 | bytes 12976128 | tf_op jit(solution)/shard_map/dot_general | solution.py:85
  161.7 46.0 %shard_map.263 = (bf16[1024,768]{1,0:T(8,128)(2,1)}, bf16[6,4,2,1280,256]{4,3,2,1,0:T(8,128)(2,1)}, f32[6,4,8,256]{3,2,1,0:T(8,128)}) custom-call(bf16[1024,768]{1,0:T(8,128)(2,1)} %convolution_convert_fusion.2.q_ref, bf16[2048,1536]{1,0:T(8,128)(2,1)} %convolution_convert_fusion.k_ref.v_ref, bf16[2048,1536]{1,0:T(8,128)(2,1)} %convolution_convert_fusion.k_ref.v_ref, ...), custom_call_target="tpu_custom_call" | custom-call | flops 16106127360 | bytes 45000000 | tf_op jit(solution)/shard_map/pallas_call | solution.py:301
  207.8 3.0 multiply_reduce_fusion.2
  212.4 3.9 fusion.17
  216.3 4.7 all-to-all-start
  225.9 7.0 %collective-permute-done.23 = f32[16]{0:T(128)S(1)} collective-permute-done((f32[16]{0:T(128)S(1)}, f32[16]{0:T(128)S(1)}, u32[]{:S(2)}, u32[]{:S(2)}) %collective-permute-start.23) | collective-permute-done | bytes 96 | tf_op jit(solution)/shard_map/ppermute | solution.py:616
  234.9 18.8 %collective-permute-done.24 = f32[16]{0:T(128)S(1)} collective-permute-done((f32[16]{0:T(128)S(1)}, f32[16]{0:T(128)S(1)}, u32[]{:S(2)}, u32[]{:S(2)}) %collective-permute-start.24) | collective-permute-done | bytes 96 | tf_op jit(solution)/shard_map/ppermute | solution.py:616
  253.7 4.4 collective-permute-start.25
  258.2 8.9 %collective-permute-done.25 = f32[16]{0:T(128)S(1)} collective-permute-done((f32[16]{0:T(128)S(1)}, f32[16]{0:T(128)S(1)}, u32[]{:S(2)}, u32[]{:S(2)}) %collective-permute-start.25) | collective-permute-done | bytes 96 | tf_op jit(solution)/shard_map/ppermute | solution.py:616
  277.2 44.8 %shard_map.264 = (bf16[1280,768]{1,0:T(8,128)(2,1)}, bf16[1280,768]{1,0:T(8,128)(2,1)}, bf16[1280,3072]{1,0:T(8,128)(2,1)}, bf16[1280,3072]{1,0:T(8,128)(2,1)}, ...) custom-call(bf16[1280,768]{1,0:T(8,128)(2,1)} %bitcast.21.x_ref.refs_0_, bf16[1280,768]{1,0:T(8,128)(2,1)} %bitcast.23.c_ref, ...), custom_call_target="tpu_custom_call" | custom-call | flops 24159191040 | bytes 30000000 | tf_op jit(solution)/shard_map/pallas_call | solution.py:479
  322.0 4.9 all-to-all-start.3
  332.9 26.2 %collective-permute-done.69.refs_5_ = bf16[1280,768]{1,0:T(8,128)(2,1)} collective-permute-done((bf16[1280,768]{1,0:T(8,128)(2,1)}, bf16[1280,768]{1,0:T(8,128)(2,1)}, u32[]{:S(2)}, u32[]{:S(2)}) %collective-permute-start.69) | collective-permute-done | bytes 1966112 | tf_op jit(solution)/shard_map/ppermute | solution.py:616
  359.1 53.0 %shard_map.267 = (f32[768,3072]{1,0:T(8,128)}, f32[3072,768]{1,0:T(8,128)}) custom-call(bf16[1280,768]{1,0:T(8,128)(2,1)} %bitcast.21.x_ref.refs_0_, bf16[1280,768]{1,0:T(8,128)(2,1)} %get-tuple-element.47.refs_1_, bf16[1280,3072]{1,0:T(8,128)(2,1)} %get-tuple-element.48.refs_2_, bf16[1280,3072]{1,0:T(8,128)(2,1)} %get-tuple-element.49.refs_3_, ...), custom_call_target="tpu_custom_call" | custom-call | flops 36238786560 | bytes 45000000 | tf_op jit(solution)/shard_map/pallas_call | solution.py:583
  412.1 4.6 all-to-all-start.2
  416.7 4.6 multiply_reduce_fusion
  422.6 2.7 convolution_convert_fusion.1.dctx_ref
  425.3 39.8 %shard_map.266 = (bf16[1024,384]{1,0:T(8,128)(2,1)}, bf16[2048,384]{1,0:T(8,128)(2,1)}, bf16[2048,384]{1,0:T(8,128)(2,1)}, f32[6,8,128]{2,1,0:T(8,128)}) custom-call(bf16[1024,768]{1,0:T(8,128)(2,1)} %convolution_convert_fusion.2.q_ref, bf16[2048,1536]{1,0:T(8,128)(2,1)} %convolution_convert_fusion.k_ref.v_ref, ...), custom_call_target="tpu_custom_call" | custom-call | flops 16106127360 | bytes 27000000 | tf_op jit(solution)/shard_map/pallas_call | solution.py:342
  465.1 39.7 %shard_map.265 = (bf16[1024,384]{1,0:T(8,128)(2,1)}, bf16[2048,384]{1,0:T(8,128)(2,1)}, bf16[2048,384]{1,0:T(8,128)(2,1)}, f32[6,8,128]{2,1,0:T(8,128)}) custom-call(bf16[1024,768]{1,0:T(8,128)(2,1)} %convolution_convert_fusion.2.q_ref, bf16[2048,1536]{1,0:T(8,128)(2,1)} %convolution_convert_fusion.k_ref.v_ref, ...), custom_call_target="tpu_custom_call" | custom-call | flops 16106127360 | bytes 27000000 | tf_op jit(solution)/shard_map/pallas_call | solution.py:342
  504.8 7.8 %fusion.5 = f32[2048,768]{0,1:T(8,128)S(1)} fusion(bf16[2048,384]{1,0:T(8,128)(2,1)S(1)} %copy-done.72, bf16[2048,384]{1,0:T(8,128)(2,1)} %get-tuple-element.40, bf16[2048,384]{1,0:T(8,128)(2,1)} %get-tuple-element.39, bf16[2048,384]{1,0:T(8,128)(2,1)} %get-tuple-element.38, bf16[768,1152]{1,0:T(8,128)(2,1)} %bitcast.122, bf16[768,1152]{1,0:T(8,128)(2,1)} %copy-done.30), kind=kOutput, calls=%fused_computation.8 | convolution fusion | flops 4861722624 | bytes 16121856 | tf_op jit(solution)/shard_map/dot_general | solution.py:89
  528.7 5.0 add_convert_fusion
  533.7 2.9 copy.183
  538.1 4.0 collective-permute-start.32
  562.4 2.7 collective-permute-start.40
  565.2 7.0 %collective-permute-done.40 = bf16[1,2,2,1,48,384]{5,4,3,2,1,0:T(8,128)(2,1)S(1)} collective-permute-done((bf16[1,2,2,1,48,384]{5,4,3,2,1,0:T(8,128)(2,1)S(1)}, bf16[1,2,2,1,48,384]{5,4,3,2,1,0:T(8,128)(2,1)S(1)}, u32[]{:S(2)}, u32[]{:S(2)}) %collective-permute-start.40) | collective-permute-done | bytes 147488 | tf_op jit(solution)/shard_map/ppermute | solution.py:616
  576.3 2.7 collective-permute-done.41
  599.4 13.7 %collective-permute-done.51 = bf16[1,2,1,1,48,512]{5,4,3,2,1,0:T(8,128)(2,1)} collective-permute-done((bf16[1,2,1,1,48,512]{5,4,3,2,1,0:T(8,128)(2,1)}, bf16[1,2,1,1,48,512]{5,4,3,2,1,0:T(8,128)(2,1)}, u32[]{:S(2)}, u32[]{:S(2)}) %collective-permute-start.51) | collective-permute-done | bytes 98336 | tf_op jit(solution)/shard_map/ppermute | solution.py:616
  614.0 5.3 collective-permute-done.46
  620.3 5.5 collective-permute-done.66
  626.8 3.1 collective-permute-done.52
  642.7 3.8 fusion.21
  648.8 4.1 fusion.20
  652.9 3.6 copy.184
  667.3 3.6 collective-permute-done.36
  672.0 2.7 collective-permute-done.37
  (487 shorter events, 177.1 us)
Async XLA Ops:
  3.2 102.7 %collective-permute-start.2 = (bf16[1,1,1,48,1280]{4,3,2,1,0:T(8,128)(2,1)S(1)}, bf16[1,1,1,48,1280]{4,3,2,1,0:T(8,128)(2,1)S(1)}, u32[]{:S(2)}, u32[]{:S(2)}) collective-permute-start(bf16[1,1,1,48,1280]{4,3,2,1,0:T(8,128)(2,1)S(1)} %fusion.69), channel_id=1, source_target_pairs={{0,12},{4,0},{8,4},{12,8},{1,13},{5,1},{9,5},{13,9},{2,14},{6,2},{... | collective-permute-start | bytes 368648 | tf_op jit(solution)/shard_map/ppermute | solution.py:638
  8.3 99.2 %collective-permute-start.3 = (bf16[1,1,1,48,1280]{4,3,2,1,0:T(8,128)(2,1)S(1)}, bf16[1,1,1,48,1280]{4,3,2,1,0:T(8,128)(2,1)}, u32[]{:S(2)}, u32[]{:S(2)}) collective-permute-start(bf16[1,1,1,48,1280]{4,3,2,1,0:T(8,128)(2,1)S(1)} %fusion.69), channel_id=1, source_target_pairs={{0,8},{4,12},{8,0},{12,4},{1,9},{5,13},{9,1},{13,5},{2,10},{6,14},... | collective-permute-start | bytes 368648 | tf_op jit(solution)/shard_map/ppermute | solution.py:638
  8.3 101.4 %collective-permute-start.4 = (bf16[1,1,1,48,1280]{4,3,2,1,0:T(8,128)(2,1)S(1)}, bf16[1,1,1,48,1280]{4,3,2,1,0:T(8,128)(2,1)}, u32[]{:S(2)}, u32[]{:S(2)}) collective-permute-start(bf16[1,1,1,48,1280]{4,3,2,1,0:T(8,128)(2,1)S(1)} %fusion.69), channel_id=1, source_target_pairs={{0,4},{4,8},{8,12},{12,0},{1,5},{5,9},{9,13},{13,1},{2,6},{6,10},{... | collective-permute-start | bytes 368648 | tf_op jit(solution)/shard_map/ppermute | solution.py:638
  10.7 32.3 %collective-permute-start.12 = (bf16[1,1,1,48,384]{4,3,2,1,0:T(8,128)(2,1)}, bf16[1,1,1,48,384]{4,3,2,1,0:T(8,128)(2,1)}, u32[]{:S(2)}, u32[]{:S(2)}) collective-permute-start(bf16[1,1,1,48,384]{4,3,2,1,0:T(8,128)(2,1)} %get-tuple-element.143), channel_id=1, source_target_pairs={{0,12},{4,0},{8,4},{12,8},{1,13},{5,1},{9,5},{13,9},{2,14},{6,2},{... | collective-permute-start | bytes 110600 | tf_op jit(solution)/shard_map/ppermute | solution.py:638
  13.5 32.1 %collective-permute-start.13 = (bf16[1,1,1,48,384]{4,3,2,1,0:T(8,128)(2,1)}, bf16[1,1,1,48,384]{4,3,2,1,0:T(8,128)(2,1)}, u32[]{:S(2)}, u32[]{:S(2)}) collective-permute-start(bf16[1,1,1,48,384]{4,3,2,1,0:T(8,128)(2,1)} %get-tuple-element.143), channel_id=1, source_target_pairs={{0,8},{4,12},{8,0},{12,4},{1,9},{5,13},{9,1},{13,5},{2,10},{6,14},... | collective-permute-start | bytes 110600 | tf_op jit(solution)/shard_map/ppermute | solution.py:638
  30.1 186.1 %all-to-all-start.1 = ((bf16[16,80,768]{2,1,0:T(8,128)(2,1)}), bf16[16,80,768]{2,1,0:T(8,128)(2,1)}, u32[]{:S(2)}, u32[]{:S(2)}) async-start(bf16[16,80,768]{2,1,0:T(8,128)(2,1)} %bitcast.22), calls=%async_computation.1 | async-start | bytes 3932160 | tf_op jit(solution)/shard_map/all_to_all | solution.py:719
  43.0 29.1 %collective-permute-start.14 = (bf16[1,1,1,48,384]{4,3,2,1,0:T(8,128)(2,1)}, bf16[1,1,1,48,384]{4,3,2,1,0:T(8,128)(2,1)S(1)}, u32[]{:S(2)}, u32[]{:S(2)}) collective-permute-start(bf16[1,1,1,48,384]{4,3,2,1,0:T(8,128)(2,1)} %get-tuple-element.143), channel_id=1, source_target_pairs={{0,4},{4,8},{8,12},{12,0},{1,5},{5,9},{9,13},{13,1},{2,6},{6,10},{... | collective-permute-start | bytes 110600 | tf_op jit(solution)/shard_map/ppermute | solution.py:638
  45.6 98.7 %collective-permute-start.1 = (bf16[512,768]{0,1:T(8,128)(2,1)S(1)}, bf16[512,768]{0,1:T(8,128)(2,1)S(1)}, u32[]{:S(2)}, u32[]{:S(2)}) collective-permute-start(bf16[512,768]{0,1:T(8,128)(2,1)S(1)} %get-tuple-element.142), channel_id=1, source_target_pairs={{1,0},{2,1},{3,2},{5,4},{6,5},{7,6},{9,8},{10,9},{11,10},{13,12},{... | collective-permute-start | bytes 2359304 | tf_op jit(solution)/shard_map/ppermute | solution.py:752
  81.8 9.5 %collective-permute-start.18 = (bf16[1,2,1,48,384]{4,3,2,1,0:T(8,128)(2,1)S(1)}, bf16[1,2,1,48,384]{4,3,2,1,0:T(8,128)(2,1)S(1)}, u32[]{:S(2)}, u32[]{:S(2)}) collective-permute-start(bf16[1,2,1,48,384]{4,3,2,1,0:T(8,128)(2,1)S(1)} %fusion.74), channel_id=1, source_target_pairs={{0,12},{4,0},{8,4},{12,8},{1,13},{5,1},{9,5},{13,9},{2,14},{6,2},{... | collective-permute-start | bytes 221192 | tf_op jit(solution)/shard_map/ppermute | solution.py:638
  104.3 40.0 %collective-permute-start = (bf16[512,768]{0,1:T(8,128)(2,1)S(1)}, bf16[512,768]{0,1:T(8,128)(2,1)S(1)}, u32[]{:S(2)}, u32[]{:S(2)}) collective-permute-start(bf16[512,768]{0,1:T(8,128)(2,1)S(1)} %get-tuple-element.141), channel_id=1, source_target_pairs={{0,1},{1,2},{2,3},{4,5},{5,6},{6,7},{8,9},{9,10},{10,11},{12,13},{... | collective-permute-start | bytes 2359304 | tf_op jit(solution)/shard_map/ppermute | solution.py:752
  105.8 8.5 %collective-permute-start.15 = (bf16[4,1,1,48,384]{4,3,2,1,0:T(8,128)(2,1)S(1)}, bf16[4,1,1,48,384]{4,3,2,1,0:T(8,128)(2,1)S(1)}, u32[]{:S(2)}, u32[]{:S(2)}) collective-permute-start(bf16[4,1,1,48,384]{4,3,2,1,0:T(8,128)(2,1)S(1)} %constant_dynamic-slice_fusion.30), channel_id=1, source_target_pairs={{0,2},{1,3},{2,0},{3,1},{4,6},{5,7},{6,4},{7,5},{8,10},{9,11},{10,... | collective-permute-start | bytes 442376 | tf_op jit(solution)/shard_map/ppermute | solution.py:616
  107.5 7.5 %collective-permute-start.8 = (bf16[1,2,1,48,1152]{4,3,2,1,0:T(8,128)(2,1)S(1)}, bf16[1,2,1,48,1152]{4,3,2,1,0:T(8,128)(2,1)S(1)}, u32[]{:S(2)}, u32[]{:S(2)}) collective-permute-start(bf16[1,2,1,48,1152]{4,3,2,1,0:T(8,128)(2,1)S(1)} %fusion.62), channel_id=1, source_target_pairs={{0,12},{4,0},{8,4},{12,8},{1,13},{5,1},{9,5},{13,9},{2,14},{6,2},{... | collective-permute-start | bytes 663560 | tf_op jit(solution)/shard_map/ppermute | solution.py:638
  109.6 20.5 %collective-permute-start.9 = (bf16[1,2,1,48,1152]{4,3,2,1,0:T(8,128)(2,1)S(1)}, bf16[1,2,1,48,1152]{4,3,2,1,0:T(8,128)(2,1)S(1)}, u32[]{:S(2)}, u32[]{:S(2)}) collective-permute-start(bf16[1,2,1,48,1152]{4,3,2,1,0:T(8,128)(2,1)S(1)} %fusion.62), channel_id=1, source_target_pairs={{0,8},{4,12},{8,0},{12,4},{1,9},{5,13},{9,1},{13,5},{2,10},{6,14},... | collective-permute-start | bytes 663560 | tf_op jit(solution)/shard_map/ppermute | solution.py:638
  114.3 15.9 %collective-permute-start.10 = (bf16[1,2,1,48,1152]{4,3,2,1,0:T(8,128)(2,1)S(1)}, bf16[1,2,1,48,1152]{4,3,2,1,0:T(8,128)(2,1)S(1)}, u32[]{:S(2)}, u32[]{:S(2)}) collective-permute-start(bf16[1,2,1,48,1152]{4,3,2,1,0:T(8,128)(2,1)S(1)} %fusion.62), channel_id=1, source_target_pairs={{0,4},{4,8},{8,12},{12,0},{1,5},{5,9},{9,13},{13,1},{2,6},{6,10},{... | collective-permute-start | bytes 663560 | tf_op jit(solution)/shard_map/ppermute | solution.py:638
  115.0 28.1 %collective-permute-start.21 = (bf16[4,2,1,48,384]{4,3,2,1,0:T(8,128)(2,1)S(1)}, bf16[4,2,1,48,384]{4,3,2,1,0:T(8,128)(2,1)S(1)}, u32[]{:S(2)}, u32[]{:S(2)}) collective-permute-start(bf16[4,2,1,48,384]{4,3,2,1,0:T(8,128)(2,1)S(1)} %constant_dynamic-slice_fusion.29), channel_id=1, source_target_pairs={{0,1},{1,0},{2,3},{3,2},{4,5},{5,4},{6,7},{7,6},{8,9},{9,8},{10,11... | collective-permute-start | bytes 884744 | tf_op jit(solution)/shard_map/ppermute | solution.py:616
  130.2 12.4 %collective-permute-start.5 = (bf16[4,1,1,48,1280]{4,3,2,1,0:T(8,128)(2,1)S(1)}, bf16[4,1,1,48,1280]{4,3,2,1,0:T(8,128)(2,1)S(1)}, u32[]{:S(2)}, u32[]{:S(2)}) collective-permute-start(bf16[4,1,1,48,1280]{4,3,2,1,0:T(8,128)(2,1)S(1)} %constant_dynamic-slice_fusion.32), channel_id=1, source_target_pairs={{0,2},{1,3},{2,0},{3,1},{4,6},{5,7},{6,4},{7,5},{8,10},{9,11},{10,... | collective-permute-start | bytes 1474568 | tf_op jit(solution)/shard_map/ppermute | solution.py:616
  130.2 13.7 %collective-permute-start.16 = (bf16[4,2,1,48,384]{4,3,2,1,0:T(8,128)(2,1)S(1)}, bf16[4,2,1,48,384]{4,3,2,1,0:T(8,128)(2,1)S(1)}, u32[]{:S(2)}, u32[]{:S(2)}) collective-permute-start(bf16[4,2,1,48,384]{4,3,2,1,0:T(8,128)(2,1)S(1)} %fusion.59), channel_id=1, source_target_pairs={{0,1},{1,0},{2,3},{3,2},{4,5},{5,4},{6,7},{7,6},{8,9},{9,8},{10,11... | collective-permute-start | bytes 884744 | tf_op jit(solution)/shard_map/ppermute | solution.py:616
  216.3 59.0 %all-to-all-start = ((bf16[16,80,768]{2,1,0:T(8,128)(2,1)}), bf16[16,80,768]{2,1,0:T(8,128)(2,1)}, u32[]{:S(2)}, u32[]{:S(2)}) async-start(bf16[16,80,768]{2,1,0:T(8,128)(2,1)} %bitcast.119), calls=%async_computation | async-start | bytes 3932160 | tf_op jit(solution)/shard_map/all_to_all | solution.py:719
  223.8 9.1 %collective-permute-start.23 = (f32[16]{0:T(128)S(1)}, f32[16]{0:T(128)S(1)}, u32[]{:S(2)}, u32[]{:S(2)}) collective-permute-start(f32[16]{0:T(128)S(1)} %add.373), channel_id=1, source_target_pairs={{0,2},{1,3},{2,0},{3,1},{4,6},{5,7},{6,4},{7,5},{8,10},{9,11},{10,... | collective-permute-start | bytes 200 | tf_op jit(solution)/shard_map/ppermute | solution.py:616
  225.6 7.7 %collective-permute-start.28 = (f32[16]{0:T(128)S(1)}, f32[16]{0:T(128)S(1)}, u32[]{:S(2)}, u32[]{:S(2)}) collective-permute-start(f32[16]{0:T(128)S(1)} %add.379), channel_id=1, source_target_pairs={{0,2},{1,3},{2,0},{3,1},{4,6},{5,7},{6,4},{7,5},{8,10},{9,11},{10,... | collective-permute-start | bytes 200 | tf_op jit(solution)/shard_map/ppermute | solution.py:616
  232.9 20.8 %collective-permute-start.24 = (f32[16]{0:T(128)S(1)}, f32[16]{0:T(128)S(1)}, u32[]{:S(2)}, u32[]{:S(2)}) collective-permute-start(f32[16]{0:T(128)S(1)} %add.374), channel_id=1, source_target_pairs={{0,4},{4,0},{8,12},{12,8},{1,5},{5,1},{9,13},{13,9},{2,6},{6,2},{1... | collective-permute-start | bytes 200 | tf_op jit(solution)/shard_map/ppermute | solution.py:616
  233.3 24.8 %collective-permute-start.29 = (f32[16]{0:T(128)S(1)}, f32[16]{0:T(128)S(1)}, u32[]{:S(2)}, u32[]{:S(2)}) collective-permute-start(f32[16]{0:T(128)S(1)} %add.380), channel_id=1, source_target_pairs={{0,4},{4,0},{8,12},{12,8},{1,5},{5,1},{9,13},{13,9},{2,6},{6,2},{1... | collective-permute-start | bytes 200 | tf_op jit(solution)/shard_map/ppermute | solution.py:616
  253.7 13.4 %collective-permute-start.25 = (f32[16]{0:T(128)S(1)}, f32[16]{0:T(128)S(1)}, u32[]{:S(2)}, u32[]{:S(2)}) collective-permute-start(f32[16]{0:T(128)S(1)} %add.375), channel_id=1, source_target_pairs={{0,8},{4,12},{8,0},{12,4},{1,9},{5,13},{9,1},{13,5},{2,10},{6,14},... | collective-permute-start | bytes 200 | tf_op jit(solution)/shard_map/ppermute | solution.py:616
  258.1 10.5 %collective-permute-start.30 = (f32[16]{0:T(128)S(1)}, f32[16]{0:T(128)S(1)}, u32[]{:S(2)}, u32[]{:S(2)}) collective-permute-start(f32[16]{0:T(128)S(1)} %add.381), channel_id=1, source_target_pairs={{0,8},{4,12},{8,0},{12,4},{1,9},{5,13},{9,1},{13,5},{2,10},{6,14},... | collective-permute-start | bytes 200 | tf_op jit(solution)/shard_map/ppermute | solution.py:616
  274.0 58.9 %collective-permute-start.70 = (bf16[1280,768]{1,0:T(8,128)(2,1)}, bf16[1280,768]{1,0:T(8,128)(2,1)}, u32[]{:S(2)}, u32[]{:S(2)}) collective-permute-start(bf16[1280,768]{1,0:T(8,128)(2,1)} %bitcast.23.c_ref), channel_id=1, source_target_pairs={{0,16},{16,0},{1,17},{17,1},{2,18},{18,2},{3,19},{19,3},{4,20},{20... | collective-permute-start | bytes 5898248 | tf_op jit(solution)/shard_map/ppermute | solution.py:616
  275.2 83.8 %collective-permute-start.69 = (bf16[1280,768]{1,0:T(8,128)(2,1)}, bf16[1280,768]{1,0:T(8,128)(2,1)}, u32[]{:S(2)}, u32[]{:S(2)}) collective-permute-start(bf16[1280,768]{1,0:T(8,128)(2,1)} %bitcast.21.x_ref.refs_0_), channel_id=1, source_target_pairs={{0,16},{16,0},{1,17},{17,1},{2,18},{18,2},{3,19},{19,3},{4,20},{20... | collective-permute-start | bytes 5898248 | tf_op jit(solution)/shard_map/ppermute | solution.py:616
  322.0 90.1 %all-to-all-start.3 = ((bf16[16,80,768]{2,1,0:T(8,128)(2,1)}), bf16[16,80,768]{2,1,0:T(8,128)(2,1)}, u32[]{:S(2)}, u32[]{:S(2)}) async-start(bf16[16,80,768]{2,1,0:T(8,128)(2,1)} %bitcast.120), calls=%async_computation.3 | async-start | bytes 3932160 | tf_op jit(solution)/shard_map/all_to_all | solution.py:719
  412.1 116.6 %all-to-all-start.2 = ((bf16[16,80,768]{2,1,0:T(8,128)(2,1)}), bf16[16,80,768]{2,1,0:T(8,128)(2,1)}, u32[]{:S(2)}, u32[]{:S(2)}) async-start(bf16[16,80,768]{2,1,0:T(8,128)(2,1)} %bitcast.118), calls=%async_computation.2 | async-start | bytes 3932160 | tf_op jit(solution)/shard_map/all_to_all | solution.py:719
  536.7 102.4 %collective-permute-start.33 = (bf16[512,768]{0,1:T(8,128)(2,1)}, bf16[512,768]{0,1:T(8,128)(2,1)}, u32[]{:S(2)}, u32[]{:S(2)}) collective-permute-start(bf16[512,768]{0,1:T(8,128)(2,1)} %get-tuple-element.138), channel_id=1, source_target_pairs={{1,0},{2,1},{3,2},{5,4},{6,5},{7,6},{9,8},{10,9},{11,10},{13,12},{... | collective-permute-start | bytes 2359304 | tf_op jit(solution)/shard_map/ppermute | solution.py:892
  538.1 103.1 %collective-permute-start.32 = (bf16[512,768]{0,1:T(8,128)(2,1)}, bf16[512,768]{0,1:T(8,128)(2,1)}, u32[]{:S(2)}, u32[]{:S(2)}) collective-permute-start(bf16[512,768]{0,1:T(8,128)(2,1)} %get-tuple-element.137), channel_id=1, source_target_pairs={{0,1},{1,2},{2,3},{4,5},{5,6},{6,7},{8,9},{9,10},{10,11},{12,13},{... | collective-permute-start | bytes 2359304 | tf_op jit(solution)/shard_map/ppermute | solution.py:893
  544.0 13.7 %collective-permute-start.39 = (bf16[2,2,2,1,48,384]{5,4,3,2,1,0:T(8,128)(2,1)}, bf16[2,2,2,1,48,384]{5,4,3,2,1,0:T(8,128)(2,1)}, u32[]{:S(2)}, u32[]{:S(2)}) collective-permute-start(bf16[2,2,2,1,48,384]{5,4,3,2,1,0:T(8,128)(2,1)} %constant_dynamic-slice_fusion.23), channel_id=1, source_target_pairs={{0,1},{1,0},{2,3},{3,2},{4,5},{5,4},{6,7},{7,6},{8,9},{9,8},{10,11... | collective-permute-start | bytes 884744 | tf_op jit(solution)/shard_map/ppermute | solution.py:616
  546.9 12.5 %collective-permute-start.49 = (bf16[2,2,2,1,48,512]{5,4,3,2,1,0:T(8,128)(2,1)}, bf16[2,2,2,1,48,512]{5,4,3,2,1,0:T(8,128)(2,1)}, u32[]{:S(2)}, u32[]{:S(2)}) collective-permute-start(bf16[2,2,2,1,48,512]{5,4,3,2,1,0:T(8,128)(2,1)} %constant_dynamic-slice_fusion.15), channel_id=1, source_target_pairs={{0,1},{1,0},{2,3},{3,2},{4,5},{5,4},{6,7},{7,6},{8,9},{9,8},{10,11... | collective-permute-start | bytes 1179656 | tf_op jit(solution)/shard_map/ppermute | solution.py:616
  551.4 9.3 %collective-permute-start.44 = (bf16[2,2,2,1,48,512]{5,4,3,2,1,0:T(8,128)(2,1)}, bf16[2,2,2,1,48,512]{5,4,3,2,1,0:T(8,128)(2,1)}, u32[]{:S(2)}, u32[]{:S(2)}) collective-permute-start(bf16[2,2,2,1,48,512]{5,4,3,2,1,0:T(8,128)(2,1)} %constant_dynamic-slice_fusion.19), channel_id=1, source_target_pairs={{0,1},{1,0},{2,3},{3,2},{4,5},{5,4},{6,7},{7,6},{8,9},{9,8},{10,11... | collective-permute-start | bytes 1179656 | tf_op jit(solution)/shard_map/ppermute | solution.py:616
  557.7 16.3 %collective-permute-start.59 = (bf16[2,2,2,1,48,640]{5,4,3,2,1,0:T(8,128)(2,1)}, bf16[2,2,2,1,48,640]{5,4,3,2,1,0:T(8,128)(2,1)S(1)}, u32[]{:S(2)}, u32[]{:S(2)}) collective-permute-start(bf16[2,2,2,1,48,640]{5,4,3,2,1,0:T(8,128)(2,1)} %constant_dynamic-slice_fusion.7), channel_id=1, source_target_pairs={{0,1},{1,0},{2,3},{3,2},{4,5},{5,4},{6,7},{7,6},{8,9},{9,8},{10,11... | collective-permute-start | bytes 1474568 | tf_op jit(solution)/shard_map/ppermute | solution.py:616
  560.7 13.9 %collective-permute-start.54 = (bf16[2,2,2,1,48,640]{5,4,3,2,1,0:T(8,128)(2,1)S(1)}, bf16[2,2,2,1,48,640]{5,4,3,2,1,0:T(8,128)(2,1)S(1)}, u32[]{:S(2)}, u32[]{:S(2)}) collective-permute-start(bf16[2,2,2,1,48,640]{5,4,3,2,1,0:T(8,128)(2,1)S(1)} %copy-done.48), channel_id=1, source_target_pairs={{0,1},{1,0},{2,3},{3,2},{4,5},{5,4},{6,7},{7,6},{8,9},{9,8},{10,11... | collective-permute-start | bytes 1474568 | tf_op jit(solution)/shard_map/ppermute | solution.py:616
  562.4 9.9 %collective-permute-start.40 = (bf16[1,2,2,1,48,384]{5,4,3,2,1,0:T(8,128)(2,1)S(1)}, bf16[1,2,2,1,48,384]{5,4,3,2,1,0:T(8,128)(2,1)S(1)}, u32[]{:S(2)}, u32[]{:S(2)}) collective-permute-start(bf16[1,2,2,1,48,384]{5,4,3,2,1,0:T(8,128)(2,1)S(1)} %constant_dynamic-slice_fusion.22), channel_id=1, source_target_pairs={{0,8},{4,12},{8,0},{12,4},{1,9},{5,13},{9,1},{13,5},{2,10},{6,14},... | collective-permute-start | bytes 442376 | tf_op jit(solution)/shard_map/ppermute | solution.py:616
  572.3 13.1 %collective-permute-start.50 = (bf16[2,2,1,1,48,512]{5,4,3,2,1,0:T(8,128)(2,1)S(1)}, bf16[2,2,1,1,48,512]{5,4,3,2,1,0:T(8,128)(2,1)S(1)}, u32[]{:S(2)}, u32[]{:S(2)}) collective-permute-start(bf16[2,2,1,1,48,512]{5,4,3,2,1,0:T(8,128)(2,1)S(1)} %constant_dynamic-slice_fusion.14), channel_id=1, source_target_pairs={{0,2},{1,3},{2,0},{3,1},{4,6},{5,7},{6,4},{7,5},{8,10},{9,11},{10,... | collective-permute-start | bytes 589832 | tf_op jit(solution)/shard_map/ppermute | solution.py:616
  574.0 12.8 %collective-permute-start.45 = (bf16[2,2,1,1,48,512]{5,4,3,2,1,0:T(8,128)(2,1)S(1)}, bf16[2,2,1,1,48,512]{5,4,3,2,1,0:T(8,128)(2,1)S(1)}, u32[]{:S(2)}, u32[]{:S(2)}) collective-permute-start(bf16[2,2,1,1,48,512]{5,4,3,2,1,0:T(8,128)(2,1)S(1)} %constant_dynamic-slice_fusion.18), channel_id=1, source_target_pairs={{0,2},{1,3},{2,0},{3,1},{4,6},{5,7},{6,4},{7,5},{8,10},{9,11},{10,... | collective-permute-start | bytes 589832 | tf_op jit(solution)/shard_map/ppermute | solution.py:616
  585.4 45.2 %collective-permute-start.60 = (bf16[1,2,2,1,48,640]{5,4,3,2,1,0:T(8,128)(2,1)}, bf16[1,2,2,1,48,640]{5,4,3,2,1,0:T(8,128)(2,1)}, u32[]{:S(2)}, u32[]{:S(2)}) collective-permute-start(bf16[1,2,2,1,48,640]{5,4,3,2,1,0:T(8,128)(2,1)} %constant_dynamic-slice_fusion.6), channel_id=1, source_target_pairs={{0,8},{4,12},{8,0},{12,4},{1,9},{5,13},{9,1},{13,5},{2,10},{6,14},... | collective-permute-start | bytes 737288 | tf_op jit(solution)/shard_map/ppermute | solution.py:616
  586.7 49.8 %collective-permute-start.55 = (bf16[1,2,2,1,48,640]{5,4,3,2,1,0:T(8,128)(2,1)}, bf16[1,2,2,1,48,640]{5,4,3,2,1,0:T(8,128)(2,1)}, u32[]{:S(2)}, u32[]{:S(2)}) collective-permute-start(bf16[1,2,2,1,48,640]{5,4,3,2,1,0:T(8,128)(2,1)} %constant_dynamic-slice_fusion.10), channel_id=1, source_target_pairs={{0,8},{4,12},{8,0},{12,4},{1,9},{5,13},{9,1},{13,5},{2,10},{6,14},... | collective-permute-start | bytes 737288 | tf_op jit(solution)/shard_map/ppermute | solution.py:616
  594.0 19.0 %collective-permute-start.51 = (bf16[1,2,1,1,48,512]{5,4,3,2,1,0:T(8,128)(2,1)}, bf16[1,2,1,1,48,512]{5,4,3,2,1,0:T(8,128)(2,1)}, u32[]{:S(2)}, u32[]{:S(2)}) collective-permute-start(bf16[1,2,1,1,48,512]{5,4,3,2,1,0:T(8,128)(2,1)} %constant_dynamic-slice_fusion.13), channel_id=1, source_target_pairs={{0,8},{4,12},{8,0},{12,4},{1,9},{5,13},{9,1},{13,5},{2,10},{6,14},... | collective-permute-start | bytes 294920 | tf_op jit(solution)/shard_map/ppermute | solution.py:616
  630.6 8.4 %collective-permute-start.67 = (bf16[1,1,1,1,48,512]{5,4,3,2,1,0:T(8,128)(2,1)S(1)}, bf16[1,1,1,1,48,512]{5,4,3,2,1,0:T(8,128)(2,1)S(1)}, u32[]{:S(2)}, u32[]{:S(2)}) collective-permute-start(bf16[1,1,1,1,48,512]{5,4,3,2,1,0:T(8,128)(2,1)S(1)} %constant_dynamic-slice_fusion), channel_id=1, source_target_pairs={{0,4},{4,0},{8,12},{12,8},{1,5},{5,1},{9,13},{13,9},{2,6},{6,2},{1... | collective-permute-start | bytes 147464 | tf_op jit(solution)/shard_map/ppermute | solution.py:616
  634.4 22.1 %collective-permute-start.53 = (bf16[48,512]{1,0:T(8,128)(2,1)}, bf16[48,512]{1,0:T(8,128)(2,1)}, u32[]{:S(2)}, u32[]{:S(2)}) collective-permute-start(bf16[48,512]{1,0:T(8,128)(2,1)} %fusion.84), channel_id=1, source_target_pairs={{0,16},{16,0},{1,17},{17,1},{2,18},{18,2},{3,19},{19,3},{4,20},{20... | collective-permute-start | bytes 147464 | tf_op jit(solution)/shard_map/ppermute | solution.py:616
  636.6 20.8 %collective-permute-start.48 = (bf16[48,512]{1,0:T(8,128)(2,1)}, bf16[48,512]{1,0:T(8,128)(2,1)}, u32[]{:S(2)}, u32[]{:S(2)}) collective-permute-start(bf16[48,512]{1,0:T(8,128)(2,1)} %fusion.83), channel_id=1, source_target_pairs={{0,16},{16,0},{1,17},{17,1},{2,18},{18,2},{3,19},{19,3},{4,20},{20... | collective-permute-start | bytes 147464 | tf_op jit(solution)/shard_map/ppermute | solution.py:616
  639.0 20.0 %collective-permute-start.61 = (bf16[1,1,2,1,48,640]{5,4,3,2,1,0:T(8,128)(2,1)}, bf16[1,1,2,1,48,640]{5,4,3,2,1,0:T(8,128)(2,1)}, u32[]{:S(2)}, u32[]{:S(2)}) collective-permute-start(bf16[1,1,2,1,48,640]{5,4,3,2,1,0:T(8,128)(2,1)} %constant_dynamic-slice_fusion.5), channel_id=1, source_target_pairs={{0,4},{4,0},{8,12},{12,8},{1,5},{5,1},{9,13},{13,9},{2,6},{6,2},{1... | collective-permute-start | bytes 368648 | tf_op jit(solution)/shard_map/ppermute | solution.py:616
  639.1 21.5 %collective-permute-start.56 = (bf16[1,1,2,1,48,640]{5,4,3,2,1,0:T(8,128)(2,1)}, bf16[1,1,2,1,48,640]{5,4,3,2,1,0:T(8,128)(2,1)}, u32[]{:S(2)}, u32[]{:S(2)}) collective-permute-start(bf16[1,1,2,1,48,640]{5,4,3,2,1,0:T(8,128)(2,1)} %constant_dynamic-slice_fusion.9), channel_id=1, source_target_pairs={{0,4},{4,0},{8,12},{12,8},{1,5},{5,1},{9,13},{13,9},{2,6},{6,2},{1... | collective-permute-start | bytes 368648 | tf_op jit(solution)/shard_map/ppermute | solution.py:616
  663.1 7.9 %collective-permute-start.57 = (bf16[1,1,1,1,48,640]{5,4,3,2,1,0:T(8,128)(2,1)S(1)}, bf16[1,1,1,1,48,640]{5,4,3,2,1,0:T(8,128)(2,1)S(1)}, u32[]{:S(2)}, u32[]{:S(2)}) collective-permute-start(bf16[1,1,1,1,48,640]{5,4,3,2,1,0:T(8,128)(2,1)S(1)} %constant_dynamic-slice_fusion.8), channel_id=1, source_target_pairs={{0,2},{1,3},{2,0},{3,1},{4,6},{5,7},{6,4},{7,5},{8,10},{9,11},{10,... | collective-permute-start | bytes 184328 | tf_op jit(solution)/shard_map/ppermute | solution.py:616
  666.4 9.0 %collective-permute-start.63 = (bf16[48,640]{1,0:T(8,128)(2,1)S(1)}, bf16[48,640]{1,0:T(8,128)(2,1)S(1)}, u32[]{:S(2)}, u32[]{:S(2)}) collective-permute-start(bf16[48,640]{1,0:T(8,128)(2,1)S(1)} %fusion.80), channel_id=1, source_target_pairs={{0,16},{16,0},{1,17},{17,1},{2,18},{18,2},{3,19},{19,3},{4,20},{20... | collective-permute-start | bytes 184328 | tf_op jit(solution)/shard_map/ppermute | solution.py:616
  (105 other events, 1123.9 us)

commit v2 on v1

v2 whole, which is shorter than its diff:
```python
import functools
import math

import jax
import jax.numpy as jnp
import numpy as np
from jax import lax
from jax.experimental import pallas as pl
from jax.experimental.pallas import tpu as pltpu
from jax.sharding import PartitionSpec as P

D = 768
HEADS = 12
HEAD = 64
BUCKETS = 32
MAXDIST = 128
WINDOW = 1024
DOCS = 4
MASKED_SCORE = -1e30
HALF = WINDOW // 2
QB = 256
SUB = 128
KB = QB + WINDOW
PAIRS = HEADS // 2
VMEM_LIMIT = 56 * 1024 * 1024


def thresholds(max_distance, half_count):
    exact_span = half_count // 2
    collected = list(range(1, exact_span + 1))
    for target_level in range(exact_span + 1, half_count):
        candidate = exact_span
        while (
            exact_span
            + int(
                math.log(candidate / exact_span)
                / math.log(max_distance / exact_span)
                * (half_count - exact_span)
            )
            < target_level
        ):
            candidate += 1
        collected.append(candidate)
    return collected


LIMITS = thresholds(MAXDIST, BUCKETS // 2)
assert LIMITS[-1] <= SUB


def bucket_table(distance):
    distance = np.asarray(distance)
    magnitude = np.abs(distance)
    bucket_id = (distance > 0).astype(np.int32) * (BUCKETS // 2)
    for boundary in LIMITS:
        bucket_id = bucket_id + (magnitude >= boundary)
    return bucket_id


def bias_buckets():
    lane = np.arange(2 * SUB)
    rows = []
    for m in (-1, 0, 1):
        rows.append(bucket_table(SUB * m - lane + np.where(lane >= SUB, 2 * SUB, 0)))
    rows.append(np.full(2 * SUB, bucket_table(-WINDOW)))
    rows.append(np.full(2 * SUB, bucket_table(WINDOW)))
    rows += [np.zeros(2 * SUB, np.int32)] * 3
    return np.stack(rows)


def grad_buckets():
    lane = np.arange(SUB)
    rows = [bucket_table(SUB * m - lane) for m in (-1, 0, 1)]
    rows += [bucket_table(SUB * (m + 1) - lane) for m in (-1, 0, 1)]
    rows.append(np.full(SUB, bucket_table(-WINDOW)))
    rows.append(np.full(SUB, bucket_table(WINDOW)))
    return np.stack(rows)


def one_hot(ids):
    return (ids[..., None] == np.arange(BUCKETS)).astype(np.float32)


def dot(a, b):
    return jnp.dot(a, b, preferred_element_type=jnp.float32)


def dot_nt(a, b):
    return lax.dot_general(a, b, (((1,), (1,)), ((), ())), preferred_element_type=jnp.float32)


def head_lanes(shape, axis, h):
    place = lax.broadcasted_iota(jnp.int32, shape, axis)
    return (place < HEAD) if h == 0 else (place >= HEAD)


def fold8(x, op):
    return op(x.reshape(x.shape[0] // 8, 8, x.shape[1]), axis=0)


def block_kind(a, b):
    m = a - b - 4
    return m, "n" if m < -1 else "p" if m > 1 else "v"


def forward_kernel(
    q_ref,
    k_ref,
    v_ref,
    qf_ref,
    kf_ref,
    live_ref,
    w_ref,
    ctx_ref,
    e_ref,
    inv_ref,
    vt,
    bias,
    s_ref,
    peak_ref,
):
    steps = q_ref.shape[0] // QB
    for h in range(2):
        for m in range(3):
            row = jnp.broadcast_to(w_ref[h, m : m + 1, :], (SUB, 2 * SUB))
            bias[h, m] = pltpu.roll(row, 0, 1, stride=1, stride_axis=0)[:, :SUB]
    for s in range(v_ref.shape[0] // QB):
        vt[:, s * QB : (s + 1) * QB] = v_ref[s * QB : (s + 1) * QB, :].T
    row_id = lax.broadcasted_iota(jnp.int32, (SUB, SUB), 0)
    col_id = lax.broadcasted_iota(jnp.int32, (SUB, SUB), 1)

    def stage(score, weigh):
        if score is not None:
            s_now, p_now = s_ref.at[score % 2], peak_ref.at[score % 2]
            rows = pl.ds(pl.multiple_of(score * QB, QB), QB)
            q, qf = q_ref[rows, :], qf_ref[rows, :]
            qx = [
                jnp.concatenate([jnp.where(head_lanes(q.shape, 1, h), q, 0), qf], axis=1)
                for h in range(2)
            ]
            tops = {}
        if weigh is not None:
            s_then, p_then = s_ref.at[weigh % 2], peak_ref.at[weigh % 2]
            totals = {(h, b): jnp.zeros((8, SUB), jnp.float32) for h in range(2) for b in range(2)}
            ct = [jnp.zeros((HEAD, QB), jnp.float32)] * 2
        for c in range(KB // QB):
            if score is not None:
                place = pl.ds(pl.multiple_of(score * QB + c * QB, QB), QB)
                kx = jnp.concatenate([k_ref[place, :], kf_ref[place, :]], axis=1)
                scores = [dot_nt(kx, qx[h]) for h in range(2)]
            if weigh is not None:
                place = pl.ds(pl.multiple_of(weigh * QB + c * QB, QB), QB)
                for h in range(2):
                    chunk = []
                    for a in range(2 * c, 2 * c + 2):
                        line = []
                        for b in range(2):
                            m, kind = block_kind(a, b)
                            if abs(m) > 4:
                                line.append(jnp.zeros((SUB, SUB), jnp.bfloat16))
                                continue
                            row = 3 * h + "nvp".index(kind)
                            cols = slice(b * SUB, (b + 1) * SUB)
                            e = jnp.exp(
                                s_then[h, a * SUB : (a + 1) * SUB, cols] - p_then[row : row + 1, cols]
                            )
                            totals[h, b] = totals[h, b] + fold8(e, jnp.sum)
                            line.append(e.astype(jnp.bfloat16))
                        chunk.append(jnp.concatenate(line, axis=1))
                    chunk = jnp.concatenate(chunk, axis=0)
                    e_ref[0, weigh, h, c * QB : (c + 1) * QB, :] = chunk
                    ct[h] = ct[h] + dot(vt[h * HEAD : (h + 1) * HEAD, place], chunk)
            if score is None:
                continue
            for h in range(2):
                for a in range(2 * c, 2 * c + 2):
                    for b in range(2):
                        m, kind = block_kind(a, b)
                        if abs(m) > 4:
                            continue
                        x = scores[h][
                            (a - 2 * c) * SUB : (a - 2 * c + 1) * SUB, b * SUB : (b + 1) * SUB
                        ]
                        if m == -4:
                            x = jnp.where(row_id >= col_id, x, MASKED_SCORE)
                        if m == 4:
                            x = jnp.where(row_id <= col_id, x, MASKED_SCORE)
                        if kind == "v":
                            x = x + bias[h, m + 1]
                        s_now[h, a * SUB : (a + 1) * SUB, b * SUB : (b + 1) * SUB] = x
                        top = fold8(x, jnp.max)
                        old = tops.get((h, b, kind))
                        tops[h, b, kind] = top if old is None else jnp.maximum(old, top)
        if score is not None:
            for h in range(2):
                neg, pos = w_ref[h, 3:4, :SUB], w_ref[h, 4:5, :SUB]
                for b in range(2):
                    peak = jnp.maximum(
                        jnp.maximum(tops[h, b, "n"] + neg, tops[h, b, "p"] + pos), tops[h, b, "v"]
                    )
                    peak = jnp.max(peak, axis=0, keepdims=True)
                    p_now[3 * h : 3 * h + 3, b * SUB : (b + 1) * SUB] = jnp.concatenate(
                        [peak - neg, peak, peak - pos], axis=0
                    )
        if weigh is not None:
            contexts = []
            for h in range(2):
                total = [jnp.sum(totals[h, b], axis=0, keepdims=True) for b in range(2)]
                inv = 1.0 / jnp.concatenate(total, axis=1)
                inv_ref[0, weigh, h : h + 1, :] = inv
                contexts.append(ct[h] * inv)
            context = jnp.concatenate(contexts, axis=0).T.astype(jnp.bfloat16)
            rows = pl.ds(pl.multiple_of(weigh * QB, QB), QB)
            own = v_ref[pl.ds(pl.multiple_of(weigh * QB + HALF, QB), QB), :]
            ctx_ref[rows, :] = jnp.where(live_ref[rows, :] > 0, context, own)

    stage(0, None)

    def both(t, _):
        stage(t, t - 1)
        return 0

    lax.fori_loop(1, steps, both, 0)
    stage(None, steps - 1)


def backward_kernel(
    q_ref,
    k_ref,
    v_ref,
    live_ref,
    e_ref,
    inv_ref,
    ctx_ref,
    dctx_ref,
    dq_ref,
    dk_ref,
    dv_ref,
    db_ref,
    kt,
    dk_acc,
    dv_acc,
    acc,
    far,
):
    steps = q_ref.shape[0] // QB
    for s in range(k_ref.shape[0] // QB):
        kt[:, s * QB : (s + 1) * QB] = k_ref[s * QB : (s + 1) * QB, :].T
    dk_acc[...] = jnp.zeros_like(dk_acc)
    dv_acc[...] = jnp.zeros_like(dv_acc)
    acc[...] = jnp.zeros_like(acc)
    far[...] = jnp.zeros_like(far)

    def block(i, _):
        rows = pl.ds(pl.multiple_of(i * QB, QB), QB)
        q = q_ref[rows, :]
        dctx = dctx_ref[rows, :].astype(jnp.float32)
        kept = jnp.where(live_ref[rows, :] > 0, dctx, 0.0)
        prod = (kept * ctx_ref[rows, :].astype(jnp.float32)).T
        kept_t = kept.T
        qs, dts, deltas = [], [], []
        for h in range(2):
            inv = inv_ref[0, i, h : h + 1, :]
            qs.append(jnp.where(head_lanes(q.shape, 1, h), q, 0))
            dts.append(
                jnp.where(head_lanes(kept_t.shape, 0, h), kept_t * inv, 0.0).astype(jnp.bfloat16)
            )
            deltas.append(jnp.sum(prod[h * HEAD : (h + 1) * HEAD], axis=0, keepdims=True) * inv)
        q_both = jnp.concatenate(qs, axis=0)
        dt_both = jnp.concatenate(dts, axis=1)
        fars = [[jnp.zeros((8, SUB), jnp.float32)] * 2 for _ in range(2)]
        dqt = [jnp.zeros((HEAD, QB), jnp.float32)] * 2

        def places(c):
            return pl.ds(pl.multiple_of(i * QB + c * QB, QB), QB)

        def products(c):
            vc = v_ref[places(c), :]
            return [dot(vc, dts[h]) for h in range(2)]

        ahead = products(0)
        for c in range(KB // QB):
            place = places(c)
            dps = ahead
            if c + 1 < KB // QB:
                ahead = products(c + 1)
            grads, weights = [], []
            for h in range(2):
                e = e_ref[0, i, h, c * QB : (c + 1) * QB, :]
                ds = e.astype(jnp.float32) * (dps[h] - deltas[h])
                for a in range(2 * c, 2 * c + 2):
                    for b in range(2):
                        m, kind = block_kind(a, b)
                        x = ds[(a - 2 * c) * SUB : (a - 2 * c + 1) * SUB, b * SUB : (b + 1) * SUB]
                        if abs(m) > 4:
                            continue
                        if kind == "v":
                            acc[h, m + 1] += x
                        else:
                            side = "np".index(kind)
                            fars[h][side] = fars[h][side] + fold8(x, jnp.sum)
                ds = ds.astype(jnp.bfloat16)
                dqt[h] = dqt[h] + dot(kt[h * HEAD : (h + 1) * HEAD, place], ds)
                grads.append(ds)
                weights.append(e)
            dk_acc[place, :] += dot(jnp.concatenate(grads, axis=1), q_both)
            dv_acc[place, :] += dot_nt(jnp.concatenate(weights, axis=1), dt_both)
        dq_ref[rows, :] = jnp.concatenate(dqt, axis=0).T.astype(jnp.bfloat16)
        own = pl.ds(pl.multiple_of(i * QB + HALF, QB), QB)
        dv_acc[own, :] += dctx - kept
        for h in range(2):
            for side in range(2):
                far[h, side] += fars[h][side]
        return 0

    lax.fori_loop(0, steps, block, 0)
    dk_ref[...] = dk_acc[...].astype(jnp.bfloat16)
    dv_ref[...] = dv_acc[...].astype(jnp.bfloat16)
    row_id = lax.broadcasted_iota(jnp.int32, (SUB, SUB), 0)
    col_id = lax.broadcasted_iota(jnp.int32, (SUB, SUB), 1)
    sublane = lax.broadcasted_iota(jnp.int32, (8, SUB), 0)
    for h in range(2):
        sums = []
        for upper in (True, False):
            for m in range(3):
                x = jnp.where((col_id >= row_id) == upper, acc[h, m], 0.0)
                y = x[:8]
                for g in range(1, SUB // 8):
                    y = y + pltpu.roll(x[8 * g : 8 * g + 8], SUB - 8 * g, 1)
                for bit in range(3):
                    y = jnp.where(
                        (sublane >> bit) % 2 == 1, pltpu.roll(y, SUB - (1 << bit), 1), y
                    )
                sums.append(jnp.sum(y, axis=0, keepdims=True))
        for side in range(2):
            sums.append(jnp.sum(far[h, side], axis=0, keepdims=True))
        db_ref[h] = jnp.concatenate(sums, axis=0)


def spec(shape, index):
    return pl.BlockSpec(shape, index)


def attention_forward(queries, keys, values, q_feat, k_feat, live, bias_rows):
    rows, span = queries.shape[0], keys.shape[0]
    steps = rows // QB
    return pl.pallas_call(
        forward_kernel,
        grid=(PAIRS,),
        in_specs=[
            spec((rows, SUB), lambda p: (0, p)),
            spec((span, SUB), lambda p: (0, p)),
            spec((span, SUB), lambda p: (0, p)),
            spec((rows, SUB), lambda p: (0, 0)),
            spec((span, SUB), lambda p: (0, 0)),
            spec((rows, SUB), lambda p: (0, 0)),
            spec((2, 8, 2 * SUB), lambda p: (p, 0, 0)),
        ],
        out_specs=[
            spec((rows, SUB), lambda p: (0, p)),
            spec((1, steps, 2, KB, QB), lambda p: (p, 0, 0, 0, 0)),
            spec((1, steps, 8, QB), lambda p: (p, 0, 0, 0)),
        ],
        out_shape=[
            jax.ShapeDtypeStruct((rows, D), jnp.bfloat16),
            jax.ShapeDtypeStruct((PAIRS, steps, 2, KB, QB), jnp.bfloat16),
            jax.ShapeDtypeStruct((PAIRS, steps, 8, QB), jnp.float32),
        ],
        scratch_shapes=[
            pltpu.VMEM((SUB, span), jnp.bfloat16),
            pltpu.VMEM((2, 3, SUB, SUB), jnp.float32),
            pltpu.VMEM((2, 2, KB, QB), jnp.float32),
            pltpu.VMEM((2, 8, QB), jnp.float32),
        ],
        compiler_params=pltpu.CompilerParams(
            dimension_semantics=("arbitrary",), vmem_limit_bytes=VMEM_LIMIT
        ),
        cost_estimate=pl.CostEstimate(
            flops=4 * rows * KB * D * 4, bytes_accessed=45_000_000, transcendentals=rows * KB * HEADS
        ),
    )(queries, keys, values, q_feat, k_feat, live, bias_rows)


def attention_backward(
    queries, keys, values, live, expo, inverse, context, d_context, first, pairs
):
    rows, span = queries.shape[0], keys.shape[0]
    steps = rows // QB
    return pl.pallas_call(
        backward_kernel,
        grid=(pairs,),
        in_specs=[
            spec((rows, SUB), lambda p: (0, p + first)),
            spec((span, SUB), lambda p: (0, p + first)),
            spec((span, SUB), lambda p: (0, p + first)),
            spec((rows, SUB), lambda p: (0, 0)),
            spec((1, steps, 2, KB, QB), lambda p: (p + first, 0, 0, 0, 0)),
            spec((1, steps, 8, QB), lambda p: (p + first, 0, 0, 0)),
            spec((rows, SUB), lambda p: (0, p + first)),
            spec((rows, SUB), lambda p: (0, p + first)),
        ],
        out_specs=[
            spec((rows, SUB), lambda p: (0, p)),
            spec((span, SUB), lambda p: (0, p)),
            spec((span, SUB), lambda p: (0, p)),
            spec((2, 8, SUB), lambda p: (p, 0, 0)),
        ],
        out_shape=[
            jax.ShapeDtypeStruct((rows, pairs * SUB), jnp.bfloat16),
            jax.ShapeDtypeStruct((span, pairs * SUB), jnp.bfloat16),
            jax.ShapeDtypeStruct((span, pairs * SUB), jnp.bfloat16),
            jax.ShapeDtypeStruct((2 * pairs, 8, SUB), jnp.float32),
        ],
        scratch_shapes=[
            pltpu.VMEM((SUB, span), jnp.bfloat16),
            pltpu.VMEM((span, SUB), jnp.float32),
            pltpu.VMEM((span, SUB), jnp.float32),
            pltpu.VMEM((2, 3, SUB, SUB), jnp.float32),
            pltpu.VMEM((2, 2, 8, SUB), jnp.float32),
        ],
        compiler_params=pltpu.CompilerParams(
            dimension_semantics=("arbitrary",), vmem_limit_bytes=VMEM_LIMIT
        ),
        cost_estimate=pl.CostEstimate(
            flops=8 * rows * KB * pairs * SUB * 4, bytes_accessed=9_000_000 * pairs, transcendentals=0
        ),
    )(queries, keys, values, live, expo, inverse, context, d_context)


FF = 3072
TILE = 768
CHUNK = 768
WTILE = 512
WCHUNK = 256


def gelu_parts(v):
    scale = 0.7978845608
    square = v * v
    t = jnp.tanh(scale * v * (1.0 + 0.044715 * square))
    half = 0.5 * (1.0 + t)
    slope = half + 0.5 * v * (1.0 - t * t) * (scale + (3 * 0.044715 * scale) * square)
    return half * v, slope


def routing(x, router, pick, experts):
    logits = dot(x, router)
    lane = lax.broadcasted_iota(jnp.int32, logits.shape, 1)
    logits = jnp.where(lane < experts, logits, MASKED_SCORE)
    expo = jnp.exp(logits - jnp.max(logits, axis=1, keepdims=True))
    probs = expo / jnp.sum(expo, axis=1, keepdims=True)
    return probs, jnp.sum(probs * pick, axis=1, keepdims=True)


def hidden_pair(x, d_rows, w_in, w_out):
    inner, slope = gelu_parts(dot(x, w_in))
    d_pre = dot_nt(d_rows, w_out) * slope
    return inner.astype(jnp.bfloat16), d_pre.astype(jnp.bfloat16)


def row_chunks(rows, size=QB):
    return [slice(s, min(s + size, rows)) for s in range(0, rows, size)]


def expert_kernel(
    experts,
    x_ref,
    c_ref,
    router_ref,
    pick_ref,
    aux_ref,
    win_ref,
    wout_ref,
    rows_ref,
    back_ref,
    act_ref,
    dpre_ref,
    drows_ref,
    dlog_ref,
    probs,
    rows_acc,
    back_acc,
):
    step = pl.program_id(0)
    pick = pick_ref[0:1, :]

    @pl.when(step == 0)
    def _():
        for r in row_chunks(x_ref.shape[0]):
            p, gate = routing(x_ref[r, :], router_ref[...], pick, experts)
            probs[r, :] = p
            drows_ref[r, :] = (gate * c_ref[r, :].astype(jnp.float32)).astype(jnp.bfloat16)
        rows_acc[...] = jnp.zeros_like(rows_acc)
        back_acc[...] = jnp.zeros_like(back_acc)

    w_in, w_out = win_ref[...], wout_ref[...]
    for r in row_chunks(x_ref.shape[0], CHUNK):
        act, dpre = hidden_pair(x_ref[r, :], drows_ref[r, :], w_in, w_out)
        act_ref[r, :] = act
        dpre_ref[r, :] = dpre
        rows_acc[r, :] += dot(act, w_out)
        back_acc[r, :] += dot_nt(dpre, w_in)

    @pl.when(step == pl.num_programs(0) - 1)
    def _():
        for r in row_chunks(x_ref.shape[0]):
            rows = rows_acc[r, :].astype(jnp.bfloat16)
            rows_ref[r, :] = rows
            d_gate = jnp.sum(
                c_ref[r, :].astype(jnp.float32) * rows.astype(jnp.float32), axis=1, keepdims=True
            )
            p = probs[r, :]
            d_probs = pick * d_gate + aux_ref[0:1, :]
            d_log = p * (d_probs - jnp.sum(d_probs * p, axis=1, keepdims=True))
            d_log = d_log.astype(jnp.bfloat16)
            dlog_ref[r, :] = d_log
            back = back_acc[r, :].astype(jnp.bfloat16).astype(jnp.float32)
            back_ref[r, :] = (back + dot_nt(d_log, router_ref[...])).astype(jnp.bfloat16)


def whole(shape):
    return pl.BlockSpec(shape, lambda t: (0,) * len(shape))


def expert_pass(x, cot, router, pick, aux, w_in, w_out, experts):
    rows = x.shape[0]
    wide = jax.ShapeDtypeStruct((rows, FF), jnp.bfloat16)
    narrow = jax.ShapeDtypeStruct((rows, D), jnp.bfloat16)
    return pl.pallas_call(
        functools.partial(expert_kernel, experts),
        grid=(FF // TILE,),
        in_specs=[
            whole((rows, D)),
            whole((rows, D)),
            whole((D, SUB)),
            whole((8, SUB)),
            whole((8, SUB)),
            pl.BlockSpec((D, TILE), lambda t: (0, t)),
            pl.BlockSpec((TILE, D), lambda t: (t, 0)),
        ],
        out_specs=[
            whole((rows, D)),
            whole((rows, D)),
            pl.BlockSpec((rows, TILE), lambda t: (0, t)),
            pl.BlockSpec((rows, TILE), lambda t: (0, t)),
            whole((rows, D)),
            whole((rows, SUB)),
        ],
        out_shape=[narrow, narrow, wide, wide, narrow, jax.ShapeDtypeStruct((rows, SUB), jnp.bfloat16)],
        scratch_shapes=[
            pltpu.VMEM((rows, SUB), jnp.float32),
            pltpu.VMEM((rows, D), jnp.float32),
            pltpu.VMEM((rows, D), jnp.float32),
        ],
        compiler_params=pltpu.CompilerParams(
            dimension_semantics=("arbitrary",), vmem_limit_bytes=VMEM_LIMIT
        ),
        cost_estimate=pl.CostEstimate(
            flops=8 * rows * D * FF, bytes_accessed=30_000_000, transcendentals=rows * FF
        ),
    )(x, cot, router, pick, aux, w_in, w_out)


def transposed(target, source, place):
    for r in row_chunks(source.shape[0]):
        at = pl.multiple_of(place + r.start, QB)
        target[:, pl.ds(at, QB)] = source[r, :].T


def hidden_kernel(experts, x_ref, c_ref, router_ref, pick_ref, win_ref, wout_ref, act_ref, dpre_ref, drows_ref):
    @pl.when(pl.program_id(0) == 0)
    def _():
        for r in row_chunks(x_ref.shape[0]):
            _, gate = routing(x_ref[r, :], router_ref[...], pick_ref[0:1, :], experts)
            drows_ref[r, :] = (gate * c_ref[r, :].astype(jnp.float32)).astype(jnp.bfloat16)

    act, dpre = hidden_pair(x_ref[...], drows_ref[...], win_ref[...], wout_ref[...])
    act_ref[...] = act
    dpre_ref[...] = dpre


def hidden_pass(x, cot, router, pick, w_in, w_out, experts):
    rows = x.shape[0]
    wide = jax.ShapeDtypeStruct((rows, FF), jnp.bfloat16)
    wide_spec = pl.BlockSpec((rows, TILE), lambda t: (0, t))
    return pl.pallas_call(
        functools.partial(hidden_kernel, experts),
        grid=(FF // TILE,),
        in_specs=[
            whole((rows, D)),
            whole((rows, D)),
            whole((D, SUB)),
            whole((8, SUB)),
            pl.BlockSpec((D, TILE), lambda t: (0, t)),
            pl.BlockSpec((TILE, D), lambda t: (t, 0)),
        ],
        out_specs=[wide_spec, wide_spec, whole((rows, D))],
        out_shape=[wide, wide, jax.ShapeDtypeStruct((rows, D), jnp.bfloat16)],
        compiler_params=pltpu.CompilerParams(
            dimension_semantics=("arbitrary",), vmem_limit_bytes=VMEM_LIMIT
        ),
        cost_estimate=pl.CostEstimate(
            flops=4 * rows * D * FF, bytes_accessed=30_000_000, transcendentals=rows * FF
        ),
    )(x, cot, router, pick, w_in, w_out)


def weight_kernel(parts, more_ref, *refs):
    x_refs, drows_refs, act_refs, dpre_refs = (refs[k * parts : (k + 1) * parts] for k in range(4))
    din_old, dout_old, din_ref, dout_ref, xt, d_rows, act_t, dpres = refs[4 * parts :]
    sizes = [x.shape[0] for x in x_refs]
    starts = [sum(sizes[:k]) for k in range(parts)]

    @pl.when(pl.program_id(0) == 0)
    def _():
        for k in range(parts):
            transposed(xt, x_refs[k], starts[k])
            d_rows[starts[k] : starts[k] + sizes[k], :] = drows_refs[k][...]

    for k in range(parts):
        transposed(act_t, act_refs[k], starts[k])
        dpres[starts[k] : starts[k] + sizes[k], :] = dpre_refs[k][...]
    din_ref[...] = dot(xt[...], dpres[...])
    dout_ref[...] = dot(act_t[...], d_rows[...])

    @pl.when(more_ref[0] > 0)
    def _():
        din_ref[...] = din_ref[...] + din_old[...]
        dout_ref[...] = dout_ref[...] + dout_old[...]


def weight_pass(rows_of, old, more):
    sizes = [x.shape[0] for x in rows_of[0]]
    total = sum(sizes)
    narrow = [pl.BlockSpec((rows, D), lambda t, m: (0, 0)) for rows in sizes]
    wide = [pl.BlockSpec((rows, WTILE), lambda t, m: (0, t)) for rows in sizes]
    old_specs = [
        pl.BlockSpec((D, WTILE), lambda t, m: (0, t * m[0])),
        pl.BlockSpec((WTILE, D), lambda t, m: (t * m[0], 0)),
    ]
    new_specs = [
        pl.BlockSpec((D, WTILE), lambda t, m: (0, t)),
        pl.BlockSpec((WTILE, D), lambda t, m: (t, 0)),
    ]
    return pl.pallas_call(
        functools.partial(weight_kernel, len(sizes)),
        grid_spec=pltpu.PrefetchScalarGridSpec(
            num_scalar_prefetch=1,
            grid=(FF // WTILE,),
            in_specs=narrow * 2 + wide * 2 + old_specs,
            out_specs=new_specs,
            scratch_shapes=[
                pltpu.VMEM((D, total), jnp.bfloat16),
                pltpu.VMEM((total, D), jnp.bfloat16),
                pltpu.VMEM((WTILE, total), jnp.bfloat16),
                pltpu.VMEM((total, WTILE), jnp.bfloat16),
            ],
        ),
        out_shape=[
            jax.ShapeDtypeStruct((D, FF), jnp.float32),
            jax.ShapeDtypeStruct((FF, D), jnp.float32),
        ],
        compiler_params=pltpu.CompilerParams(
            dimension_semantics=("arbitrary",), vmem_limit_bytes=VMEM_LIMIT
        ),
        cost_estimate=pl.CostEstimate(
            flops=4 * total * D * FF, bytes_accessed=50_000_000, transcendentals=0
        ),
    )(jnp.full((1,), more, jnp.int32), *[array for group in rows_of for array in group], *old)


EPSILON = 1e-06
AUX_WEIGHT = 0.01
PRECISE = lax.Precision.HIGHEST
GROUP = ("shard", "seq")
EVERY = ("rep", "shard", "seq")


def exchange(x, axis, hop):
    count = lax.axis_size(axis)
    return lax.ppermute(x, axis, [(i, i ^ hop) for i in range(count)])


def bits_of(axis):
    return lax.axis_size(axis).bit_length() - 1


def bit_at(axis, bit):
    return (lax.axis_index(axis) >> bit) & 1


def both_halves(x, axis, bit, dim):
    other = exchange(x, axis, 1 << bit)
    size = x.shape[dim]
    rec = jnp.concatenate([other, x, other], axis=dim)
    return lax.dynamic_slice_in_dim(rec, (1 - bit_at(axis, bit)) * size, 2 * size, axis=dim)


def all_blocks(x, axis, dim):
    count = lax.axis_size(axis)
    size = x.shape[dim]
    turned = [
        lax.ppermute(x, axis, [(i, (i + k) % count) for i in range(count)])
        for k in range(count - 1, 0, -1)
    ]
    rec = jnp.concatenate(turned + [x] + turned, axis=dim)
    start = (count - 1 - lax.axis_index(axis)) * size
    return lax.dynamic_slice_in_dim(rec, start, count * size, axis=dim)


def gather_rows(parts, meanwhile):
    seq_bits = bits_of("seq")
    near = list(range(seq_bits - 1, 0, -1))
    state = [x.reshape((1,) * (1 + seq_bits) + x.shape) for x in parts]
    for hop in range(seq_bits + 1):
        if hop == 1:
            *state, meanwhile = together(*state, meanwhile)
        for turn, y in enumerate(state):
            what = (["shard"] + near + [0] if turn % 2 == 0 else near + ["shard", 0])[hop]
            if what == "shard":
                state[turn] = all_blocks(y, "shard", 0)
            else:
                state[turn] = both_halves(y, "seq", what, seq_bits - what)
    return [y.reshape(-1, y.shape[-1]) for y in state], meanwhile


def half_kept(x, axis, bit, dim):
    low = lax.index_in_dim(x, 0, dim)
    high = lax.index_in_dim(x, 1, dim)
    mine = bit_at(axis, bit) == 1
    got = exchange(jnp.where(mine, low, high), axis, 1 << bit)
    kept = jnp.where(mine, high, low)
    return (kept.astype(jnp.float32) + got.astype(jnp.float32)).astype(jnp.bfloat16)


def rep_sums(y):
    total = y.astype(jnp.float32)
    for bit in range(bits_of("rep")):
        y = total.astype(jnp.bfloat16)
        total = y.astype(jnp.float32) + exchange(y, "rep", 1 << bit).astype(jnp.float32)
    return total


def blocks_of(x):
    bits = bits_of("shard") + bits_of("seq")
    return x.reshape((2,) * bits + (x.shape[0] >> bits, x.shape[1]))


def scatter_hop(state, hop):
    seq_bits, shard_bits = bits_of("seq"), bits_of("shard")
    far = [("shard", b) for b in range(shard_bits - 1, -1, -1)]
    near = [("seq", b) for b in range(seq_bits - 1, 0, -1)]
    out = []
    for turn, x in enumerate(state):
        axis, bit = ([("seq", 0)] + (near + far if turn % 2 == 0 else far + near))[hop]
        dim = shard_bits - 1 - bit if axis == "shard" else shard_bits + seq_bits - 1 - bit
        out.append(half_kept(x, axis, bit, dim))
    return out


def sum_everywhere(x):
    for axis in ("seq", "shard", "rep"):
        for bit in range(bits_of(axis)):
            x = x + exchange(x, axis, 1 << bit)
    return x


def together(*values):
    return lax.optimization_barrier(values)


def rms_norm(vectors, gains):
    return (
        vectors * lax.rsqrt(jnp.mean(vectors * vectors, axis=-1, keepdims=True) + EPSILON) * gains
    )


def dot_tn(a, b):
    return lax.dot_general(a, b, (((0,), (0,)), ((), ())), preferred_element_type=jnp.float32)


def wide_row(values):
    row = jnp.pad(values.astype(jnp.float32), (0, SUB - values.shape[0]))
    return jnp.broadcast_to(row[None, :], (8, SUB))


def routed_across(x):
    return lax.all_to_all(x, GROUP, split_axis=0, concat_axis=0, tiled=True)


def prepare_kernel(experts, capacity, parts, len_ref, first_ref, ids_ref, cot_ref, *refs):
    qf_ref, kf_ref, live_ref = refs[:3]
    hot_refs, sent_refs = refs[3 : 3 + len(parts)], refs[3 + len(parts) :]
    ends = [len_ref[0, 0]]
    for d in range(1, DOCS):
        ends.append(ends[-1] + len_ref[0, d])
    first = first_ref[0]
    rows, span = qf_ref.shape[0], kf_ref.shape[0]

    def doc_of(places):
        return sum((places >= end).astype(jnp.int32) for end in ends)

    places = first + lax.broadcasted_iota(jnp.int32, (rows, SUB), 0)
    lane = lax.broadcasted_iota(jnp.int32, (rows, SUB), 1)
    hit = (doc_of(places) == lane) & (lane < DOCS)
    qf_ref[...] = jnp.where(hit, 1.0, 0.0).astype(jnp.bfloat16)
    live_ref[...] = jnp.where(places < ends[-1], 1.0, 0.0).astype(jnp.bfloat16)
    places = first - HALF + lax.broadcasted_iota(jnp.int32, (span, SUB), 0)
    lane = lax.broadcasted_iota(jnp.int32, (span, SUB), 1)
    hit = (doc_of(places) == lane) & (places >= 0) & (places < ends[-1])
    kf_ref[...] = jnp.where((lane < DOCS) & ~hit, MASKED_SCORE, 0.0).astype(jnp.bfloat16)

    live = first + lax.broadcasted_iota(jnp.int32, (1, rows), 1) < ends[-1]
    expert = lax.broadcasted_iota(jnp.int32, (experts, rows), 0)
    chosen = jnp.where((ids_ref[...] == expert) & live, 1.0, 0.0)
    before = lax.broadcasted_iota(jnp.int32, (rows, rows), 0)
    upto = before <= lax.broadcasted_iota(jnp.int32, (rows, rows), 1)
    ranked = dot(chosen.astype(jnp.bfloat16), jnp.where(upto, 1.0, 0.0).astype(jnp.bfloat16))
    slot = chosen * (ranked - 1.0 + capacity * expert.astype(jnp.float32))
    slot = jnp.where(live, jnp.sum(slot, axis=0, keepdims=True), -1.0)
    for (start, stop), hot_ref, sent_ref in zip(parts, hot_refs, sent_refs):
        size = stop - start
        for r in row_chunks(hot_ref.shape[0]):
            shape = (r.stop - r.start, rows)
            place = (r.start + lax.broadcasted_iota(jnp.int32, shape, 0)).astype(jnp.float32)
            owner = jnp.floor((place + 0.5) * (1.0 / size))
            held = owner * capacity + start + (place - owner * size)
            hot = jnp.where(slot == held, 1.0, 0.0).astype(jnp.bfloat16)
            hot_ref[r, :] = hot
            sent_ref[r, :] = dot(hot, cot_ref[...]).astype(jnp.bfloat16)


def prepare(doc_lengths, first_place, expert_ids, cotangent, experts, capacity, parts):
    rows = cotangent.shape[0]
    span = rows + 2 * HALF
    sizes = [experts * (stop - start) for start, stop in parts]
    narrow = lambda n: jax.ShapeDtypeStruct((n, SUB), jnp.bfloat16)
    smem = pl.BlockSpec(memory_space=pltpu.SMEM)
    vmem = pl.BlockSpec(memory_space=pltpu.VMEM)
    out = pl.pallas_call(
        functools.partial(prepare_kernel, experts, capacity, parts),
        in_specs=[smem, smem, vmem, vmem],
        out_specs=[vmem] * (3 + 2 * len(parts)),
        out_shape=[narrow(rows), narrow(span), narrow(rows)]
        + [jax.ShapeDtypeStruct((size, rows), jnp.bfloat16) for size in sizes]
        + [jax.ShapeDtypeStruct((size, D), jnp.bfloat16) for size in sizes],
        compiler_params=pltpu.CompilerParams(vmem_limit_bytes=VMEM_LIMIT),
        cost_estimate=pl.CostEstimate(
            flops=2 * sum(sizes) * rows * D, bytes_accessed=8_000_000, transcendentals=0
        ),
    )(doc_lengths, first_place.reshape(1), expert_ids.reshape(1, rows), cotangent)
    return *out[:3], out[3 : 3 + len(parts)], out[3 + len(parts) :]


def shards(
    tokens,
    doc_lengths,
    expert_ids,
    cotangent,
    gain_attn,
    gain_ffn,
    w_query,
    w_key,
    w_value,
    w_attn_out,
    rel_table,
    w_router,
    w_expert_in,
    w_expert_out,
):
    rows = tokens.shape[0]
    seq_count = lax.axis_size("seq")
    rep_count = lax.axis_size("rep")
    experts = lax.axis_size(GROUP)
    all_devices = lax.axis_size(EVERY)
    capacity = 5 * rows // (4 * experts)
    slots = experts * capacity
    shard_rows = w_query.shape[0]
    table_rows = rel_table.shape[0]
    w_in, w_out = w_expert_in[0], w_expert_out[0]

    def across(values):
        return routed_across(values.reshape(experts, -1, D)).reshape(-1, D)

    def collected(pieces):
        return sum(dot_tn(hot, piece) for hot, piece in zip(hots, pieces))

    def joined(pieces):
        return jnp.concatenate([p.reshape(experts, -1, D) for p in pieces], axis=1).reshape(slots, D)

    def split(values):
        values = values.reshape(experts, capacity, D)
        return [values[:, start:stop].reshape(-1, D) for start, stop in parts]

    few = capacity // 2 // 16 * 16
    parts = [(0, few), (few, capacity)] if few else [(0, capacity)]
    first_place = lax.axis_index("seq") * rows
    q_feat, k_feat, live, hots, cot_sent = prepare(
        doc_lengths, first_place, expert_ids, cotangent, experts, capacity, parts
    )
    is_live = first_place + jnp.arange(rows, dtype=jnp.int32) < jnp.sum(doc_lengths)
    chosen = (expert_ids == jnp.arange(experts, dtype=jnp.int32)[None, :]) & is_live[:, None]
    is_live, chosen_f = is_live.astype(jnp.float32)[:, None], chosen.astype(jnp.float32)
    counts = jnp.sum(chosen_f, axis=0)

    up = [(i, i + 1) for i in range(seq_count - 1)]
    down = [(i + 1, i) for i in range(seq_count - 1)]
    token_span = jnp.concatenate(
        [lax.ppermute(tokens[rows - HALF :], "seq", up), tokens, lax.ppermute(tokens[:HALF], "seq", down)],
        axis=0,
    )
    small = jnp.concatenate(
        [
            w_router,
            gain_attn[:, None],
            gain_ffn[:, None],
            jnp.pad(rel_table, ((0, shard_rows - table_rows), (0, 0))),
            jnp.broadcast_to(counts.astype(jnp.bfloat16)[None, :], (shard_rows, experts)),
        ],
        axis=1,
    )
    small = jnp.pad(small, ((0, 0), (0, SUB - small.shape[1])))
    (w_q, w_k, w_v), cot_sent = gather_rows(
        [jnp.concatenate([w_query, small], axis=1), w_key, w_value], joined(cot_sent)
    )
    w_q, extra = w_q[:, :D], w_q[:, D:]
    router = extra[:, :experts]
    router_wide = jnp.pad(router, ((0, 0), (0, SUB - experts)))
    g_attn = extra[:, experts].astype(jnp.float32)
    g_ffn = extra[:, experts + 1].astype(jnp.float32)
    blocks = extra.reshape(experts, shard_rows, SUB)
    table = blocks[:, :table_rows, experts + 2 : experts + 2 + HEADS]
    table = table.reshape(BUCKETS, HEADS).astype(jnp.float32)
    counts_at = experts + 2 + HEADS
    counts_all = jnp.sum(blocks[:, 0, counts_at : counts_at + experts].astype(jnp.float32), axis=0)
    for bit in range(bits_of("rep")):
        counts_all = counts_all + exchange(counts_all, "rep", 1 << bit)
    live_all = jnp.sum(counts_all)
    shares = counts_all / live_all
    me = lax.axis_index(GROUP)
    pick = wide_row(jnp.arange(experts) == me)
    aux = wide_row((AUX_WEIGHT * experts / live_all) * shares)

    w_attn_out, cot_sent, w_q, w_k, w_v = together(w_attn_out, cot_sent, w_q, w_k, w_v)
    w_proj = lax.all_gather(w_attn_out, GROUP, axis=0, tiled=True)
    cot_rows = across(cot_sent)

    inputs = tokens.astype(jnp.float32)
    normed_span = rms_norm(token_span.astype(jnp.float32), g_attn).astype(jnp.bfloat16)
    normed_one = normed_span[HALF : HALF + rows]
    queries = dot(normed_one, w_q).astype(jnp.bfloat16)
    keys = dot(normed_span, w_k).astype(jnp.bfloat16)
    values = dot(normed_span, w_v).astype(jnp.bfloat16)
    bias_rows = jnp.einsum("rxb,bh->hrx", one_hot(bias_buckets()), table, precision=PRECISE)
    context, expo, inverse = attention_forward(queries, keys, values, q_feat, k_feat, live, bias_rows)
    hidden_state = inputs + dot(context, w_proj)

    ffn_normed, ffn_pull = jax.vjp(rms_norm, hidden_state, g_ffn)
    normed_two = ffn_normed.astype(jnp.bfloat16)
    x_sent = [dot(hot, normed_two).astype(jnp.bfloat16) for hot in hots]
    x_sent[0], cot_rows = together(x_sent[0], cot_rows)
    x_parts = []
    for sent in x_sent:
        if x_parts:
            sent, x_parts[-1] = together(sent, x_parts[-1])
        x_parts.append(across(sent))
    cot_parts = split(cot_rows)
    if rep_count == 2:
        cot_other = exchange(cot_rows, "rep", 1)
        x_other = [exchange(x, "rep", 1) for x in x_parts]
        x_parts[0], x_other[0] = together(x_parts[0], x_other[0])
    done = []
    for x, c in zip(x_parts, cot_parts):
        done.append(expert_pass(x, c, router_wide, pick, aux, w_in, w_out, experts))
    out_parts, back_parts, acts, d_pres, d_row_parts, d_logit_parts = zip(*done)
    blank = [jnp.zeros(shape, jnp.float32) for shape in ((D, WTILE), (WTILE, D))]
    d_expert = weight_pass((x_parts, d_row_parts, acts, d_pres), blank, 0)
    back_all = across(joined(back_parts))
    if rep_count == 2:
        hidden = []
        for x, c in zip(x_other, split(cot_other)):
            hidden += hidden_pass(x, c, router_wide, pick, w_in, w_out, experts)
        back_all, *rest = together(back_all, *d_expert, *hidden)
        d_expert, hidden = rest[:2], rest[2:]
    d_normed_two = collected(split(back_all))
    d_normed_two, *out_parts = together(d_normed_two, *out_parts)
    out_all = across(joined(out_parts))
    d_router = sum(dot_tn(x, d) for x, d in zip(x_parts, d_logit_parts))[:, :experts]

    router_probs = jax.nn.softmax(dot(normed_two, router), axis=-1)
    gating = jnp.sum(router_probs * chosen_f, axis=1)
    hidden_back, d_gain_ffn = ffn_pull(d_normed_two)
    d_hidden = cotangent.astype(jnp.float32) + hidden_back
    d_attn = d_hidden.astype(jnp.bfloat16)
    d_context = dot_nt(d_attn, w_proj).astype(jnp.bfloat16)
    d_attn_out = dot_tn(context, d_attn)
    more = jnp.concatenate([d_router, d_gain_ffn[:, None]], axis=1)
    more = jnp.pad(more, ((0, 0), (0, SUB - more.shape[1])))

    d_q, d_k, d_v, d_bias = attention_backward(
        queries, keys, values, live, expo, inverse, context, d_context, 0, PAIRS
    )
    d_q, d_k, d_v, out_all = together(d_q, d_k, d_v, out_all)
    d_table = jnp.einsum("hrx,rxb->bh", d_bias, one_hot(grad_buckets()), precision=PRECISE)
    d_table = jnp.pad(
        d_table.reshape(experts, table_rows, HEADS), ((0, 0), (0, shard_rows - table_rows), (0, 0))
    ).reshape(D, HEADS)
    more = jnp.concatenate([d_router, d_gain_ffn[:, None], d_table], axis=1)
    more = jnp.pad(more, ((0, 0), (0, SUB - more.shape[1])))
    d_query, d_key, d_value = (
        dot_tn(n, d) for n, d in ((normed_one, d_q), (normed_span, d_k), (normed_span, d_v))
    )
    grads = [
        jnp.concatenate([g.astype(jnp.bfloat16) for g in pair], axis=1)
        for pair in ((d_query, d_attn_out, more), (d_key, d_value))
    ]
    mass = jnp.sum(router_probs * is_live, axis=0)
    mass, *grads = together(mass, *grads)
    mass_all = sum_everywhere(mass)
    grads = [blocks_of(g) for g in grads]
    for hop in range(bits_of("shard") + bits_of("seq")):
        grads = scatter_hop(grads, hop)
        if hop == 0 and rep_count == 2:
            *grads, x_other[0] = together(*grads, x_other[0])
            rows_other = (x_other, hidden[2::3], hidden[0::3], hidden[1::3])
            d_expert = weight_pass(rows_other, d_expert, 1)
        if hop == 1:
            *grads, d_q, d_k, d_v = together(*grads, d_q, d_k, d_v)
        if hop == 2:
            *grads, out_all = together(*grads, out_all)
    d_span = dot_nt(d_k, w_k) + dot_nt(d_v, w_v)
    d_own = d_span[HALF : HALF + rows] + dot_nt(d_q, w_q)
    from_above = lax.ppermute(d_span[:HALF].astype(jnp.bfloat16), "seq", down)
    from_below = lax.ppermute(d_span[HALF + rows :].astype(jnp.bfloat16), "seq", up)
    if rep_count != 2:
        d_expert = [
            lax.psum(g.astype(jnp.bfloat16), "rep").astype(jnp.float32) for g in d_expert
        ]
    left, right = (rep_sums(g.reshape(shard_rows, -1)) for g in grads)
    d_query, d_attn_out, more = left[:, :D], left[:, D : 2 * D], left[:, 2 * D :]
    d_key, d_value = right[:, :D], right[:, D:]
    d_gain_attn = sum(
        jnp.sum(g * w.astype(jnp.float32), axis=1)
        for g, w in ((d_query, w_query), (d_key, w_key), (d_value, w_value))
    ) / gain_attn.astype(jnp.float32)
    balance = experts * jnp.sum(shares * mass_all) / live_all
    importance = experts * mass_all / (rows * all_devices)
    expert_rows = collected(split(out_all))
    mixed = (hidden_state + gating[:, None] * expert_rows).astype(jnp.bfloat16)
    gap = jnp.zeros((rows - HALF, D), jnp.float32)
    d_normed_one = (
        d_own
        + jnp.concatenate([from_below.astype(jnp.float32), gap], axis=0)
        + jnp.concatenate([gap, from_above.astype(jnp.float32)], axis=0)
    )
    _, attn_pull = jax.vjp(lambda v: rms_norm(v, g_attn), inputs)
    d_tokens = d_hidden + attn_pull(d_normed_one)[0]
    return (
        mixed,
        balance,
        importance,
        d_tokens,
        d_gain_attn,
        more[:, experts],
        d_query,
        d_key,
        d_value,
        d_attn_out,
        more[:table_rows, experts + 1 : experts + 1 + HEADS],
        more[:, :experts],
        d_expert[0][None],
        d_expert[1][None],
    )


def solution(mesh):
    split = P(EVERY, None)
    shared = P(GROUP, None)
    gains = P(GROUP)
    stacked = P(GROUP, None, None)
    weights = (shared,) * 6 + (stacked,) * 2
    return jax.shard_map(
        shards,
        mesh=mesh,
        in_specs=(split, P(("rep", "shard"), None), split, split, gains, gains) + weights,
        out_specs=(split, P(), P(), split, gains, gains) + weights,
        check_vma=False,
    )
```

time: 689 us -> 551 us (0.80)
  waiting for transfers between devices: 180 us -> 75.1 us
  starting transfers between devices: 105 us -> 76.8 us
  Pallas kernels: 223 us -> 200 us
  between operations: 6.1 us -> 18.9 us
  local copies, waits for them, and re-layouts: 51.2 us -> 58.3 us
    ppermute x55 -> x25, waiting for transfers between devices: 131 us -> 44.1 us  [exchange(): return lax.ppermute(x, axis, [(i, i ^ hop) for i in range(count)])]
    ppermute x12 -> x9, waiting for transfers between devices: 49.3 us -> 8.54 us  [all_blocks(): lax.ppermute(x, axis, [(i, (i + k) % count) for i in range(count)])]
    ppermute x55 -> x25, starting transfers between devices: 56.5 us -> 26.8 us  [exchange(): return lax.ppermute(x, axis, [(i, i ^ hop) for i in range(count)])]
    pallas_call x4 -> x7, Pallas kernels: 178 us -> 159 us  [the longest x2 48.2 us: weight_pass(): pl.pallas_call(functools.partial(weight_kernel, len(sizes)), grid_spec=pl...]
    all_to_all x4 -> x5, waiting for transfers between devices: 0.01 us -> 14.4 us  [routed_across(): return lax.all_to_all(x, GROUP, split_axis=0, concat_axis=0, tiled=True)]
    dynamic_slice x28 -> x0, local copies, waits for them, and re-layouts: 10.1 us -> none  [half_kept(): sent = lax.dynamic_slice_in_dim(x, (1 - mine) * size, size, axis=dim)]
    ppermute x12 -> x9, starting transfers between devices: 22.1 us -> 12.1 us  [all_blocks(): lax.ppermute(x, axis, [(i, (i + k) % count) for i in range(count)])]
    slice x18 -> x16, local copies, waits for them, and re-layouts: 9.78 us -> 19.1 us  [the longest x8 14.3 us: split(): return [values[:, start:stop].reshape(-1, D) for start, stop in parts]]
  transfers between devices with their start and end apart: 75 -> 44, of which waited for: 28 -> 15; matrix products, arithmetic and copies ran while one was open for 22% -> 21% of each run, Pallas kernels for 33% -> 37%
where the time goes in v2:
time: 551 us; the launch traced here: 541 us
  Pallas kernels  200 us (36%)
  starting transfers between devices  76.8 us (14%)
  waiting for transfers between devices  75.1 us (14%)
  matrix products  62.8 us (11%)
  local copies, waits for them, and re-layouts  58.3 us (11%)
  other arithmetic  49 us (9%)
  between operations  18.9 us (3%)
    pallas_call x2, Pallas kernels, weight_pass(): pl.pallas_call(functools.partial(weight_kernel, len(sizes)), grid_spec=pl...  48.2 us
    pallas_call x1, Pallas kernels, attention_backward(): pl.pallas_call(backward_kernel, grid=(pairs,), in_specs=[spec((rows, SUB)...  45.4 us
    ppermute x25, waiting for transfers between devices, exchange(): return lax.ppermute(x, axis, [(i, i ^ hop) for i in range(count)])  44.1 us
    pallas_call x2, Pallas kernels, expert_pass(): pl.pallas_call(functools.partial(expert_kernel, experts), grid=(FF // TIL...  40.6 us
    pallas_call x1, Pallas kernels, attention_forward(): pl.pallas_call(forward_kernel, grid=(PAIRS,), in_specs=[spec((rows, SUB),...  35.3 us
    all_to_all x5, starting transfers between devices, routed_across(): return lax.all_to_all(x, GROUP, split_axis=0, concat_axis=0, tiled=True)  28.1 us
    ppermute x25, starting transfers between devices, exchange(): return lax.ppermute(x, axis, [(i, i ^ hop) for i in range(count)])  26.8 us
    pallas_call x2, Pallas kernels, hidden_pass(): pl.pallas_call(functools.partial(hidden_kernel, experts), grid=(FF // TIL...  24.5 us
  transfers between devices with their start and end apart: 44, of which 15 were waited for; matrix products, arithmetic and copies ran while one was open for 21% of the time, Pallas kernels for 37%

profile of v2, /device:TPU:0, one launch (start us, length us, event | category | flops | bytes accessed | tf_op | source)
XLA Modules:
  0.0 540.8 jit_solution(4909689064869143933)
XLA Ops:
  13.4 5.0 collective-permute-start.2
  19.5 2.8 collective-permute-start.6
  23.4 6.0 %shard_map.263 = (bf16[1024,128]{1,0:T(8,128)(2,1)}, bf16[2048,128]{1,0:T(8,128)(2,1)}, bf16[1024,128]{1,0:T(8,128)(2,1)}, bf16[512,1024]{1,0:T(8,128)(2,1)}, bf...) custom-call(s32[1,4]{1,0:T(1,128)} %len_ref.1, s32[1]{0:T(128)} %bitcast.6.first_ref, ...), custom_call_target="tpu_custom_call" | custom-call | flops 2013265920 | bytes 8000000 | tf_op jit(solution)/shard_map/pallas_call | solution.py:840
  29.4 2.9 pad_maximum_fusion.3
  34.1 4.5 collective-permute-done.8
  44.2 3.1 collective-permute-start
  53.7 4.0 collective-permute-done.13
  60.7 9.5 %collective-permute-done.15 = bf16[4,1,1,48,768]{4,3,2,1,0:T(8,128)(2,1)S(1)} collective-permute-done((bf16[4,1,1,48,768]{4,3,2,1,0:T(8,128)(2,1)}, bf16[4,1,1,48,768]{4,3,2,1,0:T(8,128)(2,1)S(1)}, u32[]{:S(2)}, u32[]{:S(2)}) %collective-permute-start.15) | collective-permute-done | bytes 294944 | tf_op jit(solution)/shard_map/ppermute | solution.py:681
  78.5 6.1 %all-to-all-start = ((bf16[16,80,768]{2,1,0:T(8,128)(2,1)}), bf16[16,80,768]{2,1,0:T(8,128)(2,1)}, u32[]{:S(2)}, u32[]{:S(2)}) async-start(bf16[16,80,768]{2,1,0:T(8,128)(2,1)} %pad_maximum_fusion.3), calls=%async_computation | async-start | bytes 3932160 | tf_op jit(solution)/shard_map/all_to_all | solution.py:788
  84.8 3.3 fusion.2
  88.1 4.0 convolution_convert_fusion.1.k_ref
  95.7 6.1 %convolution_convert_fusion.v_ref = bf16[2048,768]{1,0:T(8,128)(2,1)} fusion(bf16[2048,768]{1,0:T(8,128)(2,1)} %copy-done.17, bf16[768,768]{1,0:T(8,128)(2,1)S(1)} %bitcast.117), kind=kOutput, calls=%fused_computation.12 | convolution fusion | flops 2417491968 | bytes 7471104 | tf_op jit(solution)/shard_map/dot_general | solution.py:85
  101.9 35.3 %shard_map.264 = (bf16[1024,768]{1,0:T(8,128)(2,1)}, bf16[6,4,2,1280,256]{4,3,2,1,0:T(8,128)(2,1)}, f32[6,4,8,256]{3,2,1,0:T(8,128)}) custom-call(bf16[1024,768]{1,0:T(8,128)(2,1)} %convolution_convert_fusion.3.q_ref, bf16[2048,768]{1,0:T(8,128)(2,1)} %convolution_convert_fusion.1.k_ref, bf16[2048,768]{1,0:T(8,128)(2,1)} %convolution_convert_fusion.v_ref, ...), custom_call_target="tpu_custom_call" | custom-call | flops 16106127360 | bytes 45000000 | tf_op jit(solution)/shard_map/pallas_call | solution.py:347
  137.1 8.0 %all-gather.2.cloned.1.call-done = bf16[768,768]{1,0:T(8,128)(2,1)} async-done(((bf16[48,768]{1,0:T(8,128)(2,1)}), bf16[768,768]{1,0:T(8,128)(2,1)}) %all-gather.2.cloned.1.call-update) | async-done | bytes 1179664 | tf_op jit(solution)/shard_map/all_gather | solution.py:945
  145.1 3.8 multiply_reduce_fusion.2
  152.4 4.5 all-to-all-start.1
  156.9 4.3 convolution_convert_fusion.8
  161.2 14.4 %all-to-all-done.1 = bf16[16,32,768]{2,1,0:T(8,128)(2,1)} async-done(((bf16[16,32,768]{2,1,0:T(8,128)(2,1)}), bf16[16,32,768]{2,1,0:T(8,128)(2,1)}, u32[]{:S(2)}, u32[]{:S(2)}) %all-to-all-start.1) | async-done | bytes 786464 | tf_op jit(solution)/shard_map/all_to_all | solution.py:788
  175.6 5.5 %all-to-all-start.2 = ((bf16[16,48,768]{2,1,0:T(8,128)(2,1)}), bf16[16,48,768]{2,1,0:T(8,128)(2,1)}, u32[]{:S(2)}, u32[]{:S(2)}) async-start(bf16[16,48,768]{2,1,0:T(8,128)(2,1)} %bitcast.123), calls=%async_computation.2 | async-start | bytes 2359296 | tf_op jit(solution)/shard_map/all_to_all | solution.py:788
  185.0 16.2 %collective-permute-done.18 = f32[16]{0:T(128)S(1)} collective-permute-done((f32[16]{0:T(128)S(1)}, f32[16]{0:T(128)S(1)}, u32[]{:S(2)}, u32[]{:S(2)}) %collective-permute-start.18) | collective-permute-done | bytes 96 | tf_op jit(solution)/shard_map/ppermute | solution.py:681
  210.3 17.0 %shard_map.265 = (bf16[512,768]{1,0:T(8,128)(2,1)}, bf16[512,768]{1,0:T(8,128)(2,1)}, bf16[512,3072]{1,0:T(8,128)(2,1)}, bf16[512,3072]{1,0:T(8,128)(2,1)}, bf16...) custom-call(bf16[512,768]{1,0:T(8,128)(2,1)} %bitcast.20.x_ref.refs_0_, bf16[512,768]{1,0:T(8,128)(2,1)} %bitcast.131, ...), custom_call_target="tpu_custom_call" | custom-call | flops 9663676416 | bytes 30000000 | tf_op jit(solution)/shard_map/pallas_call | solution.py:529
  227.3 23.5 %shard_map.266 = (bf16[768,768]{1,0:T(8,128)(2,1)}, bf16[768,768]{1,0:T(8,128)(2,1)}, bf16[768,3072]{1,0:T(8,128)(2,1)}, bf16[768,3072]{1,0:T(8,128)(2,1)}, bf16...) custom-call(bf16[768,768]{1,0:T(8,128)(2,1)} %bitcast.27.x_ref.refs_1_, bf16[768,768]{1,0:T(8,128)(2,1)} %bitcast.125, ...), custom_call_target="tpu_custom_call" | custom-call | flops 14495514624 | bytes 30000000 | tf_op jit(solution)/shard_map/pallas_call | solution.py:529
  250.8 2.7 pad_maximum_fusion.4
  253.5 6.2 %all-to-all-start.3 = ((bf16[16,80,768]{2,1,0:T(8,128)(2,1)}), bf16[16,80,768]{2,1,0:T(8,128)(2,1)}, u32[]{:S(2)}, u32[]{:S(2)}) async-start(bf16[16,80,768]{2,1,0:T(8,128)(2,1)} %pad_maximum_fusion.4), calls=%async_computation.3 | async-start | bytes 3932160 | tf_op jit(solution)/shard_map/all_to_all | solution.py:788
  270.9 10.8 %shard_map.268 = (bf16[512,3072]{1,0:T(8,128)(2,1)}, bf16[512,3072]{1,0:T(8,128)(2,1)}, bf16[512,768]{1,0:T(8,128)(2,1)}) custom-call(bf16[512,768]{1,0:T(8,128)(2,1)} %collective-permute-done.17.x_ref.refs_0_, bf16[512,768]{1,0:T(8,128)(2,1)} %bitcast.133, bf16[768,128]{1,0:T(8,128)(2,1)} %pad.38.router_ref, f32[8,128]{1,0:T(8,128)} %broadcast_in_dim.26.pick_ref, ...), custom_call_target="tpu_custom_call" | custom-call | flops 4831838208 | bytes 30000000 | tf_op jit(solution)/shard_map/pallas_call | solution.py:586
  286.6 21.6 %shard_map.267 = (f32[768,3072]{1,0:T(8,128)}, f32[3072,768]{1,0:T(8,128)}) custom-call(s32[1]{0:T(128)} %constant.61.clone.1.more_ref, bf16[512,768]{1,0:T(8,128)(2,1)} %bitcast.20.x_ref.refs_0_, bf16[768,768]{1,0:T(8,128)(2,1)} %bitcast.27.x_ref.refs_1_, bf16[512,768]{1,0:T(8,128)(2,1)} %get-tuple-element.121.refs_2_, ...), custom_call_target="tpu_custom_call" | custom-call | flops 12079595520 | bytes 50000000 | tf_op jit(solution)/shard_map/pallas_call | solution.py:645
  311.4 13.6 %shard_map.269 = (bf16[768,3072]{1,0:T(8,128)(2,1)}, bf16[768,3072]{1,0:T(8,128)(2,1)}, bf16[768,768]{1,0:T(8,128)(2,1)}) custom-call(bf16[768,768]{1,0:T(8,128)(2,1)} %copy-done.46, bf16[768,768]{1,0:T(8,128)(2,1)} %bitcast.124, bf16[768,128]{1,0:T(8,128)(2,1)} %pad.38.router_ref, f32[8,128]{1,0:T(8,128)} %broadcast_in_dim.26.pick_ref, ...), custom_call_target="tpu_custom_call" | custom-call | flops 7247757312 | bytes 30000000 | tf_op jit(solution)/shard_map/pallas_call | solution.py:586
  334.4 5.8 %all-to-all-start.4 = ((bf16[16,80,768]{2,1,0:T(8,128)(2,1)}), bf16[16,80,768]{2,1,0:T(8,128)(2,1)}, u32[]{:S(2)}, u32[]{:S(2)}) async-start(bf16[16,80,768]{2,1,0:T(8,128)(2,1)} %pad_maximum_fusion.5), calls=%async_computation.4 | async-start | bytes 3932160 | tf_op jit(solution)/shard_map/all_to_all | solution.py:788
  340.2 3.2 fusion.3
  343.5 2.6 convolution_convert_fusion.2.dctx_ref
  346.1 45.4 %shard_map.270 = (bf16[1024,768]{1,0:T(8,128)(2,1)}, bf16[2048,768]{1,0:T(8,128)(2,1)}, bf16[2048,768]{1,0:T(8,128)(2,1)}, f32[12,8,128]{2,1,0:T(8,128)}) custom-call(bf16[1024,768]{1,0:T(8,128)(2,1)} %convolution_convert_fusion.3.q_ref, bf16[2048,768]{1,0:T(8,128)(2,1)} %convolution_convert_fusion.1.k_ref, bf16[2048,768]{1,0:T(8,128)(2,1)} %convolution_convert_fusion.v_ref, ...), custom_call_target="tpu_custom_call" | custom-call | flops 32212254720 | bytes 54000000 | tf_op jit(solution)/shard_map/pallas_call | solution.py:389
  392.8 4.8 convolution_convert_fusion.4
  397.6 3.5 convolution_convert_fusion.7
  401.4 2.7 convolution_convert_fusion.5
  404.1 2.8 convolution_convert_fusion.6
  410.2 4.4 copy.80
  414.6 4.3 copy.81
  418.9 2.9 broadcast_select_fusion.1
  433.5 2.8 collective-permute-start.30
  438.6 3.0 collective-permute-done.31
  453.0 26.6 %shard_map.271 = (f32[768,3072]{1,0:T(8,128)}, f32[3072,768]{1,0:T(8,128)}) custom-call(s32[1]{0:T(128)} %constant.65.clone.1.more_ref, bf16[512,768]{1,0:T(8,128)(2,1)} %collective-permute-done.17.x_ref.refs_0_, bf16[768,768]{1,0:T(8,128)(2,1)} %copy-done.46, bf16[512,768]{1,0:T(8,128)(2,1)} %get-tuple-element.166.refs_2_, ...), custom_call_target="tpu_custom_call" | custom-call | flops 12079595520 | bytes 50000000 | tf_op jit(solution)/shard_map/pallas_call | solution.py:645
  482.4 2.6 fusion.59
  485.0 4.5 fusion.53
  492.1 3.9 collective-permute-start.32
  504.9 2.8 copy.84
  510.6 2.7 collective-permute-done.34
  522.2 4.2 fusion.5
  527.1 2.8 fusion.4
  (306 shorter events, 138.8 us)
Async XLA Ops:
  13.4 26.7 %collective-permute-start.2 = (bf16[1,1,1,48,896]{4,3,2,1,0:T(8,128)(2,1)S(1)}, bf16[1,1,1,48,896]{4,3,2,1,0:T(8,128)(2,1)S(1)}, u32[]{:S(2)}, u32[]{:S(2)}) collective-permute-start(bf16[1,1,1,48,896]{4,3,2,1,0:T(8,128)(2,1)S(1)} %fusion.37), channel_id=1, source_target_pairs={{0,12},{4,0},{8,4},{12,8},{1,13},{5,1},{9,5},{13,9},{2,14},{6,2},{... | collective-permute-start | bytes 258056 | tf_op jit(solution)/shard_map/ppermute | solution.py:703
  18.5 21.7 %collective-permute-start.3 = (bf16[1,1,1,48,896]{4,3,2,1,0:T(8,128)(2,1)S(1)}, bf16[1,1,1,48,896]{4,3,2,1,0:T(8,128)(2,1)S(1)}, u32[]{:S(2)}, u32[]{:S(2)}) collective-permute-start(bf16[1,1,1,48,896]{4,3,2,1,0:T(8,128)(2,1)S(1)} %fusion.37), channel_id=1, source_target_pairs={{0,8},{4,12},{8,0},{12,4},{1,9},{5,13},{9,1},{13,5},{2,10},{6,14},... | collective-permute-start | bytes 258056 | tf_op jit(solution)/shard_map/ppermute | solution.py:703
  18.5 21.7 %collective-permute-start.4 = (bf16[1,1,1,48,896]{4,3,2,1,0:T(8,128)(2,1)S(1)}, bf16[1,1,1,48,896]{4,3,2,1,0:T(8,128)(2,1)S(1)}, u32[]{:S(2)}, u32[]{:S(2)}) collective-permute-start(bf16[1,1,1,48,896]{4,3,2,1,0:T(8,128)(2,1)S(1)} %fusion.37), channel_id=1, source_target_pairs={{0,4},{4,8},{8,12},{12,0},{1,5},{5,9},{9,13},{13,1},{2,6},{6,10},{... | collective-permute-start | bytes 258056 | tf_op jit(solution)/shard_map/ppermute | solution.py:703
  19.5 12.9 %collective-permute-start.6 = (bf16[1,1,1,48,768]{4,3,2,1,0:T(8,128)(2,1)}, bf16[1,1,1,48,768]{4,3,2,1,0:T(8,128)(2,1)S(1)}, u32[]{:S(2)}, u32[]{:S(2)}) collective-permute-start(bf16[1,1,1,48,768]{4,3,2,1,0:T(8,128)(2,1)} %bitcast.138), channel_id=1, source_target_pairs={{0,12},{4,0},{8,4},{12,8},{1,13},{5,1},{9,5},{13,9},{2,14},{6,2},{... | collective-permute-start | bytes 221192 | tf_op jit(solution)/shard_map/ppermute | solution.py:703
  22.3 10.2 %collective-permute-start.7 = (bf16[1,1,1,48,768]{4,3,2,1,0:T(8,128)(2,1)}, bf16[1,1,1,48,768]{4,3,2,1,0:T(8,128)(2,1)S(1)}, u32[]{:S(2)}, u32[]{:S(2)}) collective-permute-start(bf16[1,1,1,48,768]{4,3,2,1,0:T(8,128)(2,1)} %bitcast.139), channel_id=1, source_target_pairs={{0,8},{4,12},{8,0},{12,4},{1,9},{5,13},{9,1},{13,5},{2,10},{6,14},... | collective-permute-start | bytes 221192 | tf_op jit(solution)/shard_map/ppermute | solution.py:703
  32.4 6.2 %collective-permute-start.8 = (bf16[1,1,1,48,768]{4,3,2,1,0:T(8,128)(2,1)S(1)}, bf16[1,1,1,48,768]{4,3,2,1,0:T(8,128)(2,1)S(1)}, u32[]{:S(2)}, u32[]{:S(2)}) collective-permute-start(bf16[1,1,1,48,768]{4,3,2,1,0:T(8,128)(2,1)S(1)} %bitcast.140), channel_id=1, source_target_pairs={{0,4},{4,8},{8,12},{12,0},{1,5},{5,9},{9,13},{13,1},{2,6},{6,10},{... | collective-permute-start | bytes 221192 | tf_op jit(solution)/shard_map/ppermute | solution.py:703
  32.5 6.9 %collective-permute-start.5 = (bf16[1,1,1,48,768]{4,3,2,1,0:T(8,128)(2,1)S(1)}, bf16[1,1,1,48,768]{4,3,2,1,0:T(8,128)(2,1)S(1)}, u32[]{:S(2)}, u32[]{:S(2)}) collective-permute-start(bf16[1,1,1,48,768]{4,3,2,1,0:T(8,128)(2,1)S(1)} %bitcast.141), channel_id=1, source_target_pairs={{0,2},{1,3},{2,0},{3,1},{4,6},{5,7},{6,4},{7,5},{8,10},{9,11},{10,... | collective-permute-start | bytes 221192 | tf_op jit(solution)/shard_map/ppermute | solution.py:681
  40.3 9.4 %collective-permute-start.11 = (bf16[1,2,1,48,768]{4,3,2,1,0:T(8,128)(2,1)}, bf16[1,2,1,48,768]{4,3,2,1,0:T(8,128)(2,1)}, u32[]{:S(2)}, u32[]{:S(2)}) collective-permute-start(bf16[1,2,1,48,768]{4,3,2,1,0:T(8,128)(2,1)} %fusion.34), channel_id=1, source_target_pairs={{0,12},{4,0},{8,4},{12,8},{1,13},{5,1},{9,5},{13,9},{2,14},{6,2},{... | collective-permute-start | bytes 442376 | tf_op jit(solution)/shard_map/ppermute | solution.py:703
  41.7 10.4 %collective-permute-start.12 = (bf16[1,2,1,48,768]{4,3,2,1,0:T(8,128)(2,1)}, bf16[1,2,1,48,768]{4,3,2,1,0:T(8,128)(2,1)}, u32[]{:S(2)}, u32[]{:S(2)}) collective-permute-start(bf16[1,2,1,48,768]{4,3,2,1,0:T(8,128)(2,1)} %fusion.34), channel_id=1, source_target_pairs={{0,8},{4,12},{8,0},{12,4},{1,9},{5,13},{9,1},{13,5},{2,10},{6,14},... | collective-permute-start | bytes 442376 | tf_op jit(solution)/shard_map/ppermute | solution.py:703
  43.0 29.2 %collective-permute-start.1 = (bf16[512,768]{1,0:T(8,128)(2,1)}, bf16[512,768]{1,0:T(8,128)(2,1)S(1)}, u32[]{:S(2)}, u32[]{:S(2)}) collective-permute-start(bf16[512,768]{1,0:T(8,128)(2,1)} %get-tuple-element.239), channel_id=1, source_target_pairs={{1,0},{2,1},{3,2},{5,4},{6,5},{7,6},{9,8},{10,9},{11,10},{13,12},{... | collective-permute-start | bytes 2359304 | tf_op jit(solution)/shard_map/ppermute | solution.py:909
  44.2 27.9 %collective-permute-start = (bf16[512,768]{1,0:T(8,128)(2,1)}, bf16[512,768]{1,0:T(8,128)(2,1)S(1)}, u32[]{:S(2)}, u32[]{:S(2)}) collective-permute-start(bf16[512,768]{1,0:T(8,128)(2,1)} %get-tuple-element.238), channel_id=1, source_target_pairs={{0,1},{1,2},{2,3},{4,5},{5,6},{6,7},{8,9},{9,10},{10,11},{12,13},{... | collective-permute-start | bytes 2359304 | tf_op jit(solution)/shard_map/ppermute | solution.py:909
  49.0 21.2 %copy-start.28 = (bf16[4,1,1,48,768]{4,3,2,1,0:T(8,128)(2,1)S(1)}, bf16[4,1,1,48,768]{4,3,2,1,0:T(8,128)(2,1)}, u32[]{:S(2)}) copy-start(bf16[4,1,1,48,768]{4,3,2,1,0:T(8,128)(2,1)} %constant_dynamic-slice_fusion.1) | copy-start | bytes 884740
  49.0 8.6 %collective-permute-start.13 = (bf16[1,2,1,48,768]{4,3,2,1,0:T(8,128)(2,1)}, bf16[1,2,1,48,768]{4,3,2,1,0:T(8,128)(2,1)S(1)}, u32[]{:S(2)}, u32[]{:S(2)}) collective-permute-start(bf16[1,2,1,48,768]{4,3,2,1,0:T(8,128)(2,1)} %fusion.34), channel_id=1, source_target_pairs={{0,4},{4,8},{8,12},{12,0},{1,5},{5,9},{9,13},{13,1},{2,6},{6,10},{... | collective-permute-start | bytes 442376 | tf_op jit(solution)/shard_map/ppermute | solution.py:703
  49.7 22.0 %collective-permute-start.9 = (bf16[4,1,1,48,896]{4,3,2,1,0:T(8,128)(2,1)S(1)}, bf16[4,1,1,48,896]{4,3,2,1,0:T(8,128)(2,1)S(1)}, u32[]{:S(2)}, u32[]{:S(2)}) collective-permute-start(bf16[4,1,1,48,896]{4,3,2,1,0:T(8,128)(2,1)S(1)} %constant_dynamic-slice_fusion.2), channel_id=1, source_target_pairs={{0,2},{1,3},{2,0},{3,1},{4,6},{5,7},{6,4},{7,5},{8,10},{9,11},{10,... | collective-permute-start | bytes 1032200 | tf_op jit(solution)/shard_map/ppermute | solution.py:681
  52.1 18.1 %collective-permute-start.15 = (bf16[4,1,1,48,768]{4,3,2,1,0:T(8,128)(2,1)}, bf16[4,1,1,48,768]{4,3,2,1,0:T(8,128)(2,1)S(1)}, u32[]{:S(2)}, u32[]{:S(2)}) collective-permute-start(bf16[4,1,1,48,768]{4,3,2,1,0:T(8,128)(2,1)} %constant_dynamic-slice_fusion.1), channel_id=1, source_target_pairs={{0,2},{1,3},{2,0},{3,1},{4,6},{5,7},{6,4},{7,5},{8,10},{9,11},{10,... | collective-permute-start | bytes 884744 | tf_op jit(solution)/shard_map/ppermute | solution.py:681
  60.5 12.5 %collective-permute-start.14 = (bf16[4,2,1,48,768]{4,3,2,1,0:T(8,128)(2,1)S(1)}, bf16[4,2,1,48,768]{4,3,2,1,0:T(8,128)(2,1)S(1)}, u32[]{:S(2)}, u32[]{:S(2)}) collective-permute-start(bf16[4,2,1,48,768]{4,3,2,1,0:T(8,128)(2,1)S(1)} %constant_dynamic-slice_fusion), channel_id=1, source_target_pairs={{0,1},{1,0},{2,3},{3,2},{4,5},{5,4},{6,7},{7,6},{8,9},{9,8},{10,11... | collective-permute-start | bytes 1769480 | tf_op jit(solution)/shard_map/ppermute | solution.py:681
  70.5 4.1 collective-permute-start.16
  72.0 4.2 collective-permute-start.10
  77.0 17.7 %copy-start.6 = (bf16[4,2,2,48,896]{4,3,2,1,0:T(8,128)(2,1)}, bf16[4,2,2,48,896]{4,3,2,1,0:T(8,128)(2,1)S(1)}, u32[]{:S(2)}) copy-start(bf16[4,2,2,48,896]{4,3,2,1,0:T(8,128)(2,1)S(1)} %fusion.13) | copy-start | bytes 4128772
  78.5 73.9 %all-to-all-start = ((bf16[16,80,768]{2,1,0:T(8,128)(2,1)}), bf16[16,80,768]{2,1,0:T(8,128)(2,1)}, u32[]{:S(2)}, u32[]{:S(2)}) async-start(bf16[16,80,768]{2,1,0:T(8,128)(2,1)} %pad_maximum_fusion.3), calls=%async_computation | async-start | bytes 3932160 | tf_op jit(solution)/shard_map/all_to_all | solution.py:788
  84.6 60.6 %all-gather.2.cloned.1.call-start = ((), (), s32[]{:S(2)}) async-start(), calls=%async_computation.5 | async-start | bytes 1253376 | tf_op jit(solution)/shard_map/all_gather | solution.py:945
  152.4 23.2 %all-to-all-start.1 = ((bf16[16,32,768]{2,1,0:T(8,128)(2,1)}), bf16[16,32,768]{2,1,0:T(8,128)(2,1)}, u32[]{:S(2)}, u32[]{:S(2)}) async-start(bf16[16,32,768]{2,1,0:T(8,128)(2,1)} %bitcast.132), calls=%async_computation.1 | async-start | bytes 1572864 | tf_op jit(solution)/shard_map/all_to_all | solution.py:788
  175.6 51.7 %all-to-all-start.2 = ((bf16[16,48,768]{2,1,0:T(8,128)(2,1)}), bf16[16,48,768]{2,1,0:T(8,128)(2,1)}, u32[]{:S(2)}, u32[]{:S(2)}) async-start(bf16[16,48,768]{2,1,0:T(8,128)(2,1)} %bitcast.123), calls=%async_computation.2 | async-start | bytes 2359296 | tf_op jit(solution)/shard_map/all_to_all | solution.py:788
  181.1 28.0 %collective-permute-start.17 = (bf16[512,768]{1,0:T(8,128)(2,1)}, bf16[512,768]{1,0:T(8,128)(2,1)}, u32[]{:S(2)}, u32[]{:S(2)}) collective-permute-start(bf16[512,768]{1,0:T(8,128)(2,1)} %bitcast.20.x_ref.refs_0_), channel_id=1, source_target_pairs={{0,16},{16,0},{1,17},{17,1},{2,18},{18,2},{3,19},{19,3},{4,20},{20... | collective-permute-start | bytes 2359304 | tf_op jit(solution)/shard_map/ppermute | solution.py:681
  183.6 17.5 %collective-permute-start.18 = (f32[16]{0:T(128)S(1)}, f32[16]{0:T(128)S(1)}, u32[]{:S(2)}, u32[]{:S(2)}) collective-permute-start(f32[16]{0:T(128)S(1)} %fusion.43), channel_id=1, source_target_pairs={{0,16},{16,0},{1,17},{17,1},{2,18},{18,2},{3,19},{19,3},{4,20},{20... | collective-permute-start | bytes 200 | tf_op jit(solution)/shard_map/ppermute | solution.py:681
  207.6 57.4 %collective-permute-start.19 = (bf16[1280,768]{1,0:T(8,128)(2,1)}, bf16[1280,768]{1,0:T(8,128)(2,1)}, u32[]{:S(2)}, u32[]{:S(2)}) collective-permute-start(bf16[1280,768]{1,0:T(8,128)(2,1)} %bitcast.18), channel_id=1, source_target_pairs={{0,16},{16,0},{1,17},{17,1},{2,18},{18,2},{3,19},{19,3},{4,20},{20... | collective-permute-start | bytes 5898248 | tf_op jit(solution)/shard_map/ppermute | solution.py:681
  227.3 23.5 %copy-start.31 = (bf16[512,768]{1,0:T(8,128)(2,1)S(1)}, bf16[512,768]{1,0:T(8,128)(2,1)}, u32[]{:S(2)}) copy-start(bf16[512,768]{1,0:T(8,128)(2,1)} %get-tuple-element.118) | copy-start | bytes 2359300
  253.5 71.6 %all-to-all-start.3 = ((bf16[16,80,768]{2,1,0:T(8,128)(2,1)}), bf16[16,80,768]{2,1,0:T(8,128)(2,1)}, u32[]{:S(2)}, u32[]{:S(2)}) async-start(bf16[16,80,768]{2,1,0:T(8,128)(2,1)} %pad_maximum_fusion.4), calls=%async_computation.3 | async-start | bytes 3932160 | tf_op jit(solution)/shard_map/all_to_all | solution.py:788
  281.8 28.6 %collective-permute-start.20 = (bf16[768,768]{1,0:T(8,128)(2,1)}, bf16[768,768]{1,0:T(8,128)(2,1)S(1)}, u32[]{:S(2)}, u32[]{:S(2)}) collective-permute-start(bf16[768,768]{1,0:T(8,128)(2,1)} %bitcast.27.x_ref.refs_1_), channel_id=1, source_target_pairs={{0,16},{16,0},{1,17},{17,1},{2,18},{18,2},{3,19},{19,3},{4,20},{20... | collective-permute-start | bytes 3538952 | tf_op jit(solution)/shard_map/ppermute | solution.py:681
  334.4 63.2 %all-to-all-start.4 = ((bf16[16,80,768]{2,1,0:T(8,128)(2,1)}), bf16[16,80,768]{2,1,0:T(8,128)(2,1)}, u32[]{:S(2)}, u32[]{:S(2)}) async-start(bf16[16,80,768]{2,1,0:T(8,128)(2,1)} %pad_maximum_fusion.5), calls=%async_computation.4 | async-start | bytes 3932160 | tf_op jit(solution)/shard_map/all_to_all | solution.py:788
  346.1 45.4 %copy-start.40 = (f32[8,128,32]{1,2,0:T(8,128)S(1)}, f32[8,128,32]{1,2,0:T(8,128)}, u32[]{:S(2)}) copy-start(f32[8,128,32]{1,2,0:T(8,128)} %constant.67.clone) | copy-start | bytes 393220
  421.8 22.2 %collective-permute-start.22 = (bf16[2,2,2,1,48,1536]{5,4,3,2,1,0:T(8,128)(2,1)}, bf16[2,2,2,1,48,1536]{5,4,3,2,1,0:T(8,128)(2,1)}, u32[]{:S(2)}, u32[]{:S(2)}) collective-permute-start(bf16[2,2,2,1,48,1536]{5,4,3,2,1,0:T(8,128)(2,1)} %broadcast_select_fusion.1), channel_id=1, source_target_pairs={{0,1},{1,0},{2,3},{3,2},{4,5},{5,4},{6,7},{7,6},{8,9},{9,8},{10,11... | collective-permute-start | bytes 3538952 | tf_op jit(solution)/shard_map/ppermute | solution.py:681
  423.3 23.3 %collective-permute-start.21 = (bf16[2,2,2,1,48,1664]{5,4,3,2,1,0:T(8,128)(2,1)}, bf16[2,2,2,1,48,1664]{5,4,3,2,1,0:T(8,128)(2,1)}, u32[]{:S(2)}, u32[]{:S(2)}) collective-permute-start(bf16[2,2,2,1,48,1664]{5,4,3,2,1,0:T(8,128)(2,1)} %broadcast_select_fusion), channel_id=1, source_target_pairs={{0,1},{1,0},{2,3},{3,2},{4,5},{5,4},{6,7},{7,6},{8,9},{9,8},{10,11... | collective-permute-start | bytes 3833864 | tf_op jit(solution)/shard_map/ppermute | solution.py:681
  423.5 3.0 collective-permute-start.27
  426.5 3.5 collective-permute-start.28
  430.0 3.5 collective-permute-start.29
  433.5 4.4 collective-permute-start.30
  438.0 3.5 collective-permute-start.31
  448.6 31.2 %collective-permute-start.23 = (bf16[2,2,1,1,48,1664]{5,4,3,2,1,0:T(8,128)(2,1)S(1)}, bf16[2,2,1,1,48,1664]{5,4,3,2,1,0:T(8,128)(2,1)S(1)}, u32[]{:S(2)}, u32[]{:S(2)}) collective-permute-start(bf16[2,2,1,1,48,1664]{5,4,3,2,1,0:T(8,128)(2,1)S(1)} %broadcast_select_fusion.2), channel_id=1, source_target_pairs={{0,2},{1,3},{2,0},{3,1},{4,6},{5,7},{6,4},{7,5},{8,10},{9,11},{10,... | collective-permute-start | bytes 1916936 | tf_op jit(solution)/shard_map/ppermute | solution.py:681
  450.6 29.0 %collective-permute-start.24 = (bf16[1,2,2,1,48,1536]{5,4,3,2,1,0:T(8,128)(2,1)S(1)}, bf16[1,2,2,1,48,1536]{5,4,3,2,1,0:T(8,128)(2,1)S(1)}, u32[]{:S(2)}, u32[]{:S(2)}) collective-permute-start(bf16[1,2,2,1,48,1536]{5,4,3,2,1,0:T(8,128)(2,1)S(1)} %broadcast_select_fusion.3), channel_id=1, source_target_pairs={{0,8},{4,12},{8,0},{12,4},{1,9},{5,13},{9,1},{13,5},{2,10},{6,14},... | collective-permute-start | bytes 1769480 | tf_op jit(solution)/shard_map/ppermute | solution.py:681
  480.2 16.0 %collective-permute-start.25 = (bf16[1,2,1,1,48,1664]{5,4,3,2,1,0:T(8,128)(2,1)S(1)}, bf16[1,2,1,1,48,1664]{5,4,3,2,1,0:T(8,128)(2,1)S(1)}, u32[]{:S(2)}, u32[]{:S(2)}) collective-permute-start(bf16[1,2,1,1,48,1664]{5,4,3,2,1,0:T(8,128)(2,1)S(1)} %broadcast_select_fusion.4), channel_id=1, source_target_pairs={{0,8},{4,12},{8,0},{12,4},{1,9},{5,13},{9,1},{13,5},{2,10},{6,14},... | collective-permute-start | bytes 958472 | tf_op jit(solution)/shard_map/ppermute | solution.py:681
  480.8 15.2 %collective-permute-start.26 = (bf16[1,1,2,1,48,1536]{5,4,3,2,1,0:T(8,128)(2,1)S(1)}, bf16[1,1,2,1,48,1536]{5,4,3,2,1,0:T(8,128)(2,1)S(1)}, u32[]{:S(2)}, u32[]{:S(2)}) collective-permute-start(bf16[1,1,2,1,48,1536]{5,4,3,2,1,0:T(8,128)(2,1)S(1)} %broadcast_select_fusion.5), channel_id=1, source_target_pairs={{0,4},{4,0},{8,12},{12,8},{1,5},{5,1},{9,13},{13,9},{2,6},{6,2},{1... | collective-permute-start | bytes 884744 | tf_op jit(solution)/shard_map/ppermute | solution.py:681
  490.8 31.3 %collective-permute-start.33 = (bf16[512,768]{0,1:T(8,128)(2,1)}, bf16[512,768]{0,1:T(8,128)(2,1)}, u32[]{:S(2)}, u32[]{:S(2)}) collective-permute-start(bf16[512,768]{0,1:T(8,128)(2,1)} %get-tuple-element.237), channel_id=1, source_target_pairs={{1,0},{2,1},{3,2},{5,4},{6,5},{7,6},{9,8},{10,9},{11,10},{13,12},{... | collective-permute-start | bytes 2359304 | tf_op jit(solution)/shard_map/ppermute | solution.py:1033
  492.1 30.0 %collective-permute-start.32 = (bf16[512,768]{0,1:T(8,128)(2,1)}, bf16[512,768]{0,1:T(8,128)(2,1)}, u32[]{:S(2)}, u32[]{:S(2)}) collective-permute-start(bf16[512,768]{0,1:T(8,128)(2,1)} %get-tuple-element.236), channel_id=1, source_target_pairs={{0,1},{1,2},{2,3},{4,5},{5,6},{6,7},{8,9},{9,10},{10,11},{12,13},{... | collective-permute-start | bytes 2359304 | tf_op jit(solution)/shard_map/ppermute | solution.py:1034
  501.3 7.7 %collective-permute-start.36 = (bf16[1,1,1,1,48,1536]{5,4,3,2,1,0:T(8,128)(2,1)}, bf16[1,1,1,1,48,1536]{5,4,3,2,1,0:T(8,128)(2,1)}, u32[]{:S(2)}, u32[]{:S(2)}) collective-permute-start(bf16[1,1,1,1,48,1536]{5,4,3,2,1,0:T(8,128)(2,1)} %broadcast_select_fusion.7), channel_id=1, source_target_pairs={{0,2},{1,3},{2,0},{3,1},{4,6},{5,7},{6,4},{7,5},{8,10},{9,11},{10,... | collective-permute-start | bytes 442376 | tf_op jit(solution)/shard_map/ppermute | solution.py:681
  507.7 5.6 %collective-permute-start.34 = (bf16[1,1,1,1,48,1664]{5,4,3,2,1,0:T(8,128)(2,1)}, bf16[1,1,1,1,48,1664]{5,4,3,2,1,0:T(8,128)(2,1)S(1)}, u32[]{:S(2)}, u32[]{:S(2)}) collective-permute-start(bf16[1,1,1,1,48,1664]{5,4,3,2,1,0:T(8,128)(2,1)} %broadcast_select_fusion.6), channel_id=1, source_target_pairs={{0,4},{4,0},{8,12},{12,8},{1,5},{5,1},{9,13},{13,9},{2,6},{6,2},{1... | collective-permute-start | bytes 479240 | tf_op jit(solution)/shard_map/ppermute | solution.py:681
  510.0 6.5 %collective-permute-start.37 = (bf16[48,1536]{1,0:T(8,128)(2,1)S(1)}, bf16[48,1536]{1,0:T(8,128)(2,1)S(1)}, u32[]{:S(2)}, u32[]{:S(2)}) collective-permute-start(bf16[48,1536]{1,0:T(8,128)(2,1)S(1)} %fusion.35), channel_id=1, source_target_pairs={{0,16},{16,0},{1,17},{17,1},{2,18},{18,2},{3,19},{19,3},{4,20},{20... | collective-permute-start | bytes 442376 | tf_op jit(solution)/shard_map/ppermute | solution.py:681
  513.3 5.3 collective-permute-start.35
  (49 other events, 245.3 us)
Sparse Core Ops, SparseCore 0:
  94.9 50.1 all-gather.1

commit v3 on v2

--- a/solution.py
+++ b/solution.py
@@ -6,6 +6,7 @@
 import numpy as np
 from jax import lax
 from jax.experimental import pallas as pl
+from jax.experimental.layout import Layout, with_layout_constraint
 from jax.experimental.pallas import tpu as pltpu
 from jax.sharding import PartitionSpec as P
 
@@ -713,8 +714,9 @@
     near = list(range(seq_bits - 1, 0, -1))
     state = [x.reshape((1,) * (1 + seq_bits) + x.shape) for x in parts]
     for hop in range(seq_bits + 1):
-        if hop == 1:
-            *state, meanwhile = together(*state, meanwhile)
+        if hop > 0:
+            values = together(*state, *meanwhile)
+            state, meanwhile = list(values[: len(parts)]), values[len(parts) :]
         for turn, y in enumerate(state):
             what = (["shard"] + near + [0] if turn % 2 == 0 else near + ["shard", 0])[hop]
             if what == "shard":
@@ -724,13 +726,13 @@
     return [y.reshape(-1, y.shape[-1]) for y in state], meanwhile
 
 
-def half_kept(x, axis, bit, dim):
-    low = lax.index_in_dim(x, 0, dim)
-    high = lax.index_in_dim(x, 1, dim)
+def half_kept(x, axis, bit, outer):
+    low, high = (x.reshape(outer, 2, -1, x.shape[1])[:, k] for k in range(2))
     mine = bit_at(axis, bit) == 1
     got = exchange(jnp.where(mine, low, high), axis, 1 << bit)
     kept = jnp.where(mine, high, low)
-    return (kept.astype(jnp.float32) + got.astype(jnp.float32)).astype(jnp.bfloat16)
+    total = (kept.astype(jnp.float32) + got.astype(jnp.float32)).astype(jnp.bfloat16)
+    return total.reshape(-1, x.shape[1])
 
 
 def rep_sums(y):
@@ -741,32 +743,30 @@
     return total
 
 
-def blocks_of(x):
-    bits = bits_of("shard") + bits_of("seq")
-    return x.reshape((2,) * bits + (x.shape[0] >> bits, x.shape[1]))
+def scatter_order(turn):
+    far = [("shard", b) for b in range(bits_of("shard") - 1, -1, -1)]
+    near = [("seq", b) for b in range(bits_of("seq") - 1, 0, -1)]
+    return [("seq", 0)] + (near + far if turn % 2 == 0 else far + near)
 
 
 def scatter_hop(state, hop):
-    seq_bits, shard_bits = bits_of("seq"), bits_of("shard")
-    far = [("shard", b) for b in range(shard_bits - 1, -1, -1)]
-    near = [("seq", b) for b in range(seq_bits - 1, 0, -1)]
+    places = [("shard", b) for b in range(bits_of("shard") - 1, -1, -1)]
+    places += [("seq", b) for b in range(bits_of("seq") - 1, -1, -1)]
     out = []
     for turn, x in enumerate(state):
-        axis, bit = ([("seq", 0)] + (near + far if turn % 2 == 0 else far + near))[hop]
-        dim = shard_bits - 1 - bit if axis == "shard" else shard_bits + seq_bits - 1 - bit
-        out.append(half_kept(x, axis, bit, dim))
+        order = scatter_order(turn)
+        left = [p for p in places if p not in order[:hop]]
+        axis, bit = order[hop]
+        out.append(half_kept(x, axis, bit, 1 << left.index((axis, bit))))
     return out
-
-
-def sum_everywhere(x):
-    for axis in ("seq", "shard", "rep"):
-        for bit in range(bits_of(axis)):
-            x = x + exchange(x, axis, 1 << bit)
-    return x
 
 
 def together(*values):
     return lax.optimization_barrier(values)
+
+
+def in_rows(x):
+    return with_layout_constraint(x, Layout(major_to_minor=(0, 1)))
 
 
 def rms_norm(vectors, gains):
@@ -920,8 +920,8 @@
         axis=1,
     )
     small = jnp.pad(small, ((0, 0), (0, SUB - small.shape[1])))
-    (w_q, w_k, w_v), cot_sent = gather_rows(
-        [jnp.concatenate([w_query, small], axis=1), w_key, w_value], joined(cot_sent)
+    (w_q, w_k, w_v), (cot_sent, w_attn_out) = gather_rows(
+        [jnp.concatenate([w_query, small], axis=1), w_key, w_value], (joined(cot_sent), w_attn_out)
     )
     w_q, extra = w_q[:, :D], w_q[:, D:]
     router = extra[:, :experts]
@@ -941,7 +941,6 @@
     pick = wide_row(jnp.arange(experts) == me)
     aux = wide_row((AUX_WEIGHT * experts / live_all) * shares)
 
-    w_attn_out, cot_sent, w_q, w_k, w_v = together(w_attn_out, cot_sent, w_q, w_k, w_v)
     w_proj = lax.all_gather(w_attn_out, GROUP, axis=0, tiled=True)
     cot_rows = across(cot_sent)
 
@@ -968,21 +967,22 @@
     if rep_count == 2:
         cot_other = exchange(cot_rows, "rep", 1)
         x_other = [exchange(x, "rep", 1) for x in x_parts]
-        x_parts[0], x_other[0] = together(x_parts[0], x_other[0])
     done = []
     for x, c in zip(x_parts, cot_parts):
-        done.append(expert_pass(x, c, router_wide, pick, aux, w_in, w_out, experts))
+        if done:
+            x, done[-1][1] = together(x, done[-1][1])
+        done.append(list(expert_pass(x, c, router_wide, pick, aux, w_in, w_out, experts)))
     out_parts, back_parts, acts, d_pres, d_row_parts, d_logit_parts = zip(*done)
     blank = [jnp.zeros(shape, jnp.float32) for shape in ((D, WTILE), (WTILE, D))]
     d_expert = weight_pass((x_parts, d_row_parts, acts, d_pres), blank, 0)
-    back_all = across(joined(back_parts))
+    back = [across(p) for p in back_parts]
     if rep_count == 2:
         hidden = []
         for x, c in zip(x_other, split(cot_other)):
             hidden += hidden_pass(x, c, router_wide, pick, w_in, w_out, experts)
-        back_all, *rest = together(back_all, *d_expert, *hidden)
+        back[-1], *rest = together(back[-1], *d_expert, *hidden)
         d_expert, hidden = rest[:2], rest[2:]
-    d_normed_two = collected(split(back_all))
+    d_normed_two = collected(back)
     d_normed_two, *out_parts = together(d_normed_two, *out_parts)
     out_all = across(joined(out_parts))
     d_router = sum(dot_tn(x, d) for x, d in zip(x_parts, d_logit_parts))[:, :experts]
@@ -1011,15 +1011,15 @@
         dot_tn(n, d) for n, d in ((normed_one, d_q), (normed_span, d_k), (normed_span, d_v))
     )
     grads = [
-        jnp.concatenate([g.astype(jnp.bfloat16) for g in pair], axis=1)
+        jnp.concatenate([in_rows(g.astype(jnp.bfloat16)) for g in pair], axis=1)
         for pair in ((d_query, d_attn_out, more), (d_key, d_value))
     ]
     mass = jnp.sum(router_probs * is_live, axis=0)
-    mass, *grads = together(mass, *grads)
-    mass_all = sum_everywhere(mass)
-    grads = [blocks_of(g) for g in grads]
+    mass_all, *grads = together(mass, *grads)
     for hop in range(bits_of("shard") + bits_of("seq")):
-        grads = scatter_hop(grads, hop)
+        axis, bit = scatter_order(0)[hop]
+        mass_all = mass_all + exchange(mass_all, axis, 1 << bit)
+        mass_all, *grads = together(mass_all, *scatter_hop(grads, hop))
         if hop == 0 and rep_count == 2:
             *grads, x_other[0] = together(*grads, x_other[0])
             rows_other = (x_other, hidden[2::3], hidden[0::3], hidden[1::3])
@@ -1036,7 +1036,9 @@
         d_expert = [
             lax.psum(g.astype(jnp.bfloat16), "rep").astype(jnp.float32) for g in d_expert
         ]
-    left, right = (rep_sums(g.reshape(shard_rows, -1)) for g in grads)
+    left, right = (rep_sums(g) for g in grads)
+    for bit in range(bits_of("rep")):
+        mass_all = mass_all + exchange(mass_all, "rep", 1 << bit)
     d_query, d_attn_out, more = left[:, :D], left[:, D : 2 * D], left[:, 2 * D :]
     d_key, d_value = right[:, :D], right[:, D:]
     d_gain_attn = sum(

time: 551 us -> 517 us (0.938)
  waiting for transfers between devices: 75.1 us -> 49 us
  local copies, waits for them, and re-layouts: 58.3 us -> 41.8 us
  starting transfers between devices: 76.8 us -> 87 us
    ppermute x25, waiting for transfers between devices: 44.1 us -> 25.1 us  [exchange(): return lax.ppermute(x, axis, [(i, i ^ hop) for i in range(count)])]
    optimization_barrier x2 -> x0, local copies, waits for them, and re-layouts: 8.69 us -> none  [together(): return lax.optimization_barrier(values)]
    all_to_all x5 -> x6, starting transfers between devices: 28.1 us -> 36.7 us  [routed_across(): return lax.all_to_all(x, GROUP, split_axis=0, concat_axis=0, tiled=True)]
    all_gather x1, waiting for transfers between devices: 7.99 us -> 0.02 us  [shards(): w_proj = lax.all_gather(w_attn_out, GROUP, axis=0, tiled=True)]
    dot_general x10, matrix products: 23.1 us -> 28.9 us  [dot_tn(): lax.dot_general(a, b, (((0,), (0,)), ((), ())), preferred_element_type=jn...]
    unnamed x130 -> x120, local copies, waits for them, and re-layouts: 21.2 us -> 16.9 us
    slice x8 -> x6, local copies, waits for them, and re-layouts: 14.3 us -> 11.6 us  [split(): return [values[:, start:stop].reshape(-1, D) for start, stop in parts]]
    all_to_all x5 -> x6, waiting for transfers between devices: 14.4 us -> 14.5 us  [routed_across(): return lax.all_to_all(x, GROUP, split_axis=0, concat_axis=0, tiled=True)]
  transfers between devices with their start and end apart: 44 -> 45, of which waited for: 15 -> 10; matrix products, arithmetic and copies ran while one was open for 21% -> 23% of each run, Pallas kernels for 37% -> 39%
where the time goes in v3:
time: 517 us; the launch traced here: 509 us
  Pallas kernels  199 us (38%)
  starting transfers between devices  87 us (17%)
  matrix products  66.4 us (13%)
  waiting for transfers between devices  49 us (9%)
  other arithmetic  46.7 us (9%)
  local copies, waits for them, and re-layouts  41.8 us (8%)
  between operations  18.6 us (4%)
    pallas_call x2, Pallas kernels, weight_pass(): pl.pallas_call(functools.partial(weight_kernel, len(sizes)), grid_spec=pl...  47.7 us
    pallas_call x1, Pallas kernels, attention_backward(): pl.pallas_call(backward_kernel, grid=(pairs,), in_specs=[spec((rows, SUB)...  45.6 us
    pallas_call x2, Pallas kernels, expert_pass(): pl.pallas_call(functools.partial(expert_kernel, experts), grid=(FF // TIL...  40.3 us
    all_to_all x6, starting transfers between devices, routed_across(): return lax.all_to_all(x, GROUP, split_axis=0, concat_axis=0, tiled=True)  36.7 us
    pallas_call x1, Pallas kernels, attention_forward(): pl.pallas_call(forward_kernel, grid=(PAIRS,), in_specs=[spec((rows, SUB),...  35.2 us
    dot_general x10, matrix products, dot_tn(): lax.dot_general(a, b, (((0,), (0,)), ((), ())), preferred_element_type=jn...  28.9 us
    ppermute x25, starting transfers between devices, exchange(): return lax.ppermute(x, axis, [(i, i ^ hop) for i in range(count)])  27.8 us
    ppermute x25, waiting for transfers between devices, exchange(): return lax.ppermute(x, axis, [(i, i ^ hop) for i in range(count)])  25.1 us
  transfers between devices with their start and end apart: 45, of which 10 were waited for; matrix products, arithmetic and copies ran while one was open for 23% of the time, Pallas kernels for 39%

profile of v3, /device:TPU:0, one launch (start us, length us, event | category | flops | bytes accessed | tf_op | source)
XLA Modules:
  0.0 508.7 jit_solution(16255872696847287297)
XLA Ops:
  13.5 5.0 collective-permute-start.2
  19.5 2.8 collective-permute-start.6
  23.5 6.0 %shard_map.263 = (bf16[1024,128]{1,0:T(8,128)(2,1)}, bf16[2048,128]{1,0:T(8,128)(2,1)}, bf16[1024,128]{1,0:T(8,128)(2,1)}, bf16[512,1024]{1,0:T(8,128)(2,1)}, bf...) custom-call(s32[1,4]{1,0:T(1,128)} %len_ref.1, s32[1]{0:T(128)} %bitcast.6.first_ref, ...), custom_call_target="tpu_custom_call" | custom-call | flops 2013265920 | bytes 8000000 | tf_op jit(solution)/shard_map/pallas_call | solution.py:840
  29.5 2.9 pad_maximum_fusion.3
  34.1 4.5 collective-permute-done.8
  43.6 3.1 collective-permute-start
  50.5 4.7 collective-permute-done.12
  56.2 13.4 %collective-permute-done.13 = bf16[4,1,1,48,768]{4,3,2,1,0:T(8,128)(2,1)S(1)} collective-permute-done((bf16[4,1,1,48,768]{4,3,2,1,0:T(8,128)(2,1)S(1)}, bf16[4,1,1,48,768]{4,3,2,1,0:T(8,128)(2,1)S(1)}, u32[]{:S(2)}, u32[]{:S(2)}) %collective-permute-start.13) | collective-permute-done | bytes 294944 | tf_op jit(solution)/shard_map/ppermute | solution.py:682
  75.1 6.2 %all-to-all-start = ((bf16[16,80,768]{2,1,0:T(8,128)(2,1)}), bf16[16,80,768]{2,1,0:T(8,128)(2,1)}, u32[]{:S(2)}, u32[]{:S(2)}) async-start(bf16[16,80,768]{2,1,0:T(8,128)(2,1)} %bitcast.17), calls=%async_computation | async-start | bytes 3932160 | tf_op jit(solution)/shard_map/all_to_all | solution.py:788
  91.2 4.0 convolution_convert_fusion.1.k_ref
  95.2 2.5 convolution_convert_fusion.3.q_ref
  98.8 3.9 convolution_convert_fusion.v_ref
  102.7 35.2 %shard_map.264 = (bf16[1024,768]{1,0:T(8,128)(2,1)}, bf16[6,4,2,1280,256]{4,3,2,1,0:T(8,128)(2,1)}, f32[6,4,8,256]{3,2,1,0:T(8,128)}) custom-call(bf16[1024,768]{1,0:T(8,128)(2,1)} %convolution_convert_fusion.3.q_ref, bf16[2048,768]{1,0:T(8,128)(2,1)} %convolution_convert_fusion.1.k_ref, bf16[2048,768]{1,0:T(8,128)(2,1)} %convolution_convert_fusion.v_ref, ...), custom_call_target="tpu_custom_call" | custom-call | flops 16106127360 | bytes 45000000 | tf_op jit(solution)/shard_map/pallas_call | solution.py:348
  138.0 3.8 multiply_reduce_fusion.2
  145.2 6.5 %all-to-all-start.1 = ((bf16[16,32,768]{2,1,0:T(8,128)(2,1)}), bf16[16,32,768]{2,1,0:T(8,128)(2,1)}, u32[]{:S(2)}, u32[]{:S(2)}) async-start(bf16[16,32,768]{2,1,0:T(8,128)(2,1)} %bitcast.237), calls=%async_computation.1 | async-start | bytes 1572864 | tf_op jit(solution)/shard_map/all_to_all | solution.py:788
  151.7 4.3 convolution_convert_fusion.8
  156.0 14.4 %all-to-all-done.1 = bf16[16,32,768]{2,1,0:T(8,128)(2,1)} async-done(((bf16[16,32,768]{2,1,0:T(8,128)(2,1)}), bf16[16,32,768]{2,1,0:T(8,128)(2,1)}, u32[]{:S(2)}, u32[]{:S(2)}) %all-to-all-start.1) | async-done | bytes 786464 | tf_op jit(solution)/shard_map/all_to_all | solution.py:788
  170.5 5.9 %all-to-all-start.2 = ((bf16[16,48,768]{2,1,0:T(8,128)(2,1)}), bf16[16,48,768]{2,1,0:T(8,128)(2,1)}, u32[]{:S(2)}, u32[]{:S(2)}) async-start(bf16[16,48,768]{2,1,0:T(8,128)(2,1)} %bitcast.228), calls=%async_computation.2 | async-start | bytes 2359296 | tf_op jit(solution)/shard_map/all_to_all | solution.py:788
  176.4 2.6 copy.150
  193.8 16.9 %shard_map.265 = (bf16[512,768]{1,0:T(8,128)(2,1)}, bf16[512,768]{1,0:T(8,128)(2,1)}, bf16[512,3072]{1,0:T(8,128)(2,1)}, bf16[512,3072]{1,0:T(8,128)(2,1)}, bf16...) custom-call(bf16[512,768]{1,0:T(8,128)(2,1)} %bitcast.20.x_ref.refs_0_, bf16[512,768]{1,0:T(8,128)(2,1)} %bitcast.236, ...), custom_call_target="tpu_custom_call" | custom-call | flops 9663676416 | bytes 30000000 | tf_op jit(solution)/shard_map/pallas_call | solution.py:530
  210.8 23.4 %shard_map.266 = (bf16[768,768]{1,0:T(8,128)(2,1)}, bf16[768,768]{1,0:T(8,128)(2,1)}, bf16[768,3072]{1,0:T(8,128)(2,1)}, bf16[768,3072]{1,0:T(8,128)(2,1)}, bf16...) custom-call(bf16[768,768]{1,0:T(8,128)(2,1)} %bitcast.22.x_ref.refs_1_, bf16[768,768]{1,0:T(8,128)(2,1)} %bitcast.231, ...), custom_call_target="tpu_custom_call" | custom-call | flops 14495514624 | bytes 30000000 | tf_op jit(solution)/shard_map/pallas_call | solution.py:530
  234.2 6.3 %all-to-all-start.4 = ((bf16[16,48,768]{2,1,0:T(8,128)(2,1)}), bf16[16,48,768]{2,1,0:T(8,128)(2,1)}, u32[]{:S(2)}, u32[]{:S(2)}) async-start(bf16[16,48,768]{2,1,0:T(8,128)(2,1)} %bitcast.229), calls=%async_computation.4 | async-start | bytes 2359296 | tf_op jit(solution)/shard_map/all_to_all | solution.py:788
  249.1 3.1 collective-permute-done.18.x_ref.refs_0_
  252.2 10.8 %shard_map.268 = (bf16[512,3072]{1,0:T(8,128)(2,1)}, bf16[512,3072]{1,0:T(8,128)(2,1)}, bf16[512,768]{1,0:T(8,128)(2,1)}) custom-call(bf16[512,768]{1,0:T(8,128)(2,1)} %collective-permute-done.18.x_ref.refs_0_, bf16[512,768]{1,0:T(8,128)(2,1)} %bitcast.238, bf16[768,128]{1,0:T(8,128)(2,1)} %pad.38.router_ref, f32[8,128]{1,0:T(8,128)} %broadcast_in_dim.26.pick_ref, ...), custom_call_target="tpu_custom_call" | custom-call | flops 4831838208 | bytes 30000000 | tf_op jit(solution)/shard_map/pallas_call | solution.py:587
  267.2 21.5 %shard_map.267 = (f32[768,3072]{1,0:T(8,128)}, f32[3072,768]{1,0:T(8,128)}) custom-call(s32[1]{0:T(128)} %constant.61.clone.1.more_ref, bf16[512,768]{1,0:T(8,128)(2,1)} %bitcast.20.x_ref.refs_0_, bf16[768,768]{1,0:T(8,128)(2,1)} %bitcast.22.x_ref.refs_1_, bf16[512,768]{1,0:T(8,128)(2,1)} %get-tuple-element.136.refs_2_, ...), custom_call_target="tpu_custom_call" | custom-call | flops 12079595520 | bytes 50000000 | tf_op jit(solution)/shard_map/pallas_call | solution.py:646
  288.7 5.8 %all-to-all-start.3 = ((bf16[16,32,768]{2,1,0:T(8,128)(2,1)}), bf16[16,32,768]{2,1,0:T(8,128)(2,1)}, u32[]{:S(2)}, u32[]{:S(2)}) async-start(bf16[16,32,768]{2,1,0:T(8,128)(2,1)} %bitcast.235), calls=%async_computation.3 | async-start | bytes 1572864 | tf_op jit(solution)/shard_map/all_to_all | solution.py:788
  297.1 13.7 %shard_map.269 = (bf16[768,3072]{1,0:T(8,128)(2,1)}, bf16[768,3072]{1,0:T(8,128)(2,1)}, bf16[768,768]{1,0:T(8,128)(2,1)}) custom-call(bf16[768,768]{1,0:T(8,128)(2,1)} %collective-permute-done.20.x_ref.refs_1_, bf16[768,768]{1,0:T(8,128)(2,1)} %bitcast.230, bf16[768,128]{1,0:T(8,128)(2,1)} %pad.38.router_ref, f32[8,128]{1,0:T(8,128)} %broadcast_in_dim.26.pick_ref, ...), custom_call_target="tpu_custom_call" | custom-call | flops 7247757312 | bytes 30000000 | tf_op jit(solution)/shard_map/pallas_call | solution.py:587
  310.8 4.4 fusion.72
  315.1 3.5 convolution_add_fusion.1
  322.7 6.0 %all-to-all-start.5 = ((bf16[16,80,768]{2,1,0:T(8,128)(2,1)}), bf16[16,80,768]{2,1,0:T(8,128)(2,1)}, u32[]{:S(2)}, u32[]{:S(2)}) async-start(bf16[16,80,768]{2,1,0:T(8,128)(2,1)} %pad_maximum_fusion.4), calls=%async_computation.5 | async-start | bytes 3932160 | tf_op jit(solution)/shard_map/all_to_all | solution.py:788
  328.7 3.2 fusion.3
  331.9 2.6 convolution_convert_fusion.2.dctx_ref
  334.6 45.6 %shard_map.270 = (bf16[1024,768]{1,0:T(8,128)(2,1)}, bf16[2048,768]{1,0:T(8,128)(2,1)}, bf16[2048,768]{1,0:T(8,128)(2,1)}, f32[12,8,128]{2,1,0:T(8,128)}) custom-call(bf16[1024,768]{1,0:T(8,128)(2,1)} %convolution_convert_fusion.3.q_ref, bf16[2048,768]{1,0:T(8,128)(2,1)} %convolution_convert_fusion.1.k_ref, bf16[2048,768]{1,0:T(8,128)(2,1)} %convolution_convert_fusion.v_ref, ...), custom_call_target="tpu_custom_call" | custom-call | flops 32212254720 | bytes 54000000 | tf_op jit(solution)/shard_map/pallas_call | solution.py:390
  381.8 4.8 convolution_convert_fusion.6
  386.6 3.5 convolution_convert_fusion.7
  390.4 2.8 convolution_convert_fusion.4
  393.2 2.8 convolution_convert_fusion.5
  401.9 2.6 collective-permute-done.21
  404.6 2.6 fusion.11
  411.5 2.8 collective-permute-start.26
  414.3 26.2 %shard_map.271 = (f32[768,3072]{1,0:T(8,128)}, f32[3072,768]{1,0:T(8,128)}) custom-call(s32[1]{0:T(128)} %constant.65.clone.1.more_ref, bf16[512,768]{1,0:T(8,128)(2,1)} %collective-permute-done.18.x_ref.refs_0_, bf16[768,768]{1,0:T(8,128)(2,1)} %collective-permute-done.20.x_ref.refs_1_, bf16[512,768]{1,0:T(8,128)(2,1)} %get-tuple-element.192.refs_2_, ...), custom_call_target="tpu_custom_call" | custom-call | flops 12079595520 | bytes 50000000 | tf_op jit(solution)/shard_map/pallas_call | solution.py:646
  442.3 2.8 collective-permute-start.28
  446.7 2.6 fusion.76
  449.4 4.5 fusion.70
  456.4 3.9 collective-permute-start.34
  467.9 2.8 copy.170
  474.4 2.6 collective-permute-done.32
  493.0 4.2 fusion.5
  (289 shorter events, 119.7 us)
Async XLA Ops:
  7.2 130.8 %all-gather.2.cloned.1.call-start = ((), (), s32[]{:S(2)}) async-start(), calls=%async_computation.6 | async-start | bytes 1253376 | tf_op jit(solution)/shard_map/all_gather | solution.py:944
  13.5 25.4 %collective-permute-start.2 = (bf16[1,1,1,48,896]{4,3,2,1,0:T(8,128)(2,1)S(1)}, bf16[1,1,1,48,896]{4,3,2,1,0:T(8,128)(2,1)S(1)}, u32[]{:S(2)}, u32[]{:S(2)}) collective-permute-start(bf16[1,1,1,48,896]{4,3,2,1,0:T(8,128)(2,1)S(1)} %fusion.55), channel_id=1, source_target_pairs={{0,12},{4,0},{8,4},{12,8},{1,13},{5,1},{9,5},{13,9},{2,14},{6,2},{... | collective-permute-start | bytes 258056 | tf_op jit(solution)/shard_map/ppermute | solution.py:704
  18.5 20.4 %collective-permute-start.3 = (bf16[1,1,1,48,896]{4,3,2,1,0:T(8,128)(2,1)S(1)}, bf16[1,1,1,48,896]{4,3,2,1,0:T(8,128)(2,1)S(1)}, u32[]{:S(2)}, u32[]{:S(2)}) collective-permute-start(bf16[1,1,1,48,896]{4,3,2,1,0:T(8,128)(2,1)S(1)} %fusion.55), channel_id=1, source_target_pairs={{0,8},{4,12},{8,0},{12,4},{1,9},{5,13},{9,1},{13,5},{2,10},{6,14},... | collective-permute-start | bytes 258056 | tf_op jit(solution)/shard_map/ppermute | solution.py:704
  18.5 20.4 %collective-permute-start.4 = (bf16[1,1,1,48,896]{4,3,2,1,0:T(8,128)(2,1)S(1)}, bf16[1,1,1,48,896]{4,3,2,1,0:T(8,128)(2,1)S(1)}, u32[]{:S(2)}, u32[]{:S(2)}) collective-permute-start(bf16[1,1,1,48,896]{4,3,2,1,0:T(8,128)(2,1)S(1)} %fusion.55), channel_id=1, source_target_pairs={{0,4},{4,8},{8,12},{12,0},{1,5},{5,9},{9,13},{13,1},{2,6},{6,10},{... | collective-permute-start | bytes 258056 | tf_op jit(solution)/shard_map/ppermute | solution.py:704
  19.5 12.9 %collective-permute-start.6 = (bf16[1,1,1,48,768]{4,3,2,1,0:T(8,128)(2,1)}, bf16[1,1,1,48,768]{4,3,2,1,0:T(8,128)(2,1)S(1)}, u32[]{:S(2)}, u32[]{:S(2)}) collective-permute-start(bf16[1,1,1,48,768]{4,3,2,1,0:T(8,128)(2,1)} %bitcast.242), channel_id=1, source_target_pairs={{0,12},{4,0},{8,4},{12,8},{1,13},{5,1},{9,5},{13,9},{2,14},{6,2},{... | collective-permute-start | bytes 221192 | tf_op jit(solution)/shard_map/ppermute | solution.py:704
  22.3 10.2 %collective-permute-start.7 = (bf16[1,1,1,48,768]{4,3,2,1,0:T(8,128)(2,1)}, bf16[1,1,1,48,768]{4,3,2,1,0:T(8,128)(2,1)S(1)}, u32[]{:S(2)}, u32[]{:S(2)}) collective-permute-start(bf16[1,1,1,48,768]{4,3,2,1,0:T(8,128)(2,1)} %bitcast.243), channel_id=1, source_target_pairs={{0,8},{4,12},{8,0},{12,4},{1,9},{5,13},{9,1},{13,5},{2,10},{6,14},... | collective-permute-start | bytes 221192 | tf_op jit(solution)/shard_map/ppermute | solution.py:704
  32.4 6.2 %collective-permute-start.8 = (bf16[1,1,1,48,768]{4,3,2,1,0:T(8,128)(2,1)S(1)}, bf16[1,1,1,48,768]{4,3,2,1,0:T(8,128)(2,1)S(1)}, u32[]{:S(2)}, u32[]{:S(2)}) collective-permute-start(bf16[1,1,1,48,768]{4,3,2,1,0:T(8,128)(2,1)S(1)} %bitcast.244), channel_id=1, source_target_pairs={{0,4},{4,8},{8,12},{12,0},{1,5},{5,9},{9,13},{13,1},{2,6},{6,10},{... | collective-permute-start | bytes 221192 | tf_op jit(solution)/shard_map/ppermute | solution.py:704
  32.5 6.2 %collective-permute-start.5 = (bf16[1,1,1,48,768]{4,3,2,1,0:T(8,128)(2,1)S(1)}, bf16[1,1,1,48,768]{4,3,2,1,0:T(8,128)(2,1)S(1)}, u32[]{:S(2)}, u32[]{:S(2)}) collective-permute-start(bf16[1,1,1,48,768]{4,3,2,1,0:T(8,128)(2,1)S(1)} %bitcast.245), channel_id=1, source_target_pairs={{0,2},{1,3},{2,0},{3,1},{4,6},{5,7},{6,4},{7,5},{8,10},{9,11},{10,... | collective-permute-start | bytes 221192 | tf_op jit(solution)/shard_map/ppermute | solution.py:682
  39.1 8.4 %collective-permute-start.10 = (bf16[1,2,1,48,768]{4,3,2,1,0:T(8,128)(2,1)S(1)}, bf16[1,2,1,48,768]{4,3,2,1,0:T(8,128)(2,1)S(1)}, u32[]{:S(2)}, u32[]{:S(2)}) collective-permute-start(bf16[1,2,1,48,768]{4,3,2,1,0:T(8,128)(2,1)S(1)} %fusion.52), channel_id=1, source_target_pairs={{0,12},{4,0},{8,4},{12,8},{1,13},{5,1},{9,5},{13,9},{2,14},{6,2},{... | collective-permute-start | bytes 442376 | tf_op jit(solution)/shard_map/ppermute | solution.py:704
  41.1 7.9 %collective-permute-start.11 = (bf16[1,2,1,48,768]{4,3,2,1,0:T(8,128)(2,1)S(1)}, bf16[1,2,1,48,768]{4,3,2,1,0:T(8,128)(2,1)S(1)}, u32[]{:S(2)}, u32[]{:S(2)}) collective-permute-start(bf16[1,2,1,48,768]{4,3,2,1,0:T(8,128)(2,1)S(1)} %fusion.52), channel_id=1, source_target_pairs={{0,8},{4,12},{8,0},{12,4},{1,9},{5,13},{9,1},{13,5},{2,10},{6,14},... | collective-permute-start | bytes 442376 | tf_op jit(solution)/shard_map/ppermute | solution.py:704
  42.4 38.9 %collective-permute-start.1 = (bf16[512,768]{1,0:T(8,128)(2,1)}, bf16[512,768]{1,0:T(8,128)(2,1)S(1)}, u32[]{:S(2)}, u32[]{:S(2)}) collective-permute-start(bf16[512,768]{1,0:T(8,128)(2,1)} %get-tuple-element.293), channel_id=1, source_target_pairs={{1,0},{2,1},{3,2},{5,4},{6,5},{7,6},{9,8},{10,9},{11,10},{13,12},{... | collective-permute-start | bytes 2359304 | tf_op jit(solution)/shard_map/ppermute | solution.py:909
  43.6 37.7 %collective-permute-start = (bf16[512,768]{1,0:T(8,128)(2,1)}, bf16[512,768]{1,0:T(8,128)(2,1)S(1)}, u32[]{:S(2)}, u32[]{:S(2)}) collective-permute-start(bf16[512,768]{1,0:T(8,128)(2,1)} %get-tuple-element.292), channel_id=1, source_target_pairs={{0,1},{1,2},{2,3},{4,5},{5,6},{6,7},{8,9},{9,10},{10,11},{12,13},{... | collective-permute-start | bytes 2359304 | tf_op jit(solution)/shard_map/ppermute | solution.py:909
  46.7 8.5 %collective-permute-start.12 = (bf16[1,2,1,48,768]{4,3,2,1,0:T(8,128)(2,1)S(1)}, bf16[1,2,1,48,768]{4,3,2,1,0:T(8,128)(2,1)S(1)}, u32[]{:S(2)}, u32[]{:S(2)}) collective-permute-start(bf16[1,2,1,48,768]{4,3,2,1,0:T(8,128)(2,1)S(1)} %fusion.52), channel_id=1, source_target_pairs={{0,4},{4,8},{8,12},{12,0},{1,5},{5,9},{9,13},{13,1},{2,6},{6,10},{... | collective-permute-start | bytes 442376 | tf_op jit(solution)/shard_map/ppermute | solution.py:704
  47.4 23.3 %collective-permute-start.9 = (bf16[4,1,1,48,896]{4,3,2,1,0:T(8,128)(2,1)S(1)}, bf16[4,1,1,48,896]{4,3,2,1,0:T(8,128)(2,1)S(1)}, u32[]{:S(2)}, u32[]{:S(2)}) collective-permute-start(bf16[4,1,1,48,896]{4,3,2,1,0:T(8,128)(2,1)S(1)} %constant_dynamic-slice_fusion.2), channel_id=1, source_target_pairs={{0,2},{1,3},{2,0},{3,1},{4,6},{5,7},{6,4},{7,5},{8,10},{9,11},{10,... | collective-permute-start | bytes 1032200 | tf_op jit(solution)/shard_map/ppermute | solution.py:682
  49.0 20.6 %collective-permute-start.13 = (bf16[4,1,1,48,768]{4,3,2,1,0:T(8,128)(2,1)S(1)}, bf16[4,1,1,48,768]{4,3,2,1,0:T(8,128)(2,1)S(1)}, u32[]{:S(2)}, u32[]{:S(2)}) collective-permute-start(bf16[4,1,1,48,768]{4,3,2,1,0:T(8,128)(2,1)S(1)} %constant_dynamic-slice_fusion.1), channel_id=1, source_target_pairs={{0,2},{1,3},{2,0},{3,1},{4,6},{5,7},{6,4},{7,5},{8,10},{9,11},{10,... | collective-permute-start | bytes 884744 | tf_op jit(solution)/shard_map/ppermute | solution.py:682
  71.9 10.2 %collective-permute-start.15 = (bf16[4,2,1,48,768]{4,3,2,1,0:T(8,128)(2,1)}, bf16[4,2,1,48,768]{4,3,2,1,0:T(8,128)(2,1)}, u32[]{:S(2)}, u32[]{:S(2)}) collective-permute-start(bf16[4,2,1,48,768]{4,3,2,1,0:T(8,128)(2,1)} %constant_dynamic-slice_fusion), channel_id=1, source_target_pairs={{0,1},{1,0},{2,3},{3,2},{4,5},{5,4},{6,7},{7,6},{8,9},{9,8},{10,11... | collective-permute-start | bytes 1769480 | tf_op jit(solution)/shard_map/ppermute | solution.py:682
  74.6 11.5 %collective-permute-start.14 = (bf16[4,2,1,48,896]{4,3,2,1,0:T(8,128)(2,1)}, bf16[4,2,1,48,896]{4,3,2,1,0:T(8,128)(2,1)}, u32[]{:S(2)}, u32[]{:S(2)}) collective-permute-start(bf16[4,2,1,48,896]{4,3,2,1,0:T(8,128)(2,1)} %fusion.33), channel_id=1, source_target_pairs={{0,1},{1,0},{2,3},{3,2},{4,5},{5,4},{6,7},{7,6},{8,9},{9,8},{10,11... | collective-permute-start | bytes 2064392 | tf_op jit(solution)/shard_map/ppermute | solution.py:682
  74.6 9.5 %collective-permute-start.16 = (bf16[4,2,1,48,768]{4,3,2,1,0:T(8,128)(2,1)}, bf16[4,2,1,48,768]{4,3,2,1,0:T(8,128)(2,1)}, u32[]{:S(2)}, u32[]{:S(2)}) collective-permute-start(bf16[4,2,1,48,768]{4,3,2,1,0:T(8,128)(2,1)} %fusion.36), channel_id=1, source_target_pairs={{0,1},{1,0},{2,3},{3,2},{4,5},{5,4},{6,7},{7,6},{8,9},{9,8},{10,11... | collective-permute-start | bytes 1769480 | tf_op jit(solution)/shard_map/ppermute | solution.py:682
  75.1 70.1 %all-to-all-start = ((bf16[16,80,768]{2,1,0:T(8,128)(2,1)}), bf16[16,80,768]{2,1,0:T(8,128)(2,1)}, u32[]{:S(2)}, u32[]{:S(2)}) async-start(bf16[16,80,768]{2,1,0:T(8,128)(2,1)} %bitcast.17), calls=%async_computation | async-start | bytes 3932160 | tf_op jit(solution)/shard_map/all_to_all | solution.py:788
  145.2 25.2 %all-to-all-start.1 = ((bf16[16,32,768]{2,1,0:T(8,128)(2,1)}), bf16[16,32,768]{2,1,0:T(8,128)(2,1)}, u32[]{:S(2)}, u32[]{:S(2)}) async-start(bf16[16,32,768]{2,1,0:T(8,128)(2,1)} %bitcast.237), calls=%async_computation.1 | async-start | bytes 1572864 | tf_op jit(solution)/shard_map/all_to_all | solution.py:788
  170.5 40.3 %all-to-all-start.2 = ((bf16[16,48,768]{2,1,0:T(8,128)(2,1)}), bf16[16,48,768]{2,1,0:T(8,128)(2,1)}, u32[]{:S(2)}, u32[]{:S(2)}) async-start(bf16[16,48,768]{2,1,0:T(8,128)(2,1)} %bitcast.228), calls=%async_computation.2 | async-start | bytes 2359296 | tf_op jit(solution)/shard_map/all_to_all | solution.py:788
  180.1 3.6 collective-permute-start.17
  190.6 54.0 %collective-permute-start.19 = (bf16[1280,768]{1,0:T(8,128)(2,1)}, bf16[1280,768]{1,0:T(8,128)(2,1)}, u32[]{:S(2)}, u32[]{:S(2)}) collective-permute-start(bf16[1280,768]{1,0:T(8,128)(2,1)} %bitcast.18), channel_id=1, source_target_pairs={{0,16},{16,0},{1,17},{17,1},{2,18},{18,2},{3,19},{19,3},{4,20},{20... | collective-permute-start | bytes 5898248 | tf_op jit(solution)/shard_map/ppermute | solution.py:682
  192.1 60.1 %collective-permute-start.18 = (bf16[512,768]{1,0:T(8,128)(2,1)}, bf16[512,768]{1,0:T(8,128)(2,1)}, u32[]{:S(2)}, u32[]{:S(2)}) collective-permute-start(bf16[512,768]{1,0:T(8,128)(2,1)} %bitcast.20.x_ref.refs_0_), channel_id=1, source_target_pairs={{0,16},{16,0},{1,17},{17,1},{2,18},{18,2},{3,19},{19,3},{4,20},{20... | collective-permute-start | bytes 2359304 | tf_op jit(solution)/shard_map/ppermute | solution.py:682
  234.2 54.5 %all-to-all-start.4 = ((bf16[16,48,768]{2,1,0:T(8,128)(2,1)}), bf16[16,48,768]{2,1,0:T(8,128)(2,1)}, u32[]{:S(2)}, u32[]{:S(2)}) async-start(bf16[16,48,768]{2,1,0:T(8,128)(2,1)} %bitcast.229), calls=%async_computation.4 | async-start | bytes 2359296 | tf_op jit(solution)/shard_map/all_to_all | solution.py:788
  263.0 34.1 %collective-permute-start.20 = (bf16[768,768]{1,0:T(8,128)(2,1)}, bf16[768,768]{1,0:T(8,128)(2,1)}, u32[]{:S(2)}, u32[]{:S(2)}) collective-permute-start(bf16[768,768]{1,0:T(8,128)(2,1)} %bitcast.22.x_ref.refs_1_), channel_id=1, source_target_pairs={{0,16},{16,0},{1,17},{17,1},{2,18},{18,2},{3,19},{19,3},{4,20},{20... | collective-permute-start | bytes 3538952 | tf_op jit(solution)/shard_map/ppermute | solution.py:682
  288.7 26.4 %all-to-all-start.3 = ((bf16[16,32,768]{2,1,0:T(8,128)(2,1)}), bf16[16,32,768]{2,1,0:T(8,128)(2,1)}, u32[]{:S(2)}, u32[]{:S(2)}) async-start(bf16[16,32,768]{2,1,0:T(8,128)(2,1)} %bitcast.235), calls=%async_computation.3 | async-start | bytes 1572864 | tf_op jit(solution)/shard_map/all_to_all | solution.py:788
  322.7 63.9 %all-to-all-start.5 = ((bf16[16,80,768]{2,1,0:T(8,128)(2,1)}), bf16[16,80,768]{2,1,0:T(8,128)(2,1)}, u32[]{:S(2)}, u32[]{:S(2)}) async-start(bf16[16,80,768]{2,1,0:T(8,128)(2,1)} %pad_maximum_fusion.4), calls=%async_computation.5 | async-start | bytes 3932160 | tf_op jit(solution)/shard_map/all_to_all | solution.py:788
  334.5 45.6 %copy-start.36 = (f32[8,128,32]{1,2,0:T(8,128)S(1)}, f32[8,128,32]{1,2,0:T(8,128)}, u32[]{:S(2)}) copy-start(f32[8,128,32]{1,2,0:T(8,128)} %constant.67.clone) | copy-start | bytes 393220
  334.6 47.0 %copy-start.27 = (bf16[768,16]{1,0:T(8,128)(2,1)S(1)}, bf16[768,16]{1,0:T(8,128)(2,1)}, u32[]{:S(2)}) copy-start(bf16[768,16]{1,0:T(8,128)(2,1)} %fusion.42) | copy-start | bytes 73732
  399.9 4.7 collective-permute-start.23
  401.4 5.7 %collective-permute-start.22 = (bf16[8,48,1664]{2,1,0:T(8,128)(2,1)}, bf16[8,48,1664]{2,1,0:T(8,128)(2,1)}, u32[]{:S(2)}, u32[]{:S(2)}) collective-permute-start(bf16[8,48,1664]{2,1,0:T(8,128)(2,1)} %fusion.16), channel_id=1, source_target_pairs={{0,1},{1,0},{2,3},{3,2},{4,5},{5,4},{6,7},{7,6},{8,9},{9,8},{10,11... | collective-permute-start | bytes 3833864 | tf_op jit(solution)/shard_map/ppermute | solution.py:682
  401.6 3.0 collective-permute-start.21
  409.2 31.3 %collective-permute-start.24 = (f32[16]{0:T(128)S(1)}, f32[16]{0:T(128)S(1)}, u32[]{:S(2)}, u32[]{:S(2)}) collective-permute-start(f32[16]{0:T(128)S(1)} %add.182), channel_id=1, source_target_pairs={{0,2},{1,3},{2,0},{3,1},{4,6},{5,7},{6,4},{7,5},{8,10},{9,11},{10,... | collective-permute-start | bytes 200 | tf_op jit(solution)/shard_map/ppermute | solution.py:682
  411.2 30.6 %collective-permute-start.25 = (bf16[4,48,1664]{2,1,0:T(8,128)(2,1)S(1)}, bf16[4,48,1664]{2,1,0:T(8,128)(2,1)S(1)}, u32[]{:S(2)}, u32[]{:S(2)}) collective-permute-start(bf16[4,48,1664]{2,1,0:T(8,128)(2,1)S(1)} %select_bitcast_fusion), channel_id=1, source_target_pairs={{0,2},{1,3},{2,0},{3,1},{4,6},{5,7},{6,4},{7,5},{8,10},{9,11},{10,... | collective-permute-start | bytes 1916936 | tf_op jit(solution)/shard_map/ppermute | solution.py:682
  411.5 29.0 %collective-permute-start.26 = (bf16[1,192,1536]{2,1,0:T(8,128)(2,1)S(1)}, bf16[1,192,1536]{2,1,0:T(8,128)(2,1)}, u32[]{:S(2)}, u32[]{:S(2)}) collective-permute-start(bf16[1,192,1536]{2,1,0:T(8,128)(2,1)S(1)} %select_bitcast_fusion.1), channel_id=1, source_target_pairs={{0,8},{4,12},{8,0},{12,4},{1,9},{5,13},{9,1},{13,5},{2,10},{6,14},... | collective-permute-start | bytes 1769480 | tf_op jit(solution)/shard_map/ppermute | solution.py:682
  442.0 18.4 %collective-permute-start.27 = (f32[16]{0:T(128)S(1)}, f32[16]{0:T(128)S(1)}, u32[]{:S(2)}, u32[]{:S(2)}) collective-permute-start(f32[16]{0:T(128)S(1)} %add.185), channel_id=1, source_target_pairs={{0,8},{4,12},{8,0},{12,4},{1,9},{5,13},{9,1},{13,5},{2,10},{6,14},... | collective-permute-start | bytes 200 | tf_op jit(solution)/shard_map/ppermute | solution.py:682
  442.3 18.9 %collective-permute-start.28 = (bf16[1,96,1664]{2,1,0:T(8,128)(2,1)S(1)}, bf16[1,96,1664]{2,1,0:T(8,128)(2,1)S(1)}, u32[]{:S(2)}, u32[]{:S(2)}) collective-permute-start(bf16[1,96,1664]{2,1,0:T(8,128)(2,1)S(1)} %select_bitcast_fusion.2), channel_id=1, source_target_pairs={{0,8},{4,12},{8,0},{12,4},{1,9},{5,13},{9,1},{13,5},{2,10},{6,14},... | collective-permute-start | bytes 958472 | tf_op jit(solution)/shard_map/ppermute | solution.py:682
  445.2 15.2 %collective-permute-start.29 = (bf16[1,96,1536]{2,1,0:T(8,128)(2,1)S(1)}, bf16[1,96,1536]{2,1,0:T(8,128)(2,1)S(1)}, u32[]{:S(2)}, u32[]{:S(2)}) collective-permute-start(bf16[1,96,1536]{2,1,0:T(8,128)(2,1)S(1)} %select_bitcast_fusion.3), channel_id=1, source_target_pairs={{0,4},{4,0},{8,12},{12,8},{1,5},{5,1},{9,13},{13,9},{2,6},{6,2},{1... | collective-permute-start | bytes 884744 | tf_op jit(solution)/shard_map/ppermute | solution.py:682
  455.2 37.8 %collective-permute-start.35 = (bf16[512,768]{0,1:T(8,128)(2,1)}, bf16[512,768]{0,1:T(8,128)(2,1)}, u32[]{:S(2)}, u32[]{:S(2)}) collective-permute-start(bf16[512,768]{0,1:T(8,128)(2,1)} %get-tuple-element.291), channel_id=1, source_target_pairs={{1,0},{2,1},{3,2},{5,4},{6,5},{7,6},{9,8},{10,9},{11,10},{13,12},{... | collective-permute-start | bytes 2359304 | tf_op jit(solution)/shard_map/ppermute | solution.py:1033
  456.4 36.5 %collective-permute-start.34 = (bf16[512,768]{0,1:T(8,128)(2,1)}, bf16[512,768]{0,1:T(8,128)(2,1)}, u32[]{:S(2)}, u32[]{:S(2)}) collective-permute-start(bf16[512,768]{0,1:T(8,128)(2,1)} %get-tuple-element.290), channel_id=1, source_target_pairs={{0,1},{1,2},{2,3},{4,5},{5,6},{6,7},{8,9},{9,10},{10,11},{12,13},{... | collective-permute-start | bytes 2359304 | tf_op jit(solution)/shard_map/ppermute | solution.py:1034
  470.7 3.7 collective-permute-start.30
  471.2 20.3 %copy-start.30 = (bf16[48,768]{1,0:T(8,128)(2,1)S(1)}, bf16[48,768]{1,0:T(8,128)(2,1)}, u32[]{:S(2)}) copy-start(bf16[48,768]{1,0:T(8,128)(2,1)} %param.22) | copy-start | bytes 221188
  471.3 5.8 %collective-permute-start.32 = (bf16[1,48,1536]{2,1,0:T(8,128)(2,1)S(1)}, bf16[1,48,1536]{2,1,0:T(8,128)(2,1)S(1)}, u32[]{:S(2)}, u32[]{:S(2)}) collective-permute-start(bf16[1,48,1536]{2,1,0:T(8,128)(2,1)S(1)} %select_bitcast_fusion.5), channel_id=1, source_target_pairs={{0,2},{1,3},{2,0},{3,1},{4,6},{5,7},{6,4},{7,5},{8,10},{9,11},{10,... | collective-permute-start | bytes 442376 | tf_op jit(solution)/shard_map/ppermute | solution.py:682
  472.9 5.9 %collective-permute-start.31 = (bf16[1,48,1664]{2,1,0:T(8,128)(2,1)S(1)}, bf16[1,48,1664]{2,1,0:T(8,128)(2,1)S(1)}, u32[]{:S(2)}, u32[]{:S(2)}) collective-permute-start(bf16[1,48,1664]{2,1,0:T(8,128)(2,1)S(1)} %select_bitcast_fusion.4), channel_id=1, source_target_pairs={{0,4},{4,0},{8,12},{12,8},{1,5},{5,1},{9,13},{13,9},{2,6},{6,2},{1... | collective-permute-start | bytes 479240 | tf_op jit(solution)/shard_map/ppermute | solution.py:682
  478.8 3.7 collective-permute-start.33
  479.4 6.5 %collective-permute-start.37 = (bf16[48,1536]{1,0:T(8,128)(2,1)}, bf16[48,1536]{1,0:T(8,128)(2,1)S(1)}, u32[]{:S(2)}, u32[]{:S(2)}) collective-permute-start(bf16[48,1536]{1,0:T(8,128)(2,1)} %fusion.53), channel_id=1, source_target_pairs={{0,16},{16,0},{1,17},{17,1},{2,18},{18,2},{3,19},{19,3},{4,20},{20... | collective-permute-start | bytes 442376 | tf_op jit(solution)/shard_map/ppermute | solution.py:682
  480.9 7.7 %collective-permute-start.36 = (bf16[48,1664]{1,0:T(8,128)(2,1)S(1)}, bf16[48,1664]{1,0:T(8,128)(2,1)S(1)}, u32[]{:S(2)}, u32[]{:S(2)}) collective-permute-start(bf16[48,1664]{1,0:T(8,128)(2,1)S(1)} %fusion.50), channel_id=1, source_target_pairs={{0,16},{16,0},{1,17},{17,1},{2,18},{18,2},{3,19},{19,3},{4,20},{20... | collective-permute-start | bytes 479240 | tf_op jit(solution)/shard_map/ppermute | solution.py:682
  (45 other events, 267.6 us)
Sparse Core Ops, SparseCore 0:
  75.2 58.4 all-gather.1
